TPU v7x, 128 devices: a whole 4x4x4 slice. The times are simulated.
128 devices in a mesh: section: 4 (over x_hi, core), seq: 8 (over x_lo, z), mp: 4 (over y).
Axes of the slice: x: 4 (x_hi: 2, x_lo: 2; x = x_hi * 2 + x_lo), y: 4, z: 4, core: 2. Of those that a mesh axis runs over, the one named last changes fastest.
Arguments:
- features: bfloat16 [128, 257, 1280], P(('section', 'seq')), may hold values from -6 to 6
- latent_param: bfloat16 [64, 1280], replicated, may hold values from -6 to 6
- query_proj: bfloat16 [1280, 1536], P(None, 'mp'), may hold values from -0.15625 to 0.15625
- key_proj: bfloat16 [1280, 1536], P(None, 'mp'), may hold values from -0.15625 to 0.15625
- value_proj: bfloat16 [1280, 1536], P(None, 'mp'), may hold values from -0.15625 to 0.15625
- out_proj: bfloat16 [1536, 1280], P('mp'), may hold values from -0.15625 to 0.15625
- hidden: bfloat16 [4, 1024, 8192], P(None, 'seq', 'mp'), may hold values from -6 to 6
- key_weight: bfloat16 [4, 1280, 8192], P('section', None, 'mp'), may hold values from -0.15625 to 0.15625
- value_weight: bfloat16 [4, 1280, 8192], P('section', None, 'mp'), may hold values from -0.15625 to 0.15625
- gate_angle: float32 [4], P('section'), may hold values from 0.3 to 1.5
- group_images: int32 [4, 8, 4], P(None, 'seq'), may hold values from 0 to 31, as said below
- token_slot: int32 [4, 8, 128], P(None, 'seq'), may hold values from 0 to 3, never falling along the last dimension, each value on 1 to 64 neighbouring positions
- attend: int32 [4, 8, 128], P(None, 'seq'), may hold values 0 or 1
Outputs:
- states: bfloat16 [4, 4, 1024, 8192], P('section', None, 'seq', 'mp')
Inputs may be any that keep to these rules, and one draw needn't show every extreme that they name: `group_images`: the 4 entries of a group are consecutive image numbers of its micro-batch, not falling from group to group; the first group of every micro-batch starts at image 0, and in micro-batch 0 the last group ends at image 32 - 1. The entries of group c lie between 4 * (c - 1) and 4 * (c + 2) - 1.
All inputs are finite; a program needn't handle non-finite values. No bound on the sum of `attend` on one device may be relied on, other than what follows from the above.
Results may differ from a plain program's by a relative error of at most 0.007.
Values may be sent and summed in bfloat16 or wider, within the bound.
No kernel may reach another device: no remote copies, remote signals or barrier semaphores. Data moves between devices by JAX's collectives and lax.ppermute only.
A program may use at most 192 MiB of HBM per device.

v0:
```python
import jax
import jax.numpy as jnp
from jax import lax
from jax.sharding import PartitionSpec as P

D = 8192
HEAD = 128
LATENTS = 64
PHEAD = 96


def passed_along(array, axis, by):
    peers = lax.axis_size(axis)
    pairs = [(i, i + by) for i in range(peers) if 0 <= i + by < peers]
    return lax.ppermute(array, axis, pairs)


def normalize(v):
    mean = jnp.mean(v, axis=-1, keepdims=True)
    cent = v - mean
    var = jnp.mean(cent * cent, axis=-1, keepdims=True)
    return cent * lax.rsqrt(var + 1e-05)


def body(
    features,
    latent_param,
    query_proj,
    key_proj,
    value_proj,
    out_proj,
    hidden,
    key_weight,
    value_weight,
    gate_angle,
    group_images,
    token_slot,
    attend,
):
    lat_start = latent_param.astype(jnp.float32)
    base = normalize(lat_start).astype(jnp.bfloat16)
    count = features.shape[0]
    local_inner = query_proj.shape[1]
    pheads_local = local_inner // PHEAD
    pquery = jnp.dot(base, query_proj, preferred_element_type=jnp.float32).astype(jnp.bfloat16)
    pquery = pquery.reshape(LATENTS, pheads_local, PHEAD)
    context = normalize(features.astype(jnp.float32)).astype(jnp.bfloat16)
    stacked = jnp.concatenate(
        [context, jnp.broadcast_to(base[None], (count, LATENTS, base.shape[1]))], axis=1
    )
    pkey = jnp.einsum("ipv,vc->ipc", stacked, key_proj, preferred_element_type=jnp.float32).astype(
        jnp.bfloat16
    )
    pval = jnp.einsum(
        "ipv,vc->ipc", stacked, value_proj, preferred_element_type=jnp.float32
    ).astype(jnp.bfloat16)
    pkey = pkey.reshape(count, -1, pheads_local, PHEAD)
    pval = pval.reshape(count, -1, pheads_local, PHEAD)
    score = jnp.einsum(
        "lhd,iphd->ihlp", pquery, pkey, preferred_element_type=jnp.float32
    ) * PHEAD ** (-0.5)
    weight = jax.nn.softmax(score, axis=-1).astype(jnp.bfloat16)
    mixed = jnp.einsum("ihlp,iphd->ilhd", weight, pval, preferred_element_type=jnp.float32)
    mixed = mixed.reshape(count, LATENTS, local_inner).astype(jnp.bfloat16)
    partial_update = jnp.einsum("ilc,cv->ilv", mixed, out_proj, preferred_element_type=jnp.float32)
    batches = hidden.shape[0]
    group_len = hidden.shape[1]
    width_local = hidden.shape[2]
    heads_local = width_local // HEAD
    section_count = lax.axis_size("section")
    seq_count = lax.axis_size("seq")
    per_batch = count * section_count * seq_count // batches
    image_ids = jnp.arange(batches, dtype=jnp.int32)[:, None] * per_batch + group_images[:, 0, :]
    total = lax.psum(partial_update, "mp")
    latents = normalize(lat_start[None] + total).astype(jnp.bfloat16)
    every = lax.all_gather(latents, ("section", "seq"), axis=0, tiled=True)
    chosen = jnp.take(every, image_ids.reshape(-1), axis=0).reshape(batches, -1, every.shape[-1])
    keys_all = jnp.einsum(
        "bkv,vc->bkc", chosen, key_weight[0], preferred_element_type=jnp.float32
    ).astype(jnp.bfloat16)
    vals_all = jnp.einsum(
        "bkv,vc->bkc", chosen, value_weight[0], preferred_element_type=jnp.float32
    ).astype(jnp.bfloat16)
    gate = jnp.tanh(gate_angle[0])
    slots_all = token_slot[:, 0, :]
    alive_all = attend[:, 0, :].astype(jnp.float32)
    key_slot = jnp.arange(keys_all.shape[1], dtype=jnp.int32) // LATENTS
    section_pos = lax.axis_index("section")
    carried = jnp.zeros((group_len, width_local), jnp.bfloat16)
    collected = jnp.zeros((batches, group_len, width_local), jnp.bfloat16)
    turns = batches + section_count - 1
    for turn in range(turns):
        batch_now = turn - section_pos
        valid = (batch_now >= 0) & (batch_now < batches)
        index_now = jnp.clip(batch_now, 0, batches - 1)
        entering = hidden[min(turn, batches - 1)]
        block = jnp.where(section_pos == 0, entering, carried)
        xf = block.astype(jnp.float32)
        squares = lax.psum(jnp.sum(xf * xf, axis=-1), "mp")
        xn = (xf * lax.rsqrt(squares / D + 1e-05)[:, None]).astype(jnp.bfloat16)
        qh = xn.reshape(group_len, heads_local, HEAD)
        kh = lax.dynamic_index_in_dim(keys_all, index_now, 0, keepdims=False).reshape(
            -1, heads_local, HEAD
        )
        vh = lax.dynamic_index_in_dim(vals_all, index_now, 0, keepdims=False).reshape(
            -1, heads_local, HEAD
        )
        score_t = jnp.einsum("thd,khd->htk", qh, kh, preferred_element_type=jnp.float32) * HEAD ** (
            -0.5
        )
        allowed = (
            key_slot[None, :]
            == lax.dynamic_index_in_dim(slots_all, index_now, 0, keepdims=False)[:, None]
        )
        score_t = jnp.where(allowed[None], score_t, -1e30)
        weight_t = jax.nn.softmax(score_t, axis=-1).astype(jnp.bfloat16)
        attn = jnp.einsum("htk,khd->thd", weight_t, vh, preferred_element_type=jnp.float32).reshape(
            group_len, width_local
        )
        result = (
            xf
            + gate
            * lax.dynamic_index_in_dim(alive_all, index_now, 0, keepdims=False)[:, None]
            * attn
        ).astype(jnp.bfloat16)
        updated = lax.dynamic_update_slice_in_dim(collected, result[None], index_now, 0)
        collected = jnp.where(valid, updated, collected)
        if turn + 1 < turns:
            carried = passed_along(result, "section", 1)
    return collected[None]


def solution(mesh):
    return jax.shard_map(
        body,
        mesh=mesh,
        in_specs=(
            P(("section", "seq"), None, None),
            P(),
            P(None, "mp"),
            P(None, "mp"),
            P(None, "mp"),
            P("mp", None),
            P(None, "seq", "mp"),
            P("section", None, "mp"),
            P("section", None, "mp"),
            P("section"),
            P(None, "seq", None),
            P(None, "seq", None),
            P(None, "seq", None),
        ),
        out_specs=P("section", None, "seq", "mp"),
        check_vma=False,
    )
```

profile of v0, /device:TPU:14, one launch (start us, length us, event | category | flops | bytes accessed | tf_op | source)
XLA Modules:
  0.0 504.9 jit_solution(15439124389194603657)
XLA Ops:
  32.4 49.1 %all-reduce.2.cloned.1.call-done = f32[4,64,1280]{2,1,0:T(8,128)} async-done(((f32[4,64,1280]{2,1,0:T(8,128)}), f32[4,64,1280]{2,1,0:T(8,128)}) %all-reduce.2.cloned.1.call-update) | async-done | bytes 1310736 | tf_op jit(solution)/shard_map/psum | solution.py:74
  88.2 9.4 %psum.57 = f32[128]{0:T(128)S(1)} all-reduce(f32[128]{0:T(128)S(1)} %fusion.42), channel_id=1, replica_groups=mesh['section'=4,'seq'=8,'mp'=4] {'mp'}, use_global_device_ids=true, to_apply=%region_10.11 | all-reduce | flops 128 | bytes 1024 | tf_op jit(solution)/shard_map/psum | solution.py:99
  98.0 109.1 %all-gather.2.cloned.1.call-done = bf16[128,64,1280]{2,1,0:T(8,128)(2,1)} async-done(((bf16[4,64,1280]{2,1,0:T(8,128)(2,1)}), bf16[128,64,1280]{2,1,0:T(8,128)(2,1)}) %all-gather.2.cloned.1.call-update) | async-done | bytes 20971536 | tf_op jit(solution)/shard_map/all_gather | solution.py:76
  207.1 9.2 %gather_fusion = bf16[16,64,1280]{2,1,0:T(8,128)(2,1)} fusion(bf16[128,64,1280]{2,1,0:T(8,128)(2,1)} %all-gather.2.cloned.1.call-done, s32[1024]{0:T(1024)S(1)} %pad_clamp_fusion), kind=kCustom, calls=%fused_computation | custom fusion | bytes 5242944 | tf_op jit(solution)/shard_map/jit(_take)/gather | solution.py:77
  218.6 8.4 %fusion.16 = bf16[4,256,2048]{2,1,0:T(8,128)(2,1)S(1)} fusion(bf16[4,256,1280]{2,1,0:T(8,128)(2,1)S(1)} %bitcast.309, bf16[1,1280,2048]{2,1,0:T(8,128)(2,1)} %param.21), kind=kOutput, calls=%fused_computation.19 | convolution fusion | flops 5370806272 | bytes 12058624 | tf_op jit(solution)/shard_map/bkv,vc->bkc/dot_general | solution.py:81
  227.0 5.8 %fusion.19 = bf16[4,256,2048]{2,1,0:T(8,128)(2,1)S(1)} fusion(bf16[4,256,1280]{2,1,0:T(8,128)(2,1)S(1)} %bitcast.310, bf16[1,1280,2048]{2,1,0:T(8,128)(2,1)S(1)} %bitcast.330), kind=kOutput, calls=%fused_computation.20 | convolution fusion | flops 5370806272 | bytes 12058624 | tf_op jit(solution)/shard_map/bkv,vc->bkc/dot_general | solution.py:78
  232.8 5.3 %constant_dynamic-slice_fusion.9 = (bf16[1,256,2048]{2,1,0:T(8,128)(2,1)}, bf16[1,256,2048]{2,1,0:T(8,128)(2,1)}, bf16[1,256,2048]{2,1,0:T(8,128)(2,1)}, bf16[1,...) fusion(bf16[4,256,2048]{2,1,0:T(8,128)(2,1)S(1)} %fusion.19, ...), kind=kLoop, calls=%fused_computation.216 | loop fusion | bytes 29360156 | tf_op jit(solution)/shard_map/jit(dynamic_index_in_dim)/dynamic_slice | solution.py:102
  248.7 6.7 %fusion.78 = f32[16,128,128]{2,1,0:T(8,128)} fusion(bf16[256,16,128]{0,2,1:T(8,128)(2,1)} %bitcast.319, f32[16,128]{1,0:T(8,128)S(1)} %fusion.260, f32[16,128,256]{2,1,0:T(8,128)} %fusion.97, pred[128,256]{1,0:T(8,128)(4,1)S(1)} %get-tuple-element.61), kind=kOutput, calls=%fused_computation.128 | convolution fusion | flops 136841472 | bytes 4235264 | tf_op jit(solution)/shard_map/htk,khd->thd/dot_general | solution.py:117
  272.9 8.8 %psum.58 = f32[128]{0:T(128)S(1)} all-reduce(f32[128]{0:T(128)S(1)} %get-tuple-element.25), channel_id=1, replica_groups=mesh['section'=4,'seq'=8,'mp'=4] {'mp'}, use_global_device_ids=true, to_apply=%region_14.15 | all-reduce | flops 128 | bytes 1024 | tf_op jit(solution)/shard_map/psum | solution.py:99
  287.0 6.6 %fusion.79 = f32[16,128,128]{2,1,0:T(8,128)} fusion(bf16[256,16,128]{0,2,1:T(8,128)(2,1)} %bitcast.313, f32[16,128]{1,0:T(8,128)S(1)} %fusion.263, f32[16,128,256]{2,1,0:T(8,128)} %fusion.126, pred[128,256]{1,0:T(8,128)(4,1)S(1)} %get-tuple-element.56), kind=kOutput, calls=%fused_computation.129 | convolution fusion | flops 136841472 | bytes 4235264 | tf_op jit(solution)/shard_map/htk,khd->thd/dot_general | solution.py:117
  305.1 5.8 %collective-permute-done.1 = bf16[128,2048]{1,0:T(8,128)(2,1)} collective-permute-done((bf16[128,2048]{1,0:T(8,128)(2,1)}, bf16[128,2048]{1,0:T(8,128)(2,1)}, u32[]{:S(2)}, u32[]{:S(2)}) %collective-permute-start.1) | collective-permute-done | bytes 524320 | tf_op jit(solution)/shard_map/ppermute | solution.py:15
  312.4 10.1 %psum.59 = f32[128]{0:T(128)S(1)} all-reduce(f32[128]{0:T(128)S(1)} %get-tuple-element.21), channel_id=1, replica_groups=mesh['section'=4,'seq'=8,'mp'=4] {'mp'}, use_global_device_ids=true, to_apply=%region_18.19 | all-reduce | flops 128 | bytes 1024 | tf_op jit(solution)/shard_map/psum | solution.py:99
  327.8 6.7 %fusion.80 = f32[16,128,128]{2,1,0:T(8,128)} fusion(bf16[256,16,128]{0,2,1:T(8,128)(2,1)} %bitcast.315, f32[16,128]{1,0:T(8,128)S(1)} %fusion.266, f32[16,128,256]{2,1,0:T(8,128)} %fusion.123, pred[128,256]{1,0:T(8,128)(4,1)S(1)} %get-tuple-element.57), kind=kOutput, calls=%fused_computation.130 | convolution fusion | flops 136841472 | bytes 4235264 | tf_op jit(solution)/shard_map/htk,khd->thd/dot_general | solution.py:117
  346.0 5.8 %collective-permute-done.2 = bf16[128,2048]{1,0:T(8,128)(2,1)} collective-permute-done((bf16[128,2048]{1,0:T(8,128)(2,1)}, bf16[128,2048]{1,0:T(8,128)(2,1)}, u32[]{:S(2)}, u32[]{:S(2)}) %collective-permute-start.2) | collective-permute-done | bytes 524320 | tf_op jit(solution)/shard_map/ppermute | solution.py:15
  353.2 8.1 %psum.60 = f32[128]{0:T(128)S(1)} all-reduce(f32[128]{0:T(128)S(1)} %get-tuple-element.17), channel_id=1, replica_groups=mesh['section'=4,'seq'=8,'mp'=4] {'mp'}, use_global_device_ids=true, to_apply=%region_22.23 | all-reduce | flops 128 | bytes 1024 | tf_op jit(solution)/shard_map/psum | solution.py:99
  366.7 6.7 %fusion.81 = f32[16,128,128]{2,1,0:T(8,128)} fusion(bf16[256,16,128]{0,2,1:T(8,128)(2,1)} %bitcast.316, f32[16,128]{1,0:T(8,128)S(1)} %fusion.269, f32[16,128,256]{2,1,0:T(8,128)} %fusion.120, pred[128,256]{1,0:T(8,128)(4,1)S(1)} %get-tuple-element.58), kind=kOutput, calls=%fused_computation.131 | convolution fusion | flops 136841472 | bytes 4235264 | tf_op jit(solution)/shard_map/htk,khd->thd/dot_general | solution.py:117
  384.8 5.8 %collective-permute-done.3 = bf16[128,2048]{1,0:T(8,128)(2,1)} collective-permute-done((bf16[128,2048]{1,0:T(8,128)(2,1)}, bf16[128,2048]{1,0:T(8,128)(2,1)}, u32[]{:S(2)}, u32[]{:S(2)}) %collective-permute-start.3) | collective-permute-done | bytes 524320 | tf_op jit(solution)/shard_map/ppermute | solution.py:15
  392.0 9.8 %psum.61 = f32[128]{0:T(128)S(1)} all-reduce(f32[128]{0:T(128)S(1)} %get-tuple-element.13), channel_id=1, replica_groups=mesh['section'=4,'seq'=8,'mp'=4] {'mp'}, use_global_device_ids=true, to_apply=%region_26.27 | all-reduce | flops 128 | bytes 1024 | tf_op jit(solution)/shard_map/psum | solution.py:99
  407.1 6.6 %fusion.82 = f32[16,128,128]{2,1,0:T(8,128)} fusion(bf16[256,16,128]{0,2,1:T(8,128)(2,1)} %bitcast.317, f32[16,128]{1,0:T(8,128)S(1)} %fusion.272, f32[16,128,256]{2,1,0:T(8,128)} %fusion.117, pred[128,256]{1,0:T(8,128)(4,1)S(1)} %get-tuple-element.59), kind=kOutput, calls=%fused_computation.132 | convolution fusion | flops 136841472 | bytes 4235264 | tf_op jit(solution)/shard_map/htk,khd->thd/dot_general | solution.py:117
  425.2 5.8 %collective-permute-done.4 = bf16[128,2048]{1,0:T(8,128)(2,1)} collective-permute-done((bf16[128,2048]{1,0:T(8,128)(2,1)}, bf16[128,2048]{1,0:T(8,128)(2,1)}, u32[]{:S(2)}, u32[]{:S(2)}) %collective-permute-start.4) | collective-permute-done | bytes 524320 | tf_op jit(solution)/shard_map/ppermute | solution.py:15
  432.5 7.9 %psum.62 = f32[128]{0:T(128)S(1)} all-reduce(f32[128]{0:T(128)S(1)} %get-tuple-element.9), channel_id=1, replica_groups=mesh['section'=4,'seq'=8,'mp'=4] {'mp'}, use_global_device_ids=true, to_apply=%region_30.31 | all-reduce | flops 128 | bytes 1024 | tf_op jit(solution)/shard_map/psum | solution.py:99
  445.7 6.7 %fusion.83 = f32[16,128,128]{2,1,0:T(8,128)} fusion(bf16[256,16,128]{0,2,1:T(8,128)(2,1)} %bitcast.318, f32[16,128]{1,0:T(8,128)S(1)} %fusion.275, f32[16,128,256]{2,1,0:T(8,128)} %fusion.114, pred[128,256]{1,0:T(8,128)(4,1)S(1)} %get-tuple-element.60), kind=kOutput, calls=%fused_computation.133 | convolution fusion | flops 136841472 | bytes 4235264 | tf_op jit(solution)/shard_map/htk,khd->thd/dot_general | solution.py:117
  471.0 9.7 %psum.63 = f32[128]{0:T(128)S(1)} all-reduce(f32[128]{0:T(128)S(1)} %get-tuple-element.5), channel_id=1, replica_groups=mesh['section'=4,'seq'=8,'mp'=4] {'mp'}, use_global_device_ids=true, to_apply=%region_34.35 | all-reduce | flops 128 | bytes 1024 | tf_op jit(solution)/shard_map/psum | solution.py:99
  486.1 6.7 %fusion.84 = f32[16,128,128]{2,1,0:T(8,128)} fusion(bf16[256,16,128]{0,2,1:T(8,128)(2,1)} %bitcast.314, f32[16,128]{1,0:T(8,128)S(1)} %fusion.278, f32[16,128,256]{2,1,0:T(8,128)} %fusion.111, pred[128,256]{1,0:T(8,128)(4,1)S(1)} %get-tuple-element.55), kind=kOutput, calls=%fused_computation.134 | convolution fusion | flops 136841472 | bytes 4235264 | tf_op jit(solution)/shard_map/htk,khd->thd/dot_general | solution.py:117
  (157 shorter events, 169.3 us)
Async XLA Ops:
  6.5 9.5 %copy-start = (bf16[1280,384]{1,0:T(8,128)(2,1)S(1)}, bf16[1280,384]{1,0:T(8,128)(2,1)}, u32[]{:S(2)}) copy-start(bf16[1280,384]{1,0:T(8,128)(2,1)} %param.16) | copy-start | bytes 2949124
  6.5 74.9 %all-reduce.2.cloned.1.call-start = ((), (), s32[]{:S(2)}) async-start(), calls=%async_computation | async-start | bytes 2621440 | tf_op jit(solution)/shard_map/psum | solution.py:74
  6.5 5.5 %copy-start.2 = (bf16[4,257,1280]{2,0,1:T(4,128)(2,1)S(1)}, bf16[4,257,1280]{2,0,1:T(4,128)(2,1)}, u32[]{:S(2)}) copy-start(bf16[4,257,1280]{2,0,1:T(4,128)(2,1)} %param.13) | copy-start | bytes 7895044
  28.1 2.6 copy-start.12
  30.5 1.9 copy-start.10
  32.3 174.8 %all-gather.2.cloned.1.call-start = ((), (), s32[]{:S(2)}) async-start(), calls=%async_computation.1 | async-start | bytes 21626880 | tf_op jit(solution)/shard_map/all_gather | solution.py:76
  81.4 1.7 copy-start.5
  83.1 2.2 copy-start.14
  83.1 2.9 copy-start.3
  84.6 2.7 copy-start.16
  86.0 11.6 %copy-start.15 = (s32[4,1,128]{2,1,0:T(1,128)S(1)}, s32[4,1,128]{2,1,0:T(1,128)}, u32[]{:S(2)}) copy-start(s32[4,1,128]{2,1,0:T(1,128)} %param.24) | copy-start | bytes 6148
  216.3 10.6 %slice-start = ((s8[5242880]{0:T(1024)(128)(4,1)}), s8[4194304]{0:T(1024)(128)(4,1)S(1)}, s32[]{:S(2)}) async-start(s8[5242880]{0:T(1024)(128)(4,1)} %bitcast.329), calls=%async_computation.2 | async-start | bytes 8388608
  218.6 8.4 %slice-start.1 = ((s8[5242880]{0:T(1024)(128)(4,1)}), s8[1048576]{0:T(1024)(128)(4,1)S(1)}, s32[]{:S(2)}) async-start(s8[5242880]{0:T(1024)(128)(4,1)} %bitcast.329), calls=%async_computation.3 | async-start | bytes 2097152
  259.4 5.4 %copy-start.7 = (bf16[1,256,2048]{2,1,0:T(8,128)(2,1)S(1)}, bf16[1,256,2048]{2,1,0:T(8,128)(2,1)}, u32[]{:S(2)}) copy-start(bf16[1,256,2048]{2,1,0:T(8,128)(2,1)} %get-tuple-element.65) | copy-start | bytes 3145732
  259.4 12.2 %collective-permute-start = (bf16[128,2048]{1,0:T(8,128)(2,1)S(1)}, bf16[128,2048]{1,0:T(8,128)(2,1)}, u32[]{:S(2)}, u32[]{:S(2)}) collective-permute-start(bf16[128,2048]{1,0:T(8,128)(2,1)S(1)} %fusion.43), channel_id=1, source_target_pairs={{0,32},{32,64},{64,96},{1,33},{33,65},{65,97},{2,34},{34,66},{66,9... | collective-permute-start | bytes 1572872 | tf_op jit(solution)/shard_map/ppermute | solution.py:15
  262.4 3.7 copy-start.8
  267.4 1.6 copy-start.4
  298.6 12.3 %collective-permute-start.1 = (bf16[128,2048]{1,0:T(8,128)(2,1)}, bf16[128,2048]{1,0:T(8,128)(2,1)}, u32[]{:S(2)}, u32[]{:S(2)}) collective-permute-start(bf16[128,2048]{1,0:T(8,128)(2,1)} %get-tuple-element.24), channel_id=1, source_target_pairs={{0,32},{32,64},{64,96},{1,33},{33,65},{65,97},{2,34},{34,66},{66,9... | collective-permute-start | bytes 1572872 | tf_op jit(solution)/shard_map/ppermute | solution.py:15
  339.5 12.3 %collective-permute-start.2 = (bf16[128,2048]{1,0:T(8,128)(2,1)}, bf16[128,2048]{1,0:T(8,128)(2,1)}, u32[]{:S(2)}, u32[]{:S(2)}) collective-permute-start(bf16[128,2048]{1,0:T(8,128)(2,1)} %get-tuple-element.20), channel_id=1, source_target_pairs={{0,32},{32,64},{64,96},{1,33},{33,65},{65,97},{2,34},{34,66},{66,9... | collective-permute-start | bytes 1572872 | tf_op jit(solution)/shard_map/ppermute | solution.py:15
  378.3 12.3 %collective-permute-start.3 = (bf16[128,2048]{1,0:T(8,128)(2,1)}, bf16[128,2048]{1,0:T(8,128)(2,1)}, u32[]{:S(2)}, u32[]{:S(2)}) collective-permute-start(bf16[128,2048]{1,0:T(8,128)(2,1)} %get-tuple-element.16), channel_id=1, source_target_pairs={{0,32},{32,64},{64,96},{1,33},{33,65},{65,97},{2,34},{34,66},{66,9... | collective-permute-start | bytes 1572872 | tf_op jit(solution)/shard_map/ppermute | solution.py:15
  418.7 12.3 %collective-permute-start.4 = (bf16[128,2048]{1,0:T(8,128)(2,1)}, bf16[128,2048]{1,0:T(8,128)(2,1)}, u32[]{:S(2)}, u32[]{:S(2)}) collective-permute-start(bf16[128,2048]{1,0:T(8,128)(2,1)} %get-tuple-element.12), channel_id=1, source_target_pairs={{0,32},{32,64},{64,96},{1,33},{33,65},{65,97},{2,34},{34,66},{66,9... | collective-permute-start | bytes 1572872 | tf_op jit(solution)/shard_map/ppermute | solution.py:15
  457.3 12.3 %collective-permute-start.5 = (bf16[128,2048]{1,0:T(8,128)(2,1)}, bf16[128,2048]{1,0:T(8,128)(2,1)}, u32[]{:S(2)}, u32[]{:S(2)}) collective-permute-start(bf16[128,2048]{1,0:T(8,128)(2,1)} %get-tuple-element.8), channel_id=1, source_target_pairs={{0,32},{32,64},{64,96},{1,33},{33,65},{65,97},{2,34},{34,66},{66,9... | collective-permute-start | bytes 1572872 | tf_op jit(solution)/shard_map/ppermute | solution.py:15
  471.0 15.1 %copy-start.6 = (bf16[128,2048]{1,0:T(8,128)(2,1)}, bf16[128,2048]{1,0:T(8,128)(2,1)S(1)}, u32[]{:S(2)}) copy-start(bf16[128,2048]{1,0:T(8,128)(2,1)S(1)} %get-tuple-element.6) | copy-start | bytes 1572868
  492.8 5.1 %copy-start.1 = (bf16[1280,384]{1,0:T(8,128)(2,1)S(1)}, bf16[1280,384]{1,0:T(8,128)(2,1)}, u32[]{:S(2)}) copy-start(bf16[1280,384]{1,0:T(8,128)(2,1)} %param.16) | copy-start | bytes 2949124
  (3 other events, 3.6 us)
Sparse Core Ops, SparseCore 0:
  32.4 49.0 all-reduce.1
  84.7 122.3 all-gather.1
where the time goes:
time: 514 us; the launch traced here: 505 us
  waiting for transfers between devices  187 us (36%)
  matrix products  112 us (22%)
  local copies, waits for them, and re-layouts  75.5 us (15%)
  blocking collectives  63.9 us (12%)
  other arithmetic  39.4 us (8%)
  between operations  14.8 us (3%)
  starting transfers between devices  12.6 us (2%)
    all_gather x1, waiting for transfers between devices, body(): every = lax.all_gather(latents, ('section', 'seq'), axis=0, tiled=True)  109 us
    psum x7, blocking collectives, body(): squares = lax.psum(jnp.sum(xf * xf, axis=-1), 'mp')  63.9 us
    psum x1, waiting for transfers between devices, body(): total = lax.psum(partial_update, 'mp')  49.1 us
    dot_general x7, matrix products, body(): jnp.einsum('htk,khd->thd', weight_t, vh, preferred_element_type=jnp.float32)  46.7 us
    ppermute x6, waiting for transfers between devices, passed_along(): return lax.ppermute(array, axis, pairs)  29 us
    dot_general x7, matrix products, body(): jnp.einsum('thd,khd->htk', qh, kh, preferred_element_type=jnp.float32)  21.6 us
    dynamic_slice x8, local copies, waits for them, and re-layouts, body(): lax.dynamic_index_in_dim(keys_all, index_now, 0, keepdims=False)  21.4 us
    reshape x8, local copies, waits for them, and re-layouts, body(): jnp.einsum('htk,khd->thd', weight_t, vh, preferred_element_type=jnp.float32)  19.1 us
  transfers between devices with their start and end apart: 8, of which 8 were waited for; matrix products, arithmetic and copies ran while one was open for 7% of the time, Pallas kernels for 0%

commit v1 on v0

v1 whole, which is shorter than its diff:
```python
import functools

import jax
import jax.numpy as jnp
from jax import lax
from jax.experimental import pallas as pl
from jax.experimental.pallas import tpu as pltpu
from jax.sharding import PartitionSpec as P

D = 8192
HEAD = 128
LATENTS = 64
PHEAD = 96
EPS = 1e-05
NEG = -1e30
F32 = jnp.float32
BF16 = jnp.bfloat16
VMEM_LIMIT = 40 * 1024 * 1024


def normalize(v):
    mean = jnp.mean(v, axis=-1, keepdims=True)
    cent = v - mean
    var = jnp.mean(cent * cent, axis=-1, keepdims=True)
    return cent * lax.rsqrt(var + EPS)


def dot(a, b):
    return jnp.dot(a, b, preferred_element_type=F32)


def dot_nt(a, b):
    return lax.dot_general(a, b, (((1,), (1,)), ((), ())), preferred_element_type=F32)


def up16(n):
    return -(-n // 16) * 16


def up128(n):
    return -(-n // 128) * 128


def resample_kernel(n, ids, feat, lat, qp, kp, vp, op, *rest):
    outs = rest[:n]
    ctx, pk, pv, pqm = rest[n:]
    patches = feat.shape[1]
    inner = qp.shape[1]
    heads = inner // PHEAD
    rows = ctx.shape[0]
    keys = LATENTS + patches
    step = pl.program_id(0)

    def head_of(shape):
        return lax.broadcasted_iota(jnp.int32, shape, 1) // PHEAD

    @pl.when(step == 0)
    def _():
        base = normalize(lat[...].astype(F32)).astype(BF16)
        pq = dot(base, qp[...]).astype(BF16).astype(F32)
        which = head_of((LATENTS, inner))
        for h in range(heads):
            pqm[h * LATENTS : (h + 1) * LATENTS, :] = jnp.where(which == h, pq, 0.0).astype(BF16)
        pk[0:LATENTS, :] = dot(base, kp[...]).astype(BF16)
        pv[0:LATENTS, :] = dot(base, vp[...]).astype(BF16)
        pad = pk.shape[0] - LATENTS - rows
        if pad:
            pk[LATENTS + rows :, :] = jnp.zeros((pad, inner), BF16)
            pv[LATENTS + rows :, :] = jnp.zeros((pad, inner), BF16)
        ctx[rows - 16 :, :] = jnp.zeros((16, ctx.shape[1]), BF16)

    for r in range(0, patches, 64):
        end = min(r + 64, patches)
        ctx[r:end, :] = normalize(feat[0, r:end, :].astype(F32)).astype(BF16)
    pk[LATENTS : LATENTS + rows, :] = dot(ctx[...], kp[...]).astype(BF16)
    pv[LATENTS : LATENTS + rows, :] = dot(ctx[...], vp[...]).astype(BF16)

    score = dot_nt(pqm[...], pk[...]) * PHEAD ** (-0.5)
    lane = lax.broadcasted_iota(jnp.int32, score.shape, 1)
    score = jnp.where(lane < keys, score, NEG)
    e = jnp.exp(score - jnp.max(score, axis=1, keepdims=True))
    weight = (e / jnp.sum(e, axis=1, keepdims=True)).astype(BF16)
    mix = dot(weight, pv[...])
    which = head_of((LATENTS, inner))
    mixed = jnp.zeros((LATENTS, inner), F32)
    for h in range(heads):
        mixed = jnp.where(which == h, mix[h * LATENTS : (h + 1) * LATENTS, :], mixed)
    update = dot(mixed.astype(BF16), op[...])
    for i in range(n):

        @pl.when(step == i)
        def _(i=i):
            outs[i][...] = update.astype(outs[i].dtype)


def resample(ids, features, latent_param, qp, kp, vp, op, dtype):
    n = ids.shape[0]
    _, patches, vdim = features.shape
    inner = qp.shape[1]
    heads = inner // PHEAD
    rows = up16(patches)
    padded = up128(LATENTS + rows)
    whole = lambda a: pl.BlockSpec(a.shape, lambda i, s: (0,) * a.ndim)
    out = jax.ShapeDtypeStruct((LATENTS, vdim), dtype)
    return pl.pallas_call(
        functools.partial(resample_kernel, n),
        out_shape=[out] * n,
        grid_spec=pltpu.PrefetchScalarGridSpec(
            num_scalar_prefetch=1,
            grid=(n,),
            in_specs=[
                pl.BlockSpec((1, patches, vdim), lambda i, s: (s[i], 0, 0)),
                whole(latent_param),
                whole(qp),
                whole(kp),
                whole(vp),
                whole(op),
            ],
            out_specs=[pl.BlockSpec((LATENTS, vdim), lambda i, s: (0, 0))] * n,
            scratch_shapes=[
                pltpu.VMEM((rows, vdim), BF16),
                pltpu.VMEM((padded, inner), BF16),
                pltpu.VMEM((padded, inner), BF16),
                pltpu.VMEM((heads * LATENTS, inner), BF16),
            ],
        ),
        compiler_params=pltpu.CompilerParams(vmem_limit_bytes=VMEM_LIMIT),
        cost_estimate=pl.CostEstimate(
            flops=n * 2 * (rows * vdim * 2 * inner + 3 * heads * LATENTS * padded * inner),
            bytes_accessed=n * patches * vdim * 2 + 4 * vdim * inner * 2,
            transcendentals=n * heads * LATENTS * padded,
        ),
        name="resample",
    )(ids, features, latent_param, qp, kp, vp, op)


def combine_kernel(lat, own, a, b, c, out):
    total = own[...] + a[...].astype(F32) + b[...].astype(F32) + c[...].astype(F32)
    out[...] = normalize(lat[...].astype(F32) + total).astype(BF16)


def combine(latent_param, own, parts):
    return pl.pallas_call(
        combine_kernel,
        out_shape=jax.ShapeDtypeStruct(latent_param.shape, BF16),
        name="combine",
    )(latent_param, own, *parts)


def project_kernel(flags, a0, a1, a2, a3, kw0, vw0, kw1, vw1, keys, vals, chosen):
    @pl.when(pl.program_id(0) == 0)
    def _():
        for i, a in enumerate((a0, a1, a2, a3)):
            chosen[i * LATENTS : (i + 1) * LATENTS, :] = a[...]

    @pl.when(flags[0] == 0)
    def _():
        keys[...] = dot(chosen[...], kw0[0]).astype(BF16)
        vals[...] = dot(chosen[...], vw0[0]).astype(BF16)

    @pl.when(flags[0] != 0)
    def _():
        keys[...] = dot(chosen[...], kw1[0]).astype(BF16)
        vals[...] = dot(chosen[...], vw1[0]).astype(BF16)


def project(flag, chunks, own, other, tile=256):
    vdim, width = own[0].shape[1:]
    rows = len(chunks) * LATENTS
    chunk = pl.BlockSpec((LATENTS, vdim), lambda i, s: (0, 0))
    w0 = pl.BlockSpec((1, vdim, tile), lambda i, s: (0, 0, i * (1 - s[0])))
    w1 = pl.BlockSpec((1, vdim, tile), lambda i, s: (0, 0, i * s[0]))
    out = pl.BlockSpec((rows, tile), lambda i, s: (0, i))
    shape = jax.ShapeDtypeStruct((rows, width), BF16)
    return pl.pallas_call(
        project_kernel,
        out_shape=[shape, shape],
        grid_spec=pltpu.PrefetchScalarGridSpec(
            num_scalar_prefetch=1,
            grid=(width // tile,),
            in_specs=[chunk] * 4 + [w0, w0, w1, w1],
            out_specs=[out, out],
            scratch_shapes=[pltpu.VMEM((rows, vdim), BF16)],
        ),
        compiler_params=pltpu.CompilerParams(vmem_limit_bytes=VMEM_LIMIT),
        cost_estimate=pl.CostEstimate(
            flops=4 * rows * vdim * width,
            bytes_accessed=4 * vdim * width + 4 * rows * width,
            transcendentals=0,
        ),
        name="project",
    )(flag, *chunks, own[0], own[1], other[0], other[1])


def layer_kernel(parts, row, ids, x, keys, vals, meta, *rest):
    squares = rest[:parts]
    y, square_out, scale_s, bias_s, high_s, gate_s, acc = rest[parts:]
    step = pl.program_id(0)
    rows = x.shape[1]
    heads = x.shape[2] // HEAD

    @pl.when(step == 0)
    def _():
        total = squares[0][...]
        for part in squares[1:]:
            total = total + part[...]
        scale = lax.rsqrt(total / D + EPS) * HEAD ** (-0.5)
        tile = jnp.concatenate(
            [scale, meta[0:1, :], meta[row : row + 1, :], jnp.zeros((rows - 3, rows), F32)], axis=0
        )
        cols = tile.T
        slot = jnp.broadcast_to(cols[:, 1:2], (rows, HEAD))
        scale_s[...] = jnp.broadcast_to(cols[:, 0:1], (rows, HEAD))
        gate_s[...] = jnp.broadcast_to(cols[:, 2:3], (rows, HEAD))
        high = jnp.where(slot > 1.5, 1.0, 0.0)
        high_s[...] = high
        half = (lax.broadcasted_iota(jnp.int32, (rows, HEAD), 1) // LATENTS).astype(F32)
        bias_s[...] = jnp.where(slot - 2.0 * high == half, 0.0, NEG)
        acc[...] = jnp.zeros_like(acc)

    high = high_s[...] > 0.5
    for h in range(heads):
        cols = slice(h * HEAD, (h + 1) * HEAD)
        q = x[0, :, cols]
        score = dot_nt(q, keys[:, cols])
        t = jnp.where(high, score[:, HEAD:], score[:, :HEAD]) * scale_s[...] + bias_s[...]
        e = jnp.exp(t - jnp.max(t, axis=1, keepdims=True))
        w = e / jnp.sum(e, axis=1, keepdims=True)
        weight = jnp.concatenate([jnp.where(high, 0.0, w), jnp.where(high, w, 0.0)], axis=1)
        attn = dot(weight.astype(BF16), vals[:, cols])
        out = (q.astype(F32) + gate_s[...] * attn).astype(BF16)
        y[:, cols] = out
        of = out.astype(F32)
        acc[...] += of * of

    @pl.when(step == pl.num_programs(0) - 1)
    def _():
        square_out[...] = jnp.sum(acc[...].T, axis=0, keepdims=True)


def layer(row, index, x, kv, meta, squares, tile=512):
    keys, vals = kv
    _, rows, width = x.shape
    nkeys = keys.shape[0]
    block = pl.BlockSpec((nkeys, tile), lambda i, s: (0, i))
    whole = lambda a: pl.BlockSpec(a.shape, lambda i, s: (0, 0))
    scratch = pltpu.VMEM((rows, HEAD), F32)
    return pl.pallas_call(
        functools.partial(layer_kernel, len(squares), row),
        out_shape=[
            jax.ShapeDtypeStruct((rows, width), BF16),
            jax.ShapeDtypeStruct((1, rows), F32),
        ],
        grid_spec=pltpu.PrefetchScalarGridSpec(
            num_scalar_prefetch=1,
            grid=(width // tile,),
            in_specs=[
                pl.BlockSpec((1, rows, tile), lambda i, s: (s[0], 0, i)),
                block,
                block,
                whole(meta),
            ]
            + [whole(a) for a in squares],
            out_specs=[
                pl.BlockSpec((rows, tile), lambda i, s: (0, i)),
                pl.BlockSpec((1, rows), lambda i, s: (0, 0)),
            ],
            scratch_shapes=[scratch] * 5,
        ),
        compiler_params=pltpu.CompilerParams(vmem_limit_bytes=VMEM_LIMIT),
        cost_estimate=pl.CostEstimate(
            flops=4 * rows * nkeys * width * 4,
            bytes_accessed=2 * (2 * nkeys * width + 2 * rows * width),
            transcendentals=rows * width,
        ),
        name="layer",
    )(index, x, keys, vals, meta, *squares)


def body(
    features,
    latent_param,
    query_proj,
    key_proj,
    value_proj,
    out_proj,
    hidden,
    key_weight,
    value_weight,
    gate_angle,
    group_images,
    token_slot,
    attend,
):
    s = lax.axis_index("section")
    c = lax.axis_index("seq")
    m = lax.axis_index("mp")
    core = s & 1
    far = s >> 1
    mates = lax.axis_size("mp")
    seqs = lax.axis_size("seq")
    sections = lax.axis_size("section")

    def mp_shift(a, k):
        return lax.ppermute(a, "mp", [(i, (i + k) % mates) for i in range(mates)])

    def core_swap(a):
        return lax.ppermute(a, "section", [(i, i ^ 1) for i in range(sections)])

    def far_swap(a):
        return lax.ppermute(a, "section", [(i, i ^ 2) for i in range(sections)])

    def cross(a):
        return lax.ppermute(a, "section", [(0, 2), (1, 3)])

    def spread(a):
        return [a] + [mp_shift(a, k) for k in (1, 2, 3)]

    own_w = (key_weight, value_weight)
    other_w = (core_swap(key_weight), core_swap(value_weight))
    gate_own = jnp.broadcast_to(jnp.tanh(gate_angle)[:, None], (1, 128))
    gate_other = core_swap(gate_own)
    gate_first = jnp.where(core == 0, gate_own, gate_other)
    gate_second = jnp.where(core == 0, gate_other, gate_own)

    order = jnp.stack([(m + 2) & 3, (m + 1) & 3, (m + 3) & 3]).astype(jnp.int32)
    weights = (query_proj, key_proj, value_proj, out_proj)
    p2, p1, p3 = resample(order, features, latent_param, *weights, BF16)
    r2, r1, r3 = mp_shift(p2, 2), mp_shift(p1, 1), mp_shift(p3, 3)
    (p0,) = resample(m[None].astype(jnp.int32), features, latent_param, *weights, F32)
    latents = combine(latent_param, p0, (r1, r2, r3))

    hf = hidden.astype(F32)
    entering = jnp.sum(hf * hf, axis=-1)
    entering = sum(spread(entering))

    left = lax.ppermute(latents, "seq", [(i, i + 1) for i in range(seqs - 1)])
    right = lax.ppermute(latents, "seq", [(i + 1, i) for i in range(seqs - 1)])
    firsts = group_images[:, 0, 0]
    start = lax.dynamic_index_in_dim(firsts, s, 0, keepdims=False)
    where_is = ((start + ((m - start) & 3)) >> 2) - c
    picked = jnp.where(where_is == 0, latents, jnp.where(where_is < 0, left, right))
    chosen_own = spread(picked)
    chosen_far = spread(far_swap(picked))

    block = (m - firsts[:, None] - token_slot[:, 0, :]) & 3
    alive = attend[:, 0, :].astype(F32)
    rows = jnp.stack(
        [block.astype(F32), alive * gate_first, alive * gate_second]
        + [jnp.zeros_like(alive)] * 5,
        axis=1,
    )
    meta_own = lax.dynamic_index_in_dim(rows, s, 0, keepdims=False)
    meta_far = lax.dynamic_index_in_dim(rows, s ^ 2, 0, keepdims=False)

    flag_first = core[None].astype(jnp.int32)
    flag_second = (1 - core)[None].astype(jnp.int32)
    first_own = project(flag_first, chosen_own, own_w, other_w)
    first_far = project(flag_first, chosen_far, own_w, other_w)
    second_own = project(flag_second, chosen_own, own_w, other_w)
    second_far = project(flag_second, chosen_far, own_w, other_w)

    zero = jnp.zeros((1,), jnp.int32)
    batch0 = core[None].astype(jnp.int32)
    batch1 = batch0 + 2

    sq0 = lax.dynamic_slice_in_dim(entering, core, 1, 0)
    sq1 = lax.dynamic_slice_in_dim(entering, core + 2, 1, 0)
    a0, qa0 = layer(1, batch0, hidden, first_own, meta_own, [sq0])
    qa0 = spread(qa0)
    a1, qa1 = layer(1, batch1, hidden, first_far, meta_far, [sq1])
    qa1 = spread(qa1)
    b0, qb0 = layer(2, zero, a0[None], second_own, meta_own, qa0)
    x0 = cross(b0)
    qb0 = cross(sum(spread(qb0)))
    b1, qb1 = layer(2, zero, a1[None], second_far, meta_far, qa1)
    x1 = cross(b1)
    qb1 = cross(sum(spread(qb1)))

    c0, qc0 = layer(1, zero, x0[None], first_far, meta_far, [qb0])
    qc0 = spread(qc0)
    c1, qc1 = layer(1, zero, x1[None], first_own, meta_own, [qb1])
    qc1 = spread(qc1)
    d0, _ = layer(2, zero, c0[None], second_far, meta_far, qc0)
    d1, _ = layer(2, zero, c1[None], second_own, meta_own, qc1)

    def split(a, b, c_, d_):
        first = jnp.where(far == 0, a, c_)
        second = jnp.where(far == 0, b, d_)
        keep = jnp.where(core == 0, first, second)
        send = jnp.where(core == 0, second, first)
        return keep, core_swap(send)

    keep0, got0 = split(a0, b0, c0, d0)
    keep1, got1 = split(a1, b1, c1, d1)
    even = core == 0
    return jnp.stack(
        [
            jnp.where(even, keep0, got0),
            jnp.where(even, got0, keep0),
            jnp.where(even, keep1, got1),
            jnp.where(even, got1, keep1),
        ]
    )[None]


def solution(mesh):
    return jax.shard_map(
        body,
        mesh=mesh,
        in_specs=(
            P(("section", "seq"), None, None),
            P(),
            P(None, "mp"),
            P(None, "mp"),
            P(None, "mp"),
            P("mp", None),
            P(None, "seq", "mp"),
            P("section", None, "mp"),
            P("section", None, "mp"),
            P("section"),
            P(None, "seq", None),
            P(None, "seq", None),
            P(None, "seq", None),
        ),
        out_specs=P("section", None, "seq", "mp"),
        check_vma=False,
    )
```

time: 514 us -> 192 us (0.37)
  the two profiles are of different devices: /device:TPU:14 before, /device:TPU:7 now
where the time goes in v1:
time: 192 us; the launch traced here: 190 us
  Pallas kernels  81.2 us (42%)
  starting transfers between devices  64.1 us (33%)
  waiting for transfers between devices  20.9 us (11%)
  local copies, waits for them, and re-layouts  17 us (9%)
  other arithmetic  3.81 us (2%)
  between operations  2.49 us (1%)
    ppermute x30, starting transfers between devices, mp_shift(): return lax.ppermute(a, 'mp', [(i, (i + k) % mates) for i in range(mates)])  41.1 us
    pallas_call x8, Pallas kernels, layer(): pl.pallas_call(functools.partial(layer_kernel, len(squares), row), out_sh...  35.3 us
    pallas_call x4, Pallas kernels, project(): pl.pallas_call(project_kernel, out_shape=[shape, shape], grid_spec=pltpu....  33.6 us
    unnamed x81, local copies, waits for them, and re-layouts  16.5 us
    pallas_call x2, Pallas kernels, resample(): pl.pallas_call(functools.partial(resample_kernel, n), out_shape=[out] * n...  10.2 us
    ppermute x4, waiting for transfers between devices, cross(): return lax.ppermute(a, 'section', [(0, 2), (1, 3)])  9.39 us
    ppermute x5, starting transfers between devices, core_swap(): return lax.ppermute(a, 'section', [(i, i ^ 1) for i in range(sections)])  8.88 us
    ppermute x1, starting transfers between devices, body(): right = lax.ppermute(latents, 'seq', [(i + 1, i) for i in range(seqs - 1)])  5.91 us
  transfers between devices with their start and end apart: 42, of which 8 were waited for; matrix products, arithmetic and copies ran while one was open for 3% of the time, Pallas kernels for 43%

profile of v1, /device:TPU:7, one launch (start us, length us, event | category | flops | bytes accessed | tf_op | source)
XLA Modules:
  0.0 189.6 jit_solution(4018651802179881882)
XLA Ops:
  3.6 7.6 %resample.3 = (bf16[64,1280]{1,0:T(8,128)(2,1)S(1)}, bf16[64,1280]{1,0:T(8,128)(2,1)S(1)}, bf16[64,1280]{1,0:T(8,128)(2,1)S(1)}) custom-call(s32[3]{0:T(128)S(1)} %pad_add_fusion.ids, bf16[4,257,1280]{2,1,0:T(8,128)(2,1)S(1)} %copy.16.feat, bf16[64,1280]{1,0:T(8,128)(2,1)S(1)} %copy-done.33, bf16[1280,384]{1,0:T(8,128)(2,1)S(1)} %copy-done.10, ...), custom_call_target="tpu_custom_call" | custom-call | flops 2283798528 | bytes 5905920 | tf_op jit(solution)/shard_map/resample/pallas_call | solution.py:105
  30.5 5.9 %collective-permute-start.4 = (bf16[64,1280]{1,0:T(8,128)(2,1)}, bf16[64,1280]{1,0:T(8,128)(2,1)S(1)}, u32[]{:S(2)}, u32[]{:S(2)}) collective-permute-start(bf16[64,1280]{1,0:T(8,128)(2,1)} %combine.1), channel_id=1, source_target_pairs={{4,0},{8,4},{12,8},{16,12},{20,16},{24,20},{28,24},{5,1},{9,5},{13... | collective-permute-start | bytes 491528 | tf_op jit(solution)/shard_map/ppermute | solution.py:338
  42.2 3.4 %collective-permute-done.3 = bf16[64,1280]{1,0:T(8,128)(2,1)S(1)} collective-permute-done((bf16[64,1280]{1,0:T(8,128)(2,1)}, bf16[64,1280]{1,0:T(8,128)(2,1)S(1)}, u32[]{:S(2)}, u32[]{:S(2)}) %collective-permute-start.3) | collective-permute-done | bytes 163872 | tf_op jit(solution)/shard_map/ppermute | solution.py:337
  49.3 3.0 %collective-permute-done.18.a0 = bf16[64,1280]{1,0:T(8,128)(2,1)S(1)} collective-permute-done((bf16[64,1280]{1,0:T(8,128)(2,1)S(1)}, bf16[64,1280]{1,0:T(8,128)(2,1)S(1)}, u32[]{:S(2)}, u32[]{:S(2)}) %collective-permute-start.18) | collective-permute-done | bytes 163872 | tf_op jit(solution)/shard_map/ppermute | solution.py:311
  52.3 3.5 %collective-permute-start.20 = (bf16[64,1280]{1,0:T(8,128)(2,1)S(1)}, bf16[64,1280]{1,0:T(8,128)(2,1)S(1)}, u32[]{:S(2)}, u32[]{:S(2)}) collective-permute-start(bf16[64,1280]{1,0:T(8,128)(2,1)S(1)} %collective-permute-done.18.a0), channel_id=1, source_target_pairs={{0,2},{1,3},{2,0},{3,1},{4,6},{5,7},{6,4},{7,5},{8,10},{9,11},{10,... | collective-permute-start | bytes 491528 | tf_op jit(solution)/shard_map/ppermute | solution.py:305
  59.2 2.8 %collective-permute-start.6 = (bf16[64,1280]{1,0:T(8,128)(2,1)S(1)}, bf16[64,1280]{1,0:T(8,128)(2,1)S(1)}, u32[]{:S(2)}, u32[]{:S(2)}) collective-permute-start(bf16[64,1280]{1,0:T(8,128)(2,1)S(1)} %select_select_fusion.a0), channel_id=1, source_target_pairs={{0,2},{1,3},{2,0},{3,1},{4,6},{5,7},{6,4},{7,5},{8,10},{9,11},{10,... | collective-permute-start | bytes 491528 | tf_op jit(solution)/shard_map/ppermute | solution.py:305
  68.9 10.0 %project.6 = (bf16[256,2048]{1,0:T(8,128)(2,1)S(1)}, bf16[256,2048]{1,0:T(8,128)(2,1)S(1)}) custom-call(s32[1]{0:T(128)} %bitcast.flags.ids, bf16[64,1280]{1,0:T(8,128)(2,1)S(1)} %copy-done.19, bf16[64,1280]{1,0:T(8,128)(2,1)S(1)} %collective-permute-done.19.a1, bf16[64,1280]{1,0:T(8,128)(2,1)S(1)} %collective-permute-done.20.a2, ...), custom_call_target="tpu_custom_call" | custom-call | flops 2684354560 | bytes 12582912 | tf_op jit(solution)/shard_map/project/pallas_call | solution.py:175
  80.9 4.3 %layer.12 = (bf16[128,2048]{1,0:T(8,128)(2,1)S(1)}, f32[1,128]{1,0:T(1,128)S(1)}) custom-call(s32[1]{0:T(128)S(6)} %add.75.ids, bf16[4,128,2048]{2,1,0:T(8,128)(2,1)S(1)} %copy-done.5, bf16[256,2048]{1,0:T(8,128)(2,1)S(1)} %get-tuple-element.40.keys, bf16[256,2048]{1,0:T(8,128)(2,1)S(1)} %get-tuple-element.41.vals, f32[8,128]{1,0:T(8,128)S(1)} %get-tuple-element.66.meta, ...), custom_call_target="tpu_custom_call" | custom-call | flops 1073741824 | bytes 3145728 | tf_op jit(solution)/shard_map/layer/pallas_call | solution.py:248
  85.2 2.7 %collective-permute-start.32 = (f32[1,128]{1,0:T(1,128)S(1)}, f32[1,128]{1,0:T(1,128)S(1)}, u32[]{:S(2)}, u32[]{:S(2)}) collective-permute-start(f32[1,128]{1,0:T(1,128)S(1)} %get-tuple-element.49.rest_0_), channel_id=1, source_target_pairs={{0,3},{1,0},{2,1},{3,2},{4,7},{5,4},{6,5},{7,6},{8,11},{9,8},{10,9... | collective-permute-start | bytes 1544 | tf_op jit(solution)/shard_map/ppermute | solution.py:305
  88.6 8.6 %project.4 = (bf16[256,2048]{1,0:T(8,128)(2,1)S(1)}, bf16[256,2048]{1,0:T(8,128)(2,1)S(1)}) custom-call(s32[1]{0:T(128)} %bitcast.flags.ids, bf16[64,1280]{1,0:T(8,128)(2,1)S(1)} %select_select_fusion.a0, bf16[64,1280]{1,0:T(8,128)(2,1)S(1)} %collective-permute-done.5.a1, bf16[64,1280]{1,0:T(8,128)(2,1)S(1)} %collective-permute-done.6.a2, ...), custom_call_target="tpu_custom_call" | custom-call | flops 2684354560 | bytes 12582912 | tf_op jit(solution)/shard_map/project/pallas_call | solution.py:175
  97.3 4.3 %layer.8 = (bf16[128,2048]{1,0:T(8,128)(2,1)S(1)}, f32[1,128]{1,0:T(1,128)S(1)}) custom-call(s32[1]{0:T(128)} %bitcast.flags.ids, bf16[4,128,2048]{2,1,0:T(8,128)(2,1)S(1)} %copy-done.6, bf16[256,2048]{1,0:T(8,128)(2,1)S(1)} %get-tuple-element.33.keys, bf16[256,2048]{1,0:T(8,128)(2,1)S(1)} %get-tuple-element.34.vals, f32[8,128]{1,0:T(8,128)S(1)} %get-tuple-element.65.meta, ...), custom_call_target="tpu_custom_call" | custom-call | flops 1073741824 | bytes 3145728 | tf_op jit(solution)/shard_map/layer/pallas_call | solution.py:248
  105.5 7.4 %project.7 = (bf16[256,2048]{1,0:T(8,128)(2,1)S(1)}, bf16[256,2048]{1,0:T(8,128)(2,1)S(1)}) custom-call(s32[1]{0:T(128)} %bitcast.11.flags, bf16[64,1280]{1,0:T(8,128)(2,1)S(1)} %copy-done.20, bf16[64,1280]{1,0:T(8,128)(2,1)S(1)} %copy-done.26, bf16[64,1280]{1,0:T(8,128)(2,1)S(1)} %copy-done.24, bf16[64,1280]{1,0:T(8,128)(2,1)S(1)} %copy-done.22, ...), custom_call_target="tpu_custom_call" | custom-call | flops 2684354560 | bytes 12582912 | tf_op jit(solution)/shard_map/project/pallas_call | solution.py:175
  113.0 7.5 %project.5 = (bf16[256,2048]{1,0:T(8,128)(2,1)S(1)}, bf16[256,2048]{1,0:T(8,128)(2,1)S(1)}) custom-call(s32[1]{0:T(128)} %bitcast.11.flags, bf16[64,1280]{1,0:T(8,128)(2,1)S(1)} %select_select_fusion.a0, bf16[64,1280]{1,0:T(8,128)(2,1)S(1)} %copy-done.32, bf16[64,1280]{1,0:T(8,128)(2,1)S(1)} %copy-done.30, bf16[64,1280]{1,0:T(8,128)(2,1)S(1)} %copy-done.28, ...), custom_call_target="tpu_custom_call" | custom-call | flops 2684354560 | bytes 12582912 | tf_op jit(solution)/shard_map/project/pallas_call | solution.py:175
  120.6 4.3 %layer.13 = (bf16[128,2048]{1,0:T(8,128)(2,1)S(1)}, f32[1,128]{1,0:T(1,128)S(1)}) custom-call(s32[1]{0:T(128)} %constant.42.clone.1.ids, bf16[1,128,2048]{2,1,0:T(8,128)(2,1)S(1)} %bitcast.33, bf16[256,2048]{1,0:T(8,128)(2,1)S(1)} %get-tuple-element.44.keys, bf16[256,2048]{1,0:T(8,128)(2,1)S(1)} %get-tuple-element.45.vals, ...), custom_call_target="tpu_custom_call" | custom-call | flops 1073741824 | bytes 3145728 | tf_op jit(solution)/shard_map/layer/pallas_call | solution.py:248
  124.9 2.7 %collective-permute-start.36 = (f32[1,128]{1,0:T(1,128)S(1)}, f32[1,128]{1,0:T(1,128)S(1)}, u32[]{:S(2)}, u32[]{:S(2)}) collective-permute-start(f32[1,128]{1,0:T(1,128)S(1)} %get-tuple-element.51), channel_id=1, source_target_pairs={{0,3},{1,0},{2,1},{3,2},{4,7},{5,4},{6,5},{7,6},{8,11},{9,8},{10,9... | collective-permute-start | bytes 1544 | tf_op jit(solution)/shard_map/ppermute | solution.py:305
  129.6 4.3 %layer.9 = (bf16[128,2048]{1,0:T(8,128)(2,1)S(1)}, f32[1,128]{1,0:T(1,128)S(1)}) custom-call(s32[1]{0:T(128)} %constant.42.clone.1.ids, bf16[1,128,2048]{2,1,0:T(8,128)(2,1)S(1)} %bitcast.32, bf16[256,2048]{1,0:T(8,128)(2,1)S(1)} %get-tuple-element.36.keys, bf16[256,2048]{1,0:T(8,128)(2,1)S(1)} %get-tuple-element.37.vals, ...), custom_call_target="tpu_custom_call" | custom-call | flops 1073741824 | bytes 3145728 | tf_op jit(solution)/shard_map/layer/pallas_call | solution.py:248
  143.2 9.4 %collective-permute-done.37.rest_0_ = f32[1,128]{1,0:T(1,128)S(1)} collective-permute-done((f32[1,128]{1,0:T(1,128)S(1)}, f32[1,128]{1,0:T(1,128)S(1)}, u32[]{:S(2)}, u32[]{:S(2)}) %collective-permute-start.37) | collective-permute-done | bytes 544 | tf_op jit(solution)/shard_map/ppermute | solution.py:314
  152.6 4.3 %layer.14 = (bf16[128,2048]{1,0:T(8,128)(2,1)S(1)}, f32[1,128]{1,0:T(1,128)S(1)}) custom-call(s32[1]{0:T(128)} %constant.42.clone.1.ids, bf16[1,128,2048]{2,1,0:T(8,128)(2,1)S(1)} %bitcast.36, bf16[256,2048]{1,0:T(8,128)(2,1)S(1)} %get-tuple-element.33.keys, bf16[256,2048]{1,0:T(8,128)(2,1)S(1)} %get-tuple-element.34.vals, ...), custom_call_target="tpu_custom_call" | custom-call | flops 1073741824 | bytes 3145728 | tf_op jit(solution)/shard_map/layer/pallas_call | solution.py:248
  158.8 3.2 %collective-permute-start.39 = (f32[1,128]{1,0:T(1,128)S(1)}, f32[1,128]{1,0:T(1,128)S(1)}, u32[]{:S(2)}, u32[]{:S(2)}) collective-permute-start(f32[1,128]{1,0:T(1,128)S(1)} %get-tuple-element.53.rest_0_), channel_id=1, source_target_pairs={{0,2},{1,3},{2,0},{3,1},{4,6},{5,7},{6,4},{7,5},{8,10},{9,11},{10,... | collective-permute-start | bytes 1544 | tf_op jit(solution)/shard_map/ppermute | solution.py:305
  162.0 4.3 %layer.10 = (bf16[128,2048]{1,0:T(8,128)(2,1)S(1)}, f32[1,128]{1,0:T(1,128)S(1)}) custom-call(s32[1]{0:T(128)} %constant.42.clone.1.ids, bf16[1,128,2048]{2,1,0:T(8,128)(2,1)S(1)} %bitcast.37, bf16[256,2048]{1,0:T(8,128)(2,1)S(1)} %get-tuple-element.40.keys, bf16[256,2048]{1,0:T(8,128)(2,1)S(1)} %copy-done.9, f32[8,128]{1,0:T(8,128)S(1)} %get-tuple-element.66.meta, ...), custom_call_target="tpu_custom_call" | custom-call | flops 1073741824 | bytes 3145728 | tf_op jit(solution)/shard_map/layer/pallas_call | solution.py:248
  166.3 2.7 %collective-permute-start.28 = (f32[1,128]{1,0:T(1,128)S(1)}, f32[1,128]{1,0:T(1,128)S(1)}, u32[]{:S(2)}, u32[]{:S(2)}) collective-permute-start(f32[1,128]{1,0:T(1,128)S(1)} %get-tuple-element.46.rest_0_), channel_id=1, source_target_pairs={{0,3},{1,0},{2,1},{3,2},{4,7},{5,4},{6,5},{7,6},{8,11},{9,8},{10,9... | collective-permute-start | bytes 1544 | tf_op jit(solution)/shard_map/ppermute | solution.py:305
  169.7 4.8 %layer.15 = (bf16[128,2048]{1,0:T(8,128)(2,1)S(1)}, f32[1,128]{1,0:T(1,128)}) custom-call(s32[1]{0:T(128)} %constant.42.clone.1.ids, bf16[1,128,2048]{2,1,0:T(8,128)(2,1)S(1)} %bitcast.35, bf16[256,2048]{1,0:T(8,128)(2,1)S(1)} %get-tuple-element.36.keys, bf16[256,2048]{1,0:T(8,128)(2,1)S(1)} %get-tuple-element.37.vals, f32[8,128]{1,0:T(8,128)S(1)} %get-tuple-element.65.meta, ...), custom_call_target="tpu_custom_call" | custom-call | flops 1073741824 | bytes 3145728 | tf_op jit(solution)/shard_map/layer/pallas_call | solution.py:248
  174.6 5.7 %collective-permute-start.41 = (bf16[128,2048]{1,0:T(8,128)(2,1)S(1)}, bf16[128,2048]{1,0:T(8,128)(2,1)S(1)}, u32[]{:S(2)}, u32[]{:S(2)}) collective-permute-start(bf16[128,2048]{1,0:T(8,128)(2,1)S(1)} %get-tuple-element.58), channel_id=1, source_target_pairs={{0,32},{32,0},{64,96},{96,64},{1,33},{33,1},{65,97},{97,65},{2,34}... | collective-permute-start | bytes 1572872 | tf_op jit(solution)/shard_map/ppermute | solution.py:308
  180.4 4.8 %layer.11 = (bf16[128,2048]{1,0:T(8,128)(2,1)S(1)}, f32[1,128]{1,0:T(1,128)}) custom-call(s32[1]{0:T(128)} %constant.42.clone.1.ids, bf16[1,128,2048]{2,1,0:T(8,128)(2,1)S(1)} %bitcast.34, bf16[256,2048]{1,0:T(8,128)(2,1)S(1)} %get-tuple-element.44.keys, bf16[256,2048]{1,0:T(8,128)(2,1)S(1)} %copy-done.35, f32[8,128]{1,0:T(8,128)S(1)} %get-tuple-element.66.meta, ...), custom_call_target="tpu_custom_call" | custom-call | flops 1073741824 | bytes 3145728 | tf_op jit(solution)/shard_map/layer/pallas_call | solution.py:248
  (178 shorter events, 65.5 us)
Async XLA Ops:
  0.0 62.9 %collective-permute-start.8 = (bf16[1,1280,2048]{2,1,0:T(8,128)(2,1)}, bf16[1,1280,2048]{2,1,0:T(8,128)(2,1)}, u32[]{:S(2)}, u32[]{:S(2)}) collective-permute-start(bf16[1,1280,2048]{2,1,0:T(8,128)(2,1)} %kw0.7), channel_id=1, source_target_pairs={{0,32},{32,0},{64,96},{96,64},{1,33},{33,1},{65,97},{97,65},{2,34}... | collective-permute-start | bytes 15728648 | tf_op jit(solution)/shard_map/ppermute | solution.py:308
  0.7 62.2 %collective-permute-start.9 = (bf16[1,1280,2048]{2,1,0:T(8,128)(2,1)}, bf16[1,1280,2048]{2,1,0:T(8,128)(2,1)}, u32[]{:S(2)}, u32[]{:S(2)}) collective-permute-start(bf16[1,1280,2048]{2,1,0:T(8,128)(2,1)} %vw0.7), channel_id=1, source_target_pairs={{0,32},{32,0},{64,96},{96,64},{1,33},{33,1},{65,97},{97,65},{2,34}... | collective-permute-start | bytes 15728648 | tf_op jit(solution)/shard_map/ppermute | solution.py:308
  11.2 15.8 %collective-permute-start = (bf16[64,1280]{1,0:T(8,128)(2,1)S(1)}, bf16[64,1280]{1,0:T(8,128)(2,1)S(1)}, u32[]{:S(2)}, u32[]{:S(2)}) collective-permute-start(bf16[64,1280]{1,0:T(8,128)(2,1)S(1)} %get-tuple-element.30), channel_id=1, source_target_pairs={{0,1},{1,2},{2,3},{3,0},{4,5},{5,6},{6,7},{7,4},{8,9},{9,10},{10,1... | collective-permute-start | bytes 491528 | tf_op jit(solution)/shard_map/ppermute | solution.py:305
  12.5 15.8 %collective-permute-start.1 = (bf16[64,1280]{1,0:T(8,128)(2,1)S(1)}, bf16[64,1280]{1,0:T(8,128)(2,1)}, u32[]{:S(2)}, u32[]{:S(2)}) collective-permute-start(bf16[64,1280]{1,0:T(8,128)(2,1)S(1)} %get-tuple-element.31), channel_id=1, source_target_pairs={{0,2},{1,3},{2,0},{3,1},{4,6},{5,7},{6,4},{7,5},{8,10},{9,11},{10,... | collective-permute-start | bytes 491528 | tf_op jit(solution)/shard_map/ppermute | solution.py:305
  15.2 13.2 %collective-permute-start.2 = (bf16[64,1280]{1,0:T(8,128)(2,1)S(1)}, bf16[64,1280]{1,0:T(8,128)(2,1)}, u32[]{:S(2)}, u32[]{:S(2)}) collective-permute-start(bf16[64,1280]{1,0:T(8,128)(2,1)S(1)} %get-tuple-element.32), channel_id=1, source_target_pairs={{0,3},{1,0},{2,1},{3,2},{4,7},{5,4},{6,5},{7,6},{8,11},{9,8},{10,9... | collective-permute-start | bytes 491528 | tf_op jit(solution)/shard_map/ppermute | solution.py:305
  28.4 19.1 %collective-permute-start.13 = (f32[4,128]{1,0:T(4,128)S(1)}, f32[4,128]{1,0:T(4,128)S(1)}, u32[]{:S(2)}, u32[]{:S(2)}) collective-permute-start(f32[4,128]{1,0:T(4,128)S(1)} %multiply_reduce_fusion), channel_id=1, source_target_pairs={{0,3},{1,0},{2,1},{3,2},{4,7},{5,4},{6,5},{7,6},{8,11},{9,8},{10,9... | collective-permute-start | bytes 6152 | tf_op jit(solution)/shard_map/ppermute | solution.py:305
  39.8 12.5 %collective-permute-start.12 = (f32[4,128]{1,0:T(4,128)S(1)}, f32[4,128]{1,0:T(4,128)S(1)}, u32[]{:S(2)}, u32[]{:S(2)}) collective-permute-start(f32[4,128]{1,0:T(4,128)S(1)} %multiply_reduce_fusion), channel_id=1, source_target_pairs={{0,2},{1,3},{2,0},{3,1},{4,6},{5,7},{6,4},{7,5},{8,10},{9,11},{10,... | collective-permute-start | bytes 6152 | tf_op jit(solution)/shard_map/ppermute | solution.py:305
  56.7 31.2 %collective-permute-start.7 = (bf16[64,1280]{1,0:T(8,128)(2,1)S(1)}, bf16[64,1280]{1,0:T(8,128)(2,1)S(1)}, u32[]{:S(2)}, u32[]{:S(2)}) collective-permute-start(bf16[64,1280]{1,0:T(8,128)(2,1)S(1)} %select_select_fusion.a0), channel_id=1, source_target_pairs={{0,3},{1,0},{2,1},{3,2},{4,7},{5,4},{6,5},{7,6},{8,11},{9,8},{10,9... | collective-permute-start | bytes 491528 | tf_op jit(solution)/shard_map/ppermute | solution.py:305
  59.2 29.3 %collective-permute-start.6 = (bf16[64,1280]{1,0:T(8,128)(2,1)S(1)}, bf16[64,1280]{1,0:T(8,128)(2,1)S(1)}, u32[]{:S(2)}, u32[]{:S(2)}) collective-permute-start(bf16[64,1280]{1,0:T(8,128)(2,1)S(1)} %select_select_fusion.a0), channel_id=1, source_target_pairs={{0,2},{1,3},{2,0},{3,1},{4,6},{5,7},{6,4},{7,5},{8,10},{9,11},{10,... | collective-permute-start | bytes 491528 | tf_op jit(solution)/shard_map/ppermute | solution.py:305
  62.9 25.7 %collective-permute-start.5 = (bf16[64,1280]{1,0:T(8,128)(2,1)S(1)}, bf16[64,1280]{1,0:T(8,128)(2,1)S(1)}, u32[]{:S(2)}, u32[]{:S(2)}) collective-permute-start(bf16[64,1280]{1,0:T(8,128)(2,1)S(1)} %select_select_fusion.a0), channel_id=1, source_target_pairs={{0,1},{1,2},{2,3},{3,0},{4,5},{5,6},{6,7},{7,4},{8,9},{9,10},{10,1... | collective-permute-start | bytes 491528 | tf_op jit(solution)/shard_map/ppermute | solution.py:305
  85.2 35.3 %collective-permute-start.32 = (f32[1,128]{1,0:T(1,128)S(1)}, f32[1,128]{1,0:T(1,128)S(1)}, u32[]{:S(2)}, u32[]{:S(2)}) collective-permute-start(f32[1,128]{1,0:T(1,128)S(1)} %get-tuple-element.49.rest_0_), channel_id=1, source_target_pairs={{0,3},{1,0},{2,1},{3,2},{4,7},{5,4},{6,5},{7,6},{8,11},{9,8},{10,9... | collective-permute-start | bytes 1544 | tf_op jit(solution)/shard_map/ppermute | solution.py:305
  87.9 32.7 %collective-permute-start.31 = (f32[1,128]{1,0:T(1,128)S(1)}, f32[1,128]{1,0:T(1,128)S(1)}, u32[]{:S(2)}, u32[]{:S(2)}) collective-permute-start(f32[1,128]{1,0:T(1,128)S(1)} %get-tuple-element.49.rest_0_), channel_id=1, source_target_pairs={{0,2},{1,3},{2,0},{3,1},{4,6},{5,7},{6,4},{7,5},{8,10},{9,11},{10,... | collective-permute-start | bytes 1544 | tf_op jit(solution)/shard_map/ppermute | solution.py:305
  87.9 32.7 %collective-permute-start.30 = (f32[1,128]{1,0:T(1,128)S(1)}, f32[1,128]{1,0:T(1,128)S(1)}, u32[]{:S(2)}, u32[]{:S(2)}) collective-permute-start(f32[1,128]{1,0:T(1,128)S(1)} %get-tuple-element.49.rest_0_), channel_id=1, source_target_pairs={{0,1},{1,2},{2,3},{3,0},{4,5},{5,6},{6,7},{7,4},{8,9},{9,10},{10,1... | collective-permute-start | bytes 1544 | tf_op jit(solution)/shard_map/ppermute | solution.py:305
  101.6 26.1 %collective-permute-start.16 = (f32[1,128]{1,0:T(1,128)S(1)}, f32[1,128]{1,0:T(1,128)S(1)}, u32[]{:S(2)}, u32[]{:S(2)}) collective-permute-start(f32[1,128]{1,0:T(1,128)S(1)} %get-tuple-element.38.rest_0_), channel_id=1, source_target_pairs={{0,3},{1,0},{2,1},{3,2},{4,7},{5,4},{6,5},{7,6},{8,11},{9,8},{10,9... | collective-permute-start | bytes 1544 | tf_op jit(solution)/shard_map/ppermute | solution.py:305
  103.8 24.6 %collective-permute-start.15 = (f32[1,128]{1,0:T(1,128)S(1)}, f32[1,128]{1,0:T(1,128)S(1)}, u32[]{:S(2)}, u32[]{:S(2)}) collective-permute-start(f32[1,128]{1,0:T(1,128)S(1)} %get-tuple-element.38.rest_0_), channel_id=1, source_target_pairs={{0,2},{1,3},{2,0},{3,1},{4,6},{5,7},{6,4},{7,5},{8,10},{9,11},{10,... | collective-permute-start | bytes 1544 | tf_op jit(solution)/shard_map/ppermute | solution.py:305
  128.3 24.3 %collective-permute-start.33 = (bf16[128,2048]{1,0:T(8,128)(2,1)S(1)}, bf16[128,2048]{1,0:T(8,128)(2,1)S(1)}, u32[]{:S(2)}, u32[]{:S(2)}) collective-permute-start(bf16[128,2048]{1,0:T(8,128)(2,1)S(1)} %get-tuple-element.50), channel_id=1, source_target_pairs={{0,64},{32,96},{1,65},{33,97},{2,66},{34,98},{3,67},{35,99},{4,68}... | collective-permute-start | bytes 1572872 | tf_op jit(solution)/shard_map/ppermute | solution.py:314
  137.8 24.2 %collective-permute-start.17 = (bf16[128,2048]{1,0:T(8,128)(2,1)S(1)}, bf16[128,2048]{1,0:T(8,128)(2,1)S(1)}, u32[]{:S(2)}, u32[]{:S(2)}) collective-permute-start(bf16[128,2048]{1,0:T(8,128)(2,1)S(1)} %get-tuple-element.39), channel_id=1, source_target_pairs={{0,64},{32,96},{1,65},{33,97},{2,66},{34,98},{3,67},{35,99},{4,68}... | collective-permute-start | bytes 1572872 | tf_op jit(solution)/shard_map/ppermute | solution.py:314
  139.1 13.5 %collective-permute-start.37 = (f32[1,128]{1,0:T(1,128)S(1)}, f32[1,128]{1,0:T(1,128)S(1)}, u32[]{:S(2)}, u32[]{:S(2)}) collective-permute-start(f32[1,128]{1,0:T(1,128)S(1)} %add_add_fusion.1), channel_id=1, source_target_pairs={{0,64},{32,96},{1,65},{33,97},{2,66},{34,98},{3,67},{35,99},{4,68}... | collective-permute-start | bytes 1544 | tf_op jit(solution)/shard_map/ppermute | solution.py:314
  141.7 20.3 %collective-permute-start.25 = (f32[1,128]{1,0:T(1,128)S(1)}, f32[1,128]{1,0:T(1,128)S(1)}, u32[]{:S(2)}, u32[]{:S(2)}) collective-permute-start(f32[1,128]{1,0:T(1,128)S(1)} %add_add_fusion.2), channel_id=1, source_target_pairs={{0,64},{32,96},{1,65},{33,97},{2,66},{34,98},{3,67},{35,99},{4,68}... | collective-permute-start | bytes 1544 | tf_op jit(solution)/shard_map/ppermute | solution.py:314
  156.9 12.2 %collective-permute-start.40 = (f32[1,128]{1,0:T(1,128)S(1)}, f32[1,128]{1,0:T(1,128)S(1)}, u32[]{:S(2)}, u32[]{:S(2)}) collective-permute-start(f32[1,128]{1,0:T(1,128)S(1)} %get-tuple-element.53.rest_0_), channel_id=1, source_target_pairs={{0,3},{1,0},{2,1},{3,2},{4,7},{5,4},{6,5},{7,6},{8,11},{9,8},{10,9... | collective-permute-start | bytes 1544 | tf_op jit(solution)/shard_map/ppermute | solution.py:305
  166.3 14.1 %collective-permute-start.28 = (f32[1,128]{1,0:T(1,128)S(1)}, f32[1,128]{1,0:T(1,128)S(1)}, u32[]{:S(2)}, u32[]{:S(2)}) collective-permute-start(f32[1,128]{1,0:T(1,128)S(1)} %get-tuple-element.46.rest_0_), channel_id=1, source_target_pairs={{0,3},{1,0},{2,1},{3,2},{4,7},{5,4},{6,5},{7,6},{8,11},{9,8},{10,9... | collective-permute-start | bytes 1544 | tf_op jit(solution)/shard_map/ppermute | solution.py:305
  169.0 11.3 %collective-permute-start.27 = (f32[1,128]{1,0:T(1,128)S(1)}, f32[1,128]{1,0:T(1,128)S(1)}, u32[]{:S(2)}, u32[]{:S(2)}) collective-permute-start(f32[1,128]{1,0:T(1,128)S(1)} %get-tuple-element.46.rest_0_), channel_id=1, source_target_pairs={{0,2},{1,3},{2,0},{3,1},{4,6},{5,7},{6,4},{7,5},{8,10},{9,11},{10,... | collective-permute-start | bytes 1544 | tf_op jit(solution)/shard_map/ppermute | solution.py:305
  169.0 11.3 %collective-permute-start.26 = (f32[1,128]{1,0:T(1,128)S(1)}, f32[1,128]{1,0:T(1,128)S(1)}, u32[]{:S(2)}, u32[]{:S(2)}) collective-permute-start(f32[1,128]{1,0:T(1,128)S(1)} %get-tuple-element.46.rest_0_), channel_id=1, source_target_pairs={{0,1},{1,2},{2,3},{3,0},{4,5},{5,6},{6,7},{7,4},{8,9},{9,10},{10,1... | collective-permute-start | bytes 1544 | tf_op jit(solution)/shard_map/ppermute | solution.py:305
  174.6 11.7 %collective-permute-start.41 = (bf16[128,2048]{1,0:T(8,128)(2,1)S(1)}, bf16[128,2048]{1,0:T(8,128)(2,1)S(1)}, u32[]{:S(2)}, u32[]{:S(2)}) collective-permute-start(bf16[128,2048]{1,0:T(8,128)(2,1)S(1)} %get-tuple-element.58), channel_id=1, source_target_pairs={{0,32},{32,0},{64,96},{96,64},{1,33},{33,1},{65,97},{97,65},{2,34}... | collective-permute-start | bytes 1572872 | tf_op jit(solution)/shard_map/ppermute | solution.py:308
  (58 other events, 440.3 us)

commit v2 on v0

v2 whole, which is shorter than its diff:
```python
import functools

import jax
import jax.numpy as jnp
from jax import lax
from jax.experimental import pallas as pl
from jax.experimental.pallas import tpu as pltpu
from jax.sharding import PartitionSpec as P

D = 8192
HEAD = 128
LATENTS = 64
PHEAD = 96
EPS = 1e-05
NEG = -1e30
LOG2E = 1.4426950408889634
F32 = jnp.float32
BF16 = jnp.bfloat16
MIB = 1024 * 1024
SPARE = 16


def normalize(v):
    mean = jnp.mean(v, axis=-1, keepdims=True)
    cent = v - mean
    var = jnp.mean(cent * cent, axis=-1, keepdims=True)
    return cent * lax.rsqrt(var + EPS)


def dot(a, b):
    return jnp.dot(a, b, preferred_element_type=F32)


def dot_nt(a, b):
    return lax.dot_general(a, b, (((1,), (1,)), ((), ())), preferred_element_type=F32)


def up16(n):
    return -(-n // 16) * 16


def up128(n):
    return -(-n // 128) * 128


def near(a):
    return pltpu.with_memory_space_constraint(a, pltpu.VMEM)


def away(a):
    return pltpu.with_memory_space_constraint(a, pltpu.HBM)


IN_VMEM = pl.BlockSpec(memory_space=pltpu.VMEM)
IN_SMEM = pl.BlockSpec(memory_space=pltpu.SMEM)
IN_HBM = pl.BlockSpec(memory_space=pltpu.HBM)


def prepare(lat, qp, kp, vp, tail, ctx, pk, pv, pqm):
    inner = qp.shape[1]
    heads = inner // PHEAD
    rows = ctx.shape[0]
    cut = inner // 256 * 256
    side = inner - cut
    tail[:, :side] = kp[:, cut:]
    tail[:, side:] = vp[:, cut:]
    base = normalize(lat[...].astype(F32)).astype(BF16)
    pq = dot(base, qp[...]).astype(BF16).astype(F32)
    which = lax.broadcasted_iota(jnp.int32, (LATENTS, inner), 1) // PHEAD
    for h in range(heads):
        pqm[h * LATENTS : (h + 1) * LATENTS, :] = jnp.where(which == h, pq, 0.0).astype(BF16)
    project_rows(base, 0, kp, vp, tail, pk, pv)
    pad = pk.shape[0] - LATENTS - rows
    if pad:
        pk[LATENTS + rows :, :] = jnp.zeros((pad, inner), BF16)
        pv[LATENTS + rows :, :inner] = jnp.zeros((pad, inner), BF16)
    pv[:, inner:] = jnp.ones((pv.shape[0], 128), BF16)
    ctx[rows - 16 :, :] = jnp.zeros((16, ctx.shape[1]), BF16)


def project_rows(a, at, kp, vp, tail, pk, pv):
    stop = at + a.shape[0]
    inner = kp.shape[1]
    cut = inner // 256 * 256
    side = inner - cut
    pk[at:stop, :cut] = dot(a, kp[:, :cut]).astype(BF16)
    pv[at:stop, :cut] = dot(a, vp[:, :cut]).astype(BF16)
    both = dot(a, tail[...]).astype(BF16)
    pk[at:stop, cut:] = both[:, :side]
    pv[at:stop, cut:inner] = both[:, side:]


def one_image(frame, kp, vp, op, tail, ctx, pk, pv, pqm):
    patches = frame.shape[0]
    inner = kp.shape[1]
    keys = LATENTS + patches
    for r in range(0, patches, 64):
        end = min(r + 64, patches)
        ctx[r:end, :] = normalize(frame[r:end, :].astype(F32)).astype(BF16)
    project_rows(ctx[...], LATENTS, kp, vp, tail, pk, pv)
    score = dot_nt(pqm[...], pk[...]) * (PHEAD ** (-0.5) * LOG2E)
    lane = lax.broadcasted_iota(jnp.int32, score.shape, 1)
    score = jnp.where(lane < keys, score, NEG)
    e = jnp.exp2(score - jnp.max(score, axis=1, keepdims=True)).astype(BF16)
    mix = dot(e, pv[...])
    inverse = 1.0 / mix[:, inner:]
    tiles = []
    for j in range(inner // 128):
        at = lax.broadcasted_iota(jnp.int32, (LATENTS, 128), 1) + j * 128
        tile = jnp.zeros((LATENTS, 128), F32)
        for h in range(j * 128 // PHEAD, (j * 128 + 127) // PHEAD + 1):
            rows_h = slice(h * LATENTS, (h + 1) * LATENTS)
            value = mix[rows_h, j * 128 : (j + 1) * 128] * inverse[rows_h, :]
            tile = jnp.where(at // PHEAD == h, value, tile)
        tiles.append(tile.astype(BF16))
    return dot(jnp.concatenate(tiles, axis=1), op[...])


def resample_scratch(patches, vdim, inner):
    rows = up16(patches)
    padded = up128(LATENTS + rows)
    cut = inner // 256 * 256
    return [
        pltpu.VMEM((vdim, 2 * (inner - cut)), BF16),
        pltpu.VMEM((rows, vdim), BF16),
        pltpu.VMEM((padded, inner), BF16),
        pltpu.VMEM((padded, inner + 128), BF16),
        pltpu.VMEM((inner // PHEAD * LATENTS, inner), BF16),
    ]


def resample_sent_kernel(n, ids, lat, feat, hid, *rest):
    weights, rest = rest[:4], rest[4:]
    sent, squares, rest = rest[:n], rest[n], rest[n + 1 :]
    held, (frames, updates, hid0, hid1), work, sems = rest[:4], rest[4:8], rest[8:-1], rest[-1]
    qp, kp, vp, op = held
    loads = [pltpu.make_async_copy(a, b, sems.at[i]) for i, (a, b) in enumerate(zip(weights, held))]
    loads.append(pltpu.make_async_copy(hid.at[ids[n]], hid0, sems.at[4]))
    loads.append(pltpu.make_async_copy(hid.at[ids[n] + 2], hid1, sems.at[5]))
    images = [pltpu.make_async_copy(feat.at[ids[i]], frames.at[i], sems.at[6 + i]) for i in range(n)]
    for load in loads[:3] + images + loads[3:]:
        load.start()
    for load in loads[:3]:
        load.wait()
    prepare(lat, qp, kp, vp, *work)
    for load in images + loads[3:4]:
        load.wait()

    def step(i, carry):
        updates[i] = one_image(frames.at[i], kp, vp, op, *work).astype(BF16)
        return carry

    lax.fori_loop(0, n, step, 0)
    lines = []
    for load, a in zip(loads[4:], (hid0, hid1)):
        load.wait()
        acc = jnp.zeros((a.shape[0], 128), F32)
        for at in range(0, a.shape[1], 128):
            v = a[:, at : at + 128].astype(F32)
            acc = acc + v * v
        lines.append(jnp.sum(acc.T, axis=0, keepdims=True))
    squares[...] = jnp.concatenate(lines, axis=0)
    high = [line.astype(BF16).astype(F32) for line in lines]
    low = [line - h for line, h in zip(lines, high)]
    spare = jnp.zeros((1, sent[0].shape[1] - 4 * 128), F32)
    line = jnp.concatenate(high + low + [spare], axis=1)
    first = lax.broadcasted_iota(jnp.int32, (SPARE, line.shape[1]), 0) == 0
    line = jnp.where(first, line, 0.0).astype(BF16)
    for i in range(n):
        sent[i][0:LATENTS, :] = updates[i]
        sent[i][LATENTS:, :] = line


def resample_sent(ids, features, latent_param, hidden, weights):
    n = ids.shape[0] - 1
    _, patches, vdim = features.shape
    _, rows, width = hidden.shape
    inner = weights[0].shape[1]
    return pl.pallas_call(
        functools.partial(resample_sent_kernel, n),
        out_shape=[pltpu.VMEM((LATENTS + SPARE, vdim), BF16)] * n
        + [pltpu.VMEM((2, rows), F32)],
        in_specs=[IN_SMEM, IN_VMEM] + [IN_HBM] * 6,
        out_specs=[IN_VMEM] * (n + 1),
        scratch_shapes=[pltpu.VMEM(w.shape, BF16) for w in weights]
        + [
            pltpu.VMEM((n, patches, vdim), BF16),
            pltpu.VMEM((n, LATENTS, vdim), BF16),
            pltpu.VMEM((rows, width), BF16),
            pltpu.VMEM((rows, width), BF16),
        ]
        + resample_scratch(patches, vdim, inner)
        + [pltpu.SemaphoreType.DMA((6 + n,))],
        compiler_params=pltpu.CompilerParams(vmem_limit_bytes=24 * MIB),
        name="resample",
    )(ids, latent_param, features, away(hidden), *[away(w) for w in weights])


def resample_own_kernel(ids, lat, feat, *rest):
    weights, out, held, frame, work, sems = (
        rest[:4],
        rest[4],
        rest[5:9],
        rest[9],
        rest[10:-1],
        rest[-1],
    )
    qp, kp, vp, op = held
    loads = [pltpu.make_async_copy(a, b, sems.at[i]) for i, (a, b) in enumerate(zip(weights, held))]
    loads.append(pltpu.make_async_copy(feat.at[ids[0]], frame, sems.at[4]))
    for load in loads:
        load.start()
    for load in loads[:3]:
        load.wait()
    prepare(lat, qp, kp, vp, *work)
    for load in loads[3:]:
        load.wait()
    out[...] = one_image(frame, kp, vp, op, *work)


def resample_own(ids, features, latent_param, weights):
    _, patches, vdim = features.shape
    inner = weights[0].shape[1]
    return pl.pallas_call(
        resample_own_kernel,
        out_shape=pltpu.VMEM((LATENTS, vdim), F32),
        in_specs=[IN_SMEM, IN_VMEM] + [IN_HBM] * 5,
        out_specs=IN_VMEM,
        scratch_shapes=[pltpu.VMEM(w.shape, BF16) for w in weights]
        + [pltpu.VMEM((patches, vdim), BF16)]
        + resample_scratch(patches, vdim, inner)
        + [pltpu.SemaphoreType.DMA((5,))],
        compiler_params=pltpu.CompilerParams(vmem_limit_bytes=20 * MIB),
        name="resample",
    )(ids, latent_param, features, *[away(w) for w in weights])


def combine_kernel(lat, squares, own, a, b, c, out, total_squares):
    total = own[...]
    sums = squares[...]
    count = squares.shape[0]
    for part in (a, b, c):
        total = total + part[:LATENTS, :].astype(F32)
        line = part[LATENTS:, :].astype(F32)[0:1, :]
        at = lambda i: line[:, i * 128 : (i + 1) * 128]
        sums = sums + jnp.concatenate([at(i) + at(count + i) for i in range(count)], axis=0)
    out[...] = normalize(lat[...].astype(F32) + total).astype(BF16)
    total_squares[...] = sums


def combine(latent_param, squares, own, parts):
    return pl.pallas_call(
        combine_kernel,
        out_shape=[
            pltpu.VMEM(latent_param.shape, BF16),
            pltpu.VMEM(squares.shape, F32),
        ],
        in_specs=[IN_VMEM] * 6,
        out_specs=[IN_VMEM] * 2,
        compiler_params=pltpu.CompilerParams(vmem_limit_bytes=8 * MIB),
        name="combine",
    )(latent_param, squares, near(own), *[near(p) for p in parts])


TILE = 512
AHEAD = 3


def project_kernel(count, moved, flags, *refs):
    chunks, refs = refs[:count], refs[count:]
    hid, own_k, own_v, other_k, other_v = refs[:5]
    keys, vals, far_keys, far_vals = refs[5:9]
    near_hid = refs[9 : 9 + moved]
    chosen, tiles, sems, out_sems, hid_sems = refs[9 + moved :]
    width = keys.shape[1]
    steps = 2 * (width // TILE)

    def fetch(step):
        cols = pl.ds(pl.multiple_of(step // 2 * TILE, TILE), TILE)

        def one(src):
            return pltpu.make_async_copy(src.at[0, :, cols], tiles.at[step], sems.at[step])

        return one

    def start(step, of_own, of_other):
        @pl.when(flags[0] == 0)
        def _():
            fetch(step)(of_own).start()

        @pl.when(flags[0] != 0)
        def _():
            fetch(step)(of_other).start()

    for step in range(AHEAD):
        start(step, *((own_v, other_v) if step % 2 else (own_k, other_k)))
    loads = [
        pltpu.make_async_copy(hid.at[flags[1 + i]], near_hid[i], hid_sems.at[i])
        for i in range(moved)
    ]
    for i, a in enumerate(chunks):
        chosen[i * LATENTS : (i + 1) * LATENTS, :] = a[...]

    def store(step, src, dst):
        cols = pl.ds(pl.multiple_of(step // 2 * TILE, TILE), TILE)
        return pltpu.make_async_copy(src.at[:, cols], dst.at[:, cols], out_sems.at[step])

    def column(j, carry):
        cols = pl.ds(pl.multiple_of(j * TILE, TILE), TILE)
        for i, (out, far) in enumerate(((keys, far_keys), (vals, far_vals))):
            step = 2 * j + i
            fetch(step)(own_k).wait()

            @pl.when(step + AHEAD < steps)
            def _():
                if (i + AHEAD) % 2:
                    start(step + AHEAD, own_v, other_v)
                else:
                    start(step + AHEAD, own_k, other_k)

            out[:, cols] = dot(chosen[...], tiles[step]).astype(BF16)
            store(step, out, far).start()
        return carry

    lax.fori_loop(0, steps // 2, column, 0)
    for load in loads:
        load.start()
    for step in range(steps):
        store(step, keys, far_keys).wait()
    for load in loads:
        load.wait()


def project(flags, chunks, own, other, hidden, moved):
    vdim, width = own[0].shape[1:]
    rows = len(chunks) * LATENTS
    steps = 2 * (width // TILE)
    return pl.pallas_call(
        functools.partial(project_kernel, len(chunks), moved),
        out_shape=[pltpu.VMEM((rows, width), BF16)] * 2
        + [pltpu.HBM((rows, width), BF16)] * 2
        + [pltpu.VMEM(hidden.shape[1:], BF16)] * moved,
        in_specs=[IN_SMEM] + [IN_VMEM] * len(chunks) + [IN_HBM] * 5,
        out_specs=[IN_VMEM] * 2 + [IN_HBM] * 2 + [IN_VMEM] * moved,
        scratch_shapes=[
            pltpu.VMEM((rows, vdim), BF16),
            pltpu.VMEM((steps, vdim, TILE), BF16),
            pltpu.SemaphoreType.DMA((steps,)),
            pltpu.SemaphoreType.DMA((steps,)),
            pltpu.SemaphoreType.DMA((2,)),
        ],
        compiler_params=pltpu.CompilerParams(vmem_limit_bytes=24 * MIB),
        cost_estimate=pl.CostEstimate(
            flops=4 * rows * vdim * width, bytes_accessed=0, transcendentals=0
        ),
        name="project",
    )(flags, *[near(a) for a in chunks], *[away(a) for a in (hidden, *own, *other)])


def layer_kernel(row, places, count, ahead, streamed, *refs):
    batches = len(places)
    xs, metas, refs = refs[:batches], refs[batches : 2 * batches], refs[2 * batches :]
    keys, vals, refs = refs[0], refs[1], refs[2:]
    squares, before, refs = refs[:count], refs[count : count + ahead], refs[count + ahead :]
    ys, square_out, refs = refs[:batches], refs[batches], refs[batches + 1 :]
    scale_s, bias_s, high_s, half_s, gate_s, acc = refs[:6]
    rows = xs[0].shape[0]
    heads = xs[0].shape[1] // HEAD
    slots = 4 * LATENTS
    loads = []
    if streamed:
        near_keys, near_vals, sems = refs[6:]
        for i, (at, _) in enumerate(places):
            loads.append(
                [
                    pltpu.make_async_copy(
                        src.at[pl.ds(at * slots, slots)], dst.at[i], sems.at[i, j]
                    )
                    for j, (src, dst) in enumerate(((keys, near_keys), (vals, near_vals)))
                ]
            )
        for load in loads[0]:
            load.start()

    total = squares[0][...]
    for part in squares[1:]:
        total = total + part[...]
    ones = jnp.ones((slots, HEAD), BF16)
    lines = [b[...] for b in before]
    for i, (at, line) in enumerate(places):
        scale = lax.rsqrt(total[line : line + 1, :] / D + EPS) * (HEAD ** (-0.5) * LOG2E)
        spare = jnp.zeros((rows - 3, rows), F32)
        gate = metas[i][row : row + 1, :]
        cols = jnp.concatenate([scale, metas[i][0:1, :], gate, spare], axis=0).T
        slot = jnp.broadcast_to(cols[:, 1:2], (rows, HEAD))
        scale_s[...] = jnp.broadcast_to(cols[:, 0:1], (rows, HEAD))
        gate_s[...] = jnp.broadcast_to(cols[:, 2:3], (rows, HEAD))
        upper = jnp.where(slot > 1.5, 1.0, 0.0)
        high_s[...] = upper
        half_s[...] = upper.astype(BF16)
        half = (lax.broadcasted_iota(jnp.int32, (rows, HEAD), 1) // LATENTS).astype(F32)
        bias_s[...] = jnp.where(slot - 2.0 * upper == half, 0.0, NEG)
        high = high_s[...] > 0.5
        if streamed:
            for load in loads[i]:
                load.wait()
            for load in loads[i + 1] if i + 1 < batches else ():
                load.start()
        sums = jnp.zeros((rows, HEAD), F32)
        for h in range(heads):
            cols = slice(h * HEAD, (h + 1) * HEAD)
            if streamed:
                k, v = near_keys[i, :, cols], near_vals[i, :, cols]
            else:
                k = keys[at * slots : (at + 1) * slots, cols]
                v = vals[at * slots : (at + 1) * slots, cols]
            q = xs[i][:, cols]
            score = dot_nt(q, k)
            t = jnp.where(high, score[:, HEAD:], score[:, :HEAD]) * scale_s[...] + bias_s[...]
            e = jnp.exp2(t - jnp.max(t, axis=1, keepdims=True)).astype(BF16)
            e_high = e * half_s[...]
            weight = jnp.concatenate([e - e_high, e_high], axis=1)
            mixed = dot(weight, jnp.concatenate([v, ones], axis=1))
            attn = mixed[:, :HEAD] / mixed[:, HEAD:]
            out = (q.astype(F32) + gate_s[...] * attn).astype(BF16)
            ys[i][:, cols] = out
            of = out.astype(F32)
            sums = sums + of * of
        acc[...] = sums
        lines.append(jnp.sum(acc[...].T, axis=0, keepdims=True))
    square_out[...] = jnp.concatenate(lines, axis=0)


def layer(row, xs, metas, kv, places, squares, before=(), streamed=False):
    keys, vals = kv
    rows, width = xs[0].shape
    slots = 4 * LATENTS
    batches = len(xs)
    scratch = pltpu.VMEM((rows, HEAD), F32)
    place = away if streamed else near
    where = IN_HBM if streamed else IN_VMEM
    extra = [pltpu.VMEM((batches, slots, width), BF16)] * 2 + [pltpu.SemaphoreType.DMA((batches, 2))]
    return pl.pallas_call(
        functools.partial(layer_kernel, row, places, len(squares), len(before), streamed),
        out_shape=[pltpu.VMEM((rows, width), BF16)] * batches
        + [pltpu.VMEM((batches + len(before), rows), F32)],
        in_specs=[IN_VMEM] * (2 * batches)
        + [where, where]
        + [IN_VMEM] * (len(squares) + len(before)),
        out_specs=[IN_VMEM] * (batches + 1),
        scratch_shapes=[scratch] * 3
        + [pltpu.VMEM((rows, HEAD), BF16)]
        + [scratch] * 2
        + (extra if streamed else []),
        compiler_params=pltpu.CompilerParams(vmem_limit_bytes=12 * MIB),
        cost_estimate=pl.CostEstimate(
            flops=16 * batches * rows * slots * width,
            bytes_accessed=0,
            transcendentals=batches * rows * width,
        ),
        name="layer",
    )(
        *[near(x) for x in xs],
        *metas,
        place(keys),
        place(vals),
        *[near(a) for a in squares],
        *[near(a) for a in before],
    )


def body(
    features,
    latent_param,
    query_proj,
    key_proj,
    value_proj,
    out_proj,
    hidden,
    key_weight,
    value_weight,
    gate_angle,
    group_images,
    token_slot,
    attend,
):
    s = lax.axis_index("section")
    c = lax.axis_index("seq")
    m = lax.axis_index("mp")
    core = s & 1
    far = s >> 1
    mates = lax.axis_size("mp")
    seqs = lax.axis_size("seq")
    sections = lax.axis_size("section")

    def mp_shift(a, k):
        return lax.ppermute(a, "mp", [(i, (i + k) % mates) for i in range(mates)])

    def core_swap(a):
        return lax.ppermute(a, "section", [(i, i ^ 1) for i in range(sections)])

    def far_swap(a):
        return lax.ppermute(a, "section", [(i, i ^ 2) for i in range(sections)])

    def cross(a):
        return lax.ppermute(a, "section", [(0, 2), (1, 3)])

    def spread(a):
        return [a] + [mp_shift(a, k) for k in (1, 2, 3)]

    other_w = (core_swap(key_weight), core_swap(value_weight))
    gate_own = jnp.broadcast_to(jnp.tanh(gate_angle)[:, None], (1, 128))
    gate_other = core_swap(gate_own)
    gate_first = jnp.where(core == 0, gate_own, gate_other)
    gate_second = jnp.where(core == 0, gate_other, gate_own)

    order = jnp.stack([(m + 2) & 3, (m + 1) & 3, (m + 3) & 3, core]).astype(jnp.int32)
    weights = (query_proj, key_proj, value_proj, out_proj)
    p2, p1, p3, squares = resample_sent(order, features, latent_param, hidden, weights)
    r2, r1, r3 = mp_shift(p2, 2), mp_shift(p1, 1), mp_shift(p3, 3)
    p0 = resample_own(m[None].astype(jnp.int32), features, latent_param, weights)
    latents, entering = combine(latent_param, squares, p0, (r1, r2, r3))

    left = lax.ppermute(latents, "seq", [(i, i + 1) for i in range(seqs - 1)])
    right = lax.ppermute(latents, "seq", [(i + 1, i) for i in range(seqs - 1)])
    firsts = group_images[:, 0, 0]
    start = lax.dynamic_index_in_dim(firsts, s, 0, keepdims=False)
    where_is = ((start + ((m - start) & 3)) >> 2) - c
    picked = jnp.where(where_is == 0, latents, jnp.where(where_is < 0, left, right))
    chosen = spread(picked) + spread(far_swap(picked))

    block = (m - firsts[:, None] - token_slot[:, 0, :]) & 3
    alive = attend[:, 0, :].astype(F32)
    rows = jnp.stack(
        [block.astype(F32), alive * gate_first, alive * gate_second]
        + [jnp.zeros_like(alive)] * 5,
        axis=1,
    )
    meta_own = lax.dynamic_index_in_dim(rows, s, 0, keepdims=False)
    meta_far = lax.dynamic_index_in_dim(rows, s ^ 2, 0, keepdims=False)

    own_w = (key_weight, value_weight)
    flags_first = jnp.stack([core, core, core + 2]).astype(jnp.int32)
    flags_second = jnp.stack([1 - core, core, core + 2]).astype(jnp.int32)
    k, v, k_away, v_away, hidden0, hidden1 = project(
        flags_first, chosen, own_w, other_w, hidden, 2
    )
    first, first_away = (k, v), (k_away, v_away)
    k, v, k_away, v_away = project(flags_second, chosen, own_w, other_w, hidden, 0)
    second, second_away = (k, v), (k_away, v_away)

    metas = [meta_own, meta_far]
    a0, a1, qa = layer(1, [hidden0, hidden1], metas, first, ((0, 0), (1, 1)), [entering])
    qa = spread(qa)
    b0, qb0 = layer(2, [a0], [meta_own], second, ((0, 0),), qa)
    x0 = cross(b0)
    b1, qb = layer(2, [a1], [meta_far], second, ((1, 1),), qa, [qb0])
    x1 = cross(b1)
    qb = cross(sum(spread(qb)))

    metas = [meta_far, meta_own]
    turned = ((1, 0), (0, 1))
    c0, c1, qc = layer(1, [x0, x1], metas, first_away, turned, [qb], streamed=True)
    qc = spread(qc)
    d0, d1, _ = layer(2, [c0, c1], metas, second_away, turned, qc, streamed=True)

    def split(a, b, c_, d_):
        first = jnp.where(far == 0, a, c_)
        second = jnp.where(far == 0, b, d_)
        keep = jnp.where(core == 0, first, second)
        send = jnp.where(core == 0, second, first)
        return keep, core_swap(send)

    keep0, got0 = split(a0, b0, c0, d0)
    keep1, got1 = split(a1, b1, c1, d1)
    even = core == 0
    return jnp.stack(
        [
            jnp.where(even, keep0, got0),
            jnp.where(even, got0, keep0),
            jnp.where(even, keep1, got1),
            jnp.where(even, got1, keep1),
        ]
    )[None]


def solution(mesh):
    return jax.shard_map(
        body,
        mesh=mesh,
        in_specs=(
            P(("section", "seq"), None, None),
            P(),
            P(None, "mp"),
            P(None, "mp"),
            P(None, "mp"),
            P("mp", None),
            P(None, "seq", "mp"),
            P("section", None, "mp"),
            P("section", None, "mp"),
            P("section"),
            P(None, "seq", None),
            P(None, "seq", None),
            P(None, "seq", None),
        ),
        out_specs=P("section", None, "seq", "mp"),
        check_vma=False,
    )
```

time: 514 us -> 133 us (0.26)
  the two profiles are of different devices: /device:TPU:14 before, /device:TPU:7 now
where the time goes in v2:
time: 133 us; the launch traced here: 132 us
  Pallas kernels  48.4 us (36%)
  starting transfers between devices  47.6 us (36%)
  waiting for transfers between devices  29 us (22%)
  local copies, waits for them, and re-layouts  2.69 us (2%)
  other arithmetic  2.61 us (2%)
  between operations  2.07 us (2%)
    ppermute x18, starting transfers between devices, mp_shift(): return lax.ppermute(a, 'mp', [(i, (i + k) % mates) for i in range(mates)])  23.7 us
    pallas_call x2, Pallas kernels, project(): pl.pallas_call(functools.partial(project_kernel, len(chunks), moved), out...  19.9 us
    pallas_call x5, Pallas kernels, layer(): pl.pallas_call(functools.partial(layer_kernel, row, places, len(squares),...  13.7 us
    ppermute x18, waiting for transfers between devices, mp_shift(): return lax.ppermute(a, 'mp', [(i, (i + k) % mates) for i in range(mates)])  12.2 us
    ppermute x5, starting transfers between devices, core_swap(): return lax.ppermute(a, 'section', [(i, i ^ 1) for i in range(sections)])  11.2 us
    pallas_call x1, Pallas kernels, resample_sent(): pl.pallas_call(functools.partial(resample_sent_kernel, n), out_shape=[plt...  9.82 us
    ppermute x3, waiting for transfers between devices, cross(): return lax.ppermute(a, 'section', [(0, 2), (1, 3)])  9.5 us
    ppermute x1, waiting for transfers between devices, far_swap(): return lax.ppermute(a, 'section', [(i, i ^ 2) for i in range(sections)])  4.97 us
  transfers between devices with their start and end apart: 29, of which 12 were waited for; matrix products, arithmetic and copies ran while one was open for 3% of the time, Pallas kernels for 19%

profile of v2, /device:TPU:7, one launch (start us, length us, event | category | flops | bytes accessed | tf_op | source)
XLA Modules:
  0.0 132.4 jit_solution(685044832161145683)
XLA Ops:
  0.7 2.1 %copy.16.feat = bf16[4,257,1280]{2,1,0:T(8,128)(2,1)S(1)} copy(bf16[4,257,1280]{2,0,1:T(4,128)(2,1)} %param.13) | data formatting | bytes 5263360 | tf_op args[0]
  2.9 9.8 %resample.2 = (bf16[80,1280]{1,0:T(8,128)(2,1)S(1)}, bf16[80,1280]{1,0:T(8,128)(2,1)S(1)}, bf16[80,1280]{1,0:T(8,128)(2,1)S(1)}, f32[2,128]{1,0:T(2,128)S(1)}) custom-call(s32[4]{0:T(128)S(1)} %pad_add_fusion.ids, bf16[64,1280]{1,0:T(8,128)(2,1)S(1)} %copy-done, bf16[4,257,1280]{2,1,0:T(8,128)(2,1)S(1)} %copy.16.feat, bf16[4,128,2048]{2,1,0:T(8,128)(2,1)} %refs_8_.3, ...), custom_call_target="tpu_custom_call" | custom-call | tf_op jit(solution)/shard_map/resample/pallas_call | solution.py:179
  14.1 2.6 %collective-permute-start.1 = (bf16[80,1280]{1,0:T(8,128)(2,1)S(1)}, bf16[80,1280]{1,0:T(8,128)(2,1)S(1)}, u32[]{:S(2)}, u32[]{:S(2)}) collective-permute-start(bf16[80,1280]{1,0:T(8,128)(2,1)S(1)} %get-tuple-element.35), channel_id=1, source_target_pairs={{0,2},{1,3},{2,0},{3,1},{4,6},{5,7},{6,4},{7,5},{8,10},{9,11},{10,... | collective-permute-start | bytes 614408 | tf_op jit(solution)/shard_map/ppermute | solution.py:497
  17.8 4.8 %resample.3.own = f32[64,1280]{1,0:T(8,128)S(1)} custom-call(s32[1]{0:T(128)} %bitcast.6.ids, bf16[64,1280]{1,0:T(8,128)(2,1)S(1)} %copy-done, bf16[4,257,1280]{2,1,0:T(8,128)(2,1)S(1)} %copy.16.feat, bf16[1280,384]{1,0:T(8,128)(2,1)} %rest_0_.3, bf16[1280,384]{1,0:T(8,128)(2,1)} %rest_1_.3, bf16[1280,384]{1,0:T(8,128)(2,1)} %rest_2_.3, ...), custom_call_target="tpu_custom_call" | custom-call | tf_op jit(solution)/shard_map/resample/pallas_call | solution.py:224
  23.2 1.4 %collective-permute-start.14 = (f32[1,128]{1,0:T(1,128)S(1)}, f32[1,128]{1,0:T(1,128)S(1)}, u32[]{:S(2)}, u32[]{:S(2)}) collective-permute-start(f32[1,128]{1,0:T(1,128)S(1)} %broadcast_in_dim.16), channel_id=1, source_target_pairs={{0,32},{32,0},{64,96},{96,64},{1,33},{33,1},{65,97},{97,65},{2,34}... | collective-permute-start | bytes 1544 | tf_op jit(solution)/shard_map/ppermute | solution.py:500
  26.0 3.6 %collective-permute-start.3 = (bf16[64,1280]{1,0:T(8,128)(2,1)S(1)}, bf16[64,1280]{1,0:T(8,128)(2,1)S(1)}, u32[]{:S(2)}, u32[]{:S(2)}) collective-permute-start(bf16[64,1280]{1,0:T(8,128)(2,1)S(1)} %get-tuple-element.37), channel_id=1, source_target_pairs={{0,4},{4,8},{8,12},{12,16},{16,20},{20,24},{24,28},{1,5},{5,9},{9,... | collective-permute-start | bytes 491528 | tf_op jit(solution)/shard_map/ppermute | solution.py:524
  29.6 4.3 %collective-permute-start.4 = (bf16[64,1280]{1,0:T(8,128)(2,1)S(1)}, bf16[64,1280]{1,0:T(8,128)(2,1)S(1)}, u32[]{:S(2)}, u32[]{:S(2)}) collective-permute-start(bf16[64,1280]{1,0:T(8,128)(2,1)S(1)} %get-tuple-element.37), channel_id=1, source_target_pairs={{4,0},{8,4},{12,8},{16,12},{20,16},{24,20},{28,24},{5,1},{9,5},{13... | collective-permute-start | bytes 491528 | tf_op jit(solution)/shard_map/ppermute | solution.py:525
  37.5 3.7 %collective-permute-start.6 = (bf16[64,1280]{1,0:T(8,128)(2,1)S(1)}, bf16[64,1280]{1,0:T(8,128)(2,1)S(1)}, u32[]{:S(2)}, u32[]{:S(2)}) collective-permute-start(bf16[64,1280]{1,0:T(8,128)(2,1)S(1)} %select_select_fusion.refs_0_), channel_id=1, source_target_pairs={{0,2},{1,3},{2,0},{3,1},{4,6},{5,7},{6,4},{7,5},{8,10},{9,11},{10,... | collective-permute-start | bytes 491528 | tf_op jit(solution)/shard_map/ppermute | solution.py:497
  43.5 5.0 %collective-permute-done.8.refs_4_ = bf16[64,1280]{1,0:T(8,128)(2,1)S(1)} collective-permute-done((bf16[64,1280]{1,0:T(8,128)(2,1)S(1)}, bf16[64,1280]{1,0:T(8,128)(2,1)S(1)}, u32[]{:S(2)}, u32[]{:S(2)}) %collective-permute-start.8) | collective-permute-done | bytes 163872 | tf_op jit(solution)/shard_map/ppermute | solution.py:503
  48.5 2.5 %collective-permute-start.10 = (bf16[64,1280]{1,0:T(8,128)(2,1)S(1)}, bf16[64,1280]{1,0:T(8,128)(2,1)S(1)}, u32[]{:S(2)}, u32[]{:S(2)}) collective-permute-start(bf16[64,1280]{1,0:T(8,128)(2,1)S(1)} %collective-permute-done.8.refs_4_), channel_id=1, source_target_pairs={{0,2},{1,3},{2,0},{3,1},{4,6},{5,7},{6,4},{7,5},{8,10},{9,11},{10,... | collective-permute-start | bytes 491528 | tf_op jit(solution)/shard_map/ppermute | solution.py:497
  51.5 4.1 %collective-permute-done.9.refs_5_ = bf16[64,1280]{1,0:T(8,128)(2,1)S(1)} collective-permute-done((bf16[64,1280]{1,0:T(8,128)(2,1)S(1)}, bf16[64,1280]{1,0:T(8,128)(2,1)S(1)}, u32[]{:S(2)}, u32[]{:S(2)}) %collective-permute-start.9) | collective-permute-done | bytes 163872 | tf_op jit(solution)/shard_map/ppermute | solution.py:497
  56.2 10.2 %project.2 = (bf16[512,2048]{1,0:T(8,128)(2,1)S(1)}, bf16[512,2048]{1,0:T(8,128)(2,1)S(1)}, bf16[512,2048]{1,0:T(8,128)(2,1)}, bf16[512,2048]{1,0:T(8,128)(2,1)}...) custom-call(s32[3]{0:T(128)S(1)} %get-tuple-element.79.flags, ...), custom_call_target="tpu_custom_call" | custom-call | flops 5368709120 | tf_op jit(solution)/shard_map/project/pallas_call | solution.py:338
  66.4 2.2 %layer.5 = (bf16[128,2048]{1,0:T(8,128)(2,1)S(1)}, bf16[128,2048]{1,0:T(8,128)(2,1)S(1)}, f32[2,128]{1,0:T(2,128)S(1)}) custom-call(bf16[128,2048]{1,0:T(8,128)(2,1)S(1)} %get-tuple-element.38.refs_0_, bf16[128,2048]{1,0:T(8,128)(2,1)S(1)} %get-tuple-element.39.refs_1_, f32[8,128]{1,0:T(8,128)S(1)} %get-tuple-element.72.refs_2_.refs_1_.refs_3_, ...), custom_call_target="tpu_custom_call" | custom-call | flops 2147483648 | tf_op jit(solution)/shard_map/layer/pallas_call | solution.py:443
  69.0 3.2 %collective-permute-start.16 = (f32[2,128]{1,0:T(2,128)S(1)}, f32[2,128]{1,0:T(2,128)S(1)}, u32[]{:S(2)}, u32[]{:S(2)}) collective-permute-start(f32[2,128]{1,0:T(2,128)S(1)} %get-tuple-element.46.refs_4_), channel_id=1, source_target_pairs={{0,2},{1,3},{2,0},{3,1},{4,6},{5,7},{6,4},{7,5},{8,10},{9,11},{10,... | collective-permute-start | bytes 3080 | tf_op jit(solution)/shard_map/ppermute | solution.py:497
  72.2 9.6 %project.3 = (bf16[512,2048]{1,0:T(8,128)(2,1)S(1)}, bf16[512,2048]{1,0:T(8,128)(2,1)S(1)}, bf16[512,2048]{1,0:T(8,128)(2,1)}, bf16[512,2048]{1,0:T(8,128)(2,1)}) custom-call(s32[3]{0:T(128)S(1)} %get-tuple-element.80.flags, bf16[64,1280]{1,0:T(8,128)(2,1)S(1)} %select_select_fusion.refs_0_, bf16[64,1280]{1,0:T(8,128)(2,1)S(1)} %collective-permute-done.5.refs_1_, ...), custom_call_target="tpu_custom_call" | custom-call | flops 5368709120 | tf_op jit(solution)/shard_map/project/pallas_call | solution.py:338
  87.4 3.0 %collective-permute-start.21 = (f32[2,128]{1,0:T(2,128)S(1)}, f32[2,128]{1,0:T(2,128)S(1)}, u32[]{:S(2)}, u32[]{:S(2)}) collective-permute-start(f32[2,128]{1,0:T(2,128)S(1)} %get-tuple-element.53), channel_id=1, source_target_pairs={{0,2},{1,3},{2,0},{3,1},{4,6},{5,7},{6,4},{7,5},{8,10},{9,11},{10,... | collective-permute-start | bytes 3080 | tf_op jit(solution)/shard_map/ppermute | solution.py:497
  91.3 2.7 %collective-permute-done.20 = f32[2,128]{1,0:T(2,128)S(1)} collective-permute-done((f32[2,128]{1,0:T(2,128)S(1)}, f32[2,128]{1,0:T(2,128)S(1)}, u32[]{:S(2)}, u32[]{:S(2)}) %collective-permute-start.20) | collective-permute-done | bytes 1056 | tf_op jit(solution)/shard_map/ppermute | solution.py:497
  95.3 9.5 %collective-permute-done.23.refs_6_ = f32[2,128]{1,0:T(2,128)S(1)} collective-permute-done((f32[2,128]{1,0:T(2,128)S(1)}, f32[2,128]{1,0:T(2,128)S(1)}, u32[]{:S(2)}, u32[]{:S(2)}) %collective-permute-start.23) | collective-permute-done | bytes 1056 | tf_op jit(solution)/shard_map/ppermute | solution.py:506
  104.8 4.2 %layer.8 = (bf16[128,2048]{1,0:T(8,128)(2,1)S(1)}, bf16[128,2048]{1,0:T(8,128)(2,1)S(1)}, f32[2,128]{1,0:T(2,128)S(1)}) custom-call(bf16[128,2048]{1,0:T(8,128)(2,1)S(1)} %collective-permute-done.18.refs_0_, bf16[128,2048]{1,0:T(8,128)(2,1)S(1)} %collective-permute-done.19.refs_1_, f32[8,128]{1,0:T(8,128)S(1)} %get-tuple-element.71.refs_3_.refs_1_.refs_2_, ...), custom_call_target="tpu_custom_call" | custom-call | flops 2147483648 | tf_op jit(solution)/shard_map/layer/pallas_call | solution.py:443
  109.0 1.5 %collective-permute-start.24 = (f32[2,128]{1,0:T(2,128)S(1)}, f32[2,128]{1,0:T(2,128)S(1)}, u32[]{:S(2)}, u32[]{:S(2)}) collective-permute-start(f32[2,128]{1,0:T(2,128)S(1)} %get-tuple-element.58.refs_6_), channel_id=1, source_target_pairs={{0,1},{1,2},{2,3},{3,0},{4,5},{5,6},{6,7},{7,4},{8,9},{9,10},{10,1... | collective-permute-start | bytes 3080 | tf_op jit(solution)/shard_map/ppermute | solution.py:497
  110.5 2.5 %collective-permute-start.26 = (f32[2,128]{1,0:T(2,128)S(1)}, f32[2,128]{1,0:T(2,128)S(1)}, u32[]{:S(2)}, u32[]{:S(2)}) collective-permute-start(f32[2,128]{1,0:T(2,128)S(1)} %get-tuple-element.58.refs_6_), channel_id=1, source_target_pairs={{0,3},{1,0},{2,1},{3,2},{4,7},{5,4},{6,5},{7,6},{8,11},{9,8},{10,9... | collective-permute-start | bytes 3080 | tf_op jit(solution)/shard_map/ppermute | solution.py:497
  114.4 4.8 %layer.9 = (bf16[128,2048]{1,0:T(8,128)(2,1)S(1)}, bf16[128,2048]{1,0:T(8,128)(2,1)S(1)}, f32[2,128]{1,0:T(2,128)}) custom-call(bf16[128,2048]{1,0:T(8,128)(2,1)S(1)} %get-tuple-element.54.refs_0_, bf16[128,2048]{1,0:T(8,128)(2,1)S(1)} %get-tuple-element.55.refs_1_, f32[8,128]{1,0:T(8,128)S(1)} %get-tuple-element.71.refs_3_.refs_1_.refs_2_, ...), custom_call_target="tpu_custom_call" | custom-call | flops 2147483648 | tf_op jit(solution)/shard_map/layer/pallas_call | solution.py:443
  119.4 9.0 %collective-permute-start.28 = (bf16[128,2048]{1,0:T(8,128)(2,1)S(1)}, bf16[128,2048]{1,0:T(8,128)(2,1)S(1)}, u32[]{:S(2)}, u32[]{:S(2)}) collective-permute-start(bf16[128,2048]{1,0:T(8,128)(2,1)S(1)} %get-tuple-element.64), channel_id=1, source_target_pairs={{0,32},{32,0},{64,96},{96,64},{1,33},{33,1},{65,97},{97,65},{2,34}... | collective-permute-start | bytes 1572872 | tf_op jit(solution)/shard_map/ppermute | solution.py:500
  130.8 1.6 %maximum_bitcast_fusion = bf16[1,4,128,2048]{3,2,1,0:T(8,128)(2,1)} fusion(bf16[1,128,2048]{2,1,0:T(8,128)(2,1)S(1)} %get-tuple-element.70, bf16[1,128,2048]{2,1,0:T(8,128)(2,1)S(1)} %get-tuple-element.69, bf16[1,128,2048]{2,1,0:T(8,128)(2,1)S(1)} %get-tuple-element.68, bf16[1,128,2048]{2,1,0:T(8,128)(2,1)S(1)} %get-tuple-element.67), kind=kLoop, calls=%fused_computation | loop fusion | flops 3145728 | bytes 4194304 | tf_op jit(solution)/shard_map/broadcast_in_dim | solution.py:577
  (72 shorter events, 22.4 us)
Async XLA Ops:
  0.0 56.2 %collective-permute-start.12 = (bf16[1,1280,2048]{2,1,0:T(8,128)(2,1)}, bf16[1,1280,2048]{2,1,0:T(8,128)(2,1)}, u32[]{:S(2)}, u32[]{:S(2)}) collective-permute-start(bf16[1,1280,2048]{2,1,0:T(8,128)(2,1)} %refs_9_.3), channel_id=1, source_target_pairs={{0,32},{32,0},{64,96},{96,64},{1,33},{33,1},{65,97},{97,65},{2,34}... | collective-permute-start | bytes 15728648 | tf_op jit(solution)/shard_map/ppermute | solution.py:500
  0.7 55.6 %collective-permute-start.13 = (bf16[1,1280,2048]{2,1,0:T(8,128)(2,1)}, bf16[1,1280,2048]{2,1,0:T(8,128)(2,1)}, u32[]{:S(2)}, u32[]{:S(2)}) collective-permute-start(bf16[1,1280,2048]{2,1,0:T(8,128)(2,1)} %refs_10_.3), channel_id=1, source_target_pairs={{0,32},{32,0},{64,96},{96,64},{1,33},{33,1},{65,97},{97,65},{2,34}... | collective-permute-start | bytes 15728648 | tf_op jit(solution)/shard_map/ppermute | solution.py:500
  12.7 10.5 %collective-permute-start = (bf16[80,1280]{1,0:T(8,128)(2,1)S(1)}, bf16[80,1280]{1,0:T(8,128)(2,1)S(1)}, u32[]{:S(2)}, u32[]{:S(2)}) collective-permute-start(bf16[80,1280]{1,0:T(8,128)(2,1)S(1)} %get-tuple-element.34), channel_id=1, source_target_pairs={{0,1},{1,2},{2,3},{3,0},{4,5},{5,6},{6,7},{7,4},{8,9},{9,10},{10,1... | collective-permute-start | bytes 614408 | tf_op jit(solution)/shard_map/ppermute | solution.py:497
  14.1 11.7 %collective-permute-start.1 = (bf16[80,1280]{1,0:T(8,128)(2,1)S(1)}, bf16[80,1280]{1,0:T(8,128)(2,1)S(1)}, u32[]{:S(2)}, u32[]{:S(2)}) collective-permute-start(bf16[80,1280]{1,0:T(8,128)(2,1)S(1)} %get-tuple-element.35), channel_id=1, source_target_pairs={{0,2},{1,3},{2,0},{3,1},{4,6},{5,7},{6,4},{7,5},{8,10},{9,11},{10,... | collective-permute-start | bytes 614408 | tf_op jit(solution)/shard_map/ppermute | solution.py:497
  16.7 9.1 %collective-permute-start.2 = (bf16[80,1280]{1,0:T(8,128)(2,1)S(1)}, bf16[80,1280]{1,0:T(8,128)(2,1)S(1)}, u32[]{:S(2)}, u32[]{:S(2)}) collective-permute-start(bf16[80,1280]{1,0:T(8,128)(2,1)S(1)} %get-tuple-element.36), channel_id=1, source_target_pairs={{0,3},{1,0},{2,1},{3,2},{4,7},{5,4},{6,5},{7,6},{8,11},{9,8},{10,9... | collective-permute-start | bytes 614408 | tf_op jit(solution)/shard_map/ppermute | solution.py:497
  23.2 17.9 %collective-permute-start.14 = (f32[1,128]{1,0:T(1,128)S(1)}, f32[1,128]{1,0:T(1,128)S(1)}, u32[]{:S(2)}, u32[]{:S(2)}) collective-permute-start(f32[1,128]{1,0:T(1,128)S(1)} %broadcast_in_dim.16), channel_id=1, source_target_pairs={{0,32},{32,0},{64,96},{96,64},{1,33},{33,1},{65,97},{97,65},{2,34}... | collective-permute-start | bytes 1544 | tf_op jit(solution)/shard_map/ppermute | solution.py:500
  26.0 9.7 %collective-permute-start.3 = (bf16[64,1280]{1,0:T(8,128)(2,1)S(1)}, bf16[64,1280]{1,0:T(8,128)(2,1)S(1)}, u32[]{:S(2)}, u32[]{:S(2)}) collective-permute-start(bf16[64,1280]{1,0:T(8,128)(2,1)S(1)} %get-tuple-element.37), channel_id=1, source_target_pairs={{0,4},{4,8},{8,12},{12,16},{16,20},{20,24},{24,28},{1,5},{5,9},{9,... | collective-permute-start | bytes 491528 | tf_op jit(solution)/shard_map/ppermute | solution.py:524
  29.6 6.6 %collective-permute-start.4 = (bf16[64,1280]{1,0:T(8,128)(2,1)S(1)}, bf16[64,1280]{1,0:T(8,128)(2,1)S(1)}, u32[]{:S(2)}, u32[]{:S(2)}) collective-permute-start(bf16[64,1280]{1,0:T(8,128)(2,1)S(1)} %get-tuple-element.37), channel_id=1, source_target_pairs={{4,0},{8,4},{12,8},{16,12},{20,16},{24,20},{28,24},{5,1},{9,5},{13... | collective-permute-start | bytes 491528 | tf_op jit(solution)/shard_map/ppermute | solution.py:525
  36.2 6.3 %collective-permute-start.5 = (bf16[64,1280]{1,0:T(8,128)(2,1)S(1)}, bf16[64,1280]{1,0:T(8,128)(2,1)S(1)}, u32[]{:S(2)}, u32[]{:S(2)}) collective-permute-start(bf16[64,1280]{1,0:T(8,128)(2,1)S(1)} %select_select_fusion.refs_0_), channel_id=1, source_target_pairs={{0,1},{1,2},{2,3},{3,0},{4,5},{5,6},{6,7},{7,4},{8,9},{9,10},{10,1... | collective-permute-start | bytes 491528 | tf_op jit(solution)/shard_map/ppermute | solution.py:497
  37.5 11.0 %collective-permute-start.6 = (bf16[64,1280]{1,0:T(8,128)(2,1)S(1)}, bf16[64,1280]{1,0:T(8,128)(2,1)S(1)}, u32[]{:S(2)}, u32[]{:S(2)}) collective-permute-start(bf16[64,1280]{1,0:T(8,128)(2,1)S(1)} %select_select_fusion.refs_0_), channel_id=1, source_target_pairs={{0,2},{1,3},{2,0},{3,1},{4,6},{5,7},{6,4},{7,5},{8,10},{9,11},{10,... | collective-permute-start | bytes 491528 | tf_op jit(solution)/shard_map/ppermute | solution.py:497
  41.2 9.8 %collective-permute-start.7 = (bf16[64,1280]{1,0:T(8,128)(2,1)S(1)}, bf16[64,1280]{1,0:T(8,128)(2,1)S(1)}, u32[]{:S(2)}, u32[]{:S(2)}) collective-permute-start(bf16[64,1280]{1,0:T(8,128)(2,1)S(1)} %select_select_fusion.refs_0_), channel_id=1, source_target_pairs={{0,3},{1,0},{2,1},{3,2},{4,7},{5,4},{6,5},{7,6},{8,11},{9,8},{10,9... | collective-permute-start | bytes 491528 | tf_op jit(solution)/shard_map/ppermute | solution.py:497
  42.5 6.0 %collective-permute-start.8 = (bf16[64,1280]{1,0:T(8,128)(2,1)S(1)}, bf16[64,1280]{1,0:T(8,128)(2,1)S(1)}, u32[]{:S(2)}, u32[]{:S(2)}) collective-permute-start(bf16[64,1280]{1,0:T(8,128)(2,1)S(1)} %select_select_fusion.refs_0_), channel_id=1, source_target_pairs={{0,64},{32,96},{64,0},{96,32},{1,65},{33,97},{65,1},{97,33},{2,66}... | collective-permute-start | bytes 491528 | tf_op jit(solution)/shard_map/ppermute | solution.py:503
  48.5 7.1 %collective-permute-start.9 = (bf16[64,1280]{1,0:T(8,128)(2,1)S(1)}, bf16[64,1280]{1,0:T(8,128)(2,1)S(1)}, u32[]{:S(2)}, u32[]{:S(2)}) collective-permute-start(bf16[64,1280]{1,0:T(8,128)(2,1)S(1)} %collective-permute-done.8.refs_4_), channel_id=1, source_target_pairs={{0,1},{1,2},{2,3},{3,0},{4,5},{5,6},{6,7},{7,4},{8,9},{9,10},{10,1... | collective-permute-start | bytes 491528 | tf_op jit(solution)/shard_map/ppermute | solution.py:497
  48.5 7.1 %collective-permute-start.10 = (bf16[64,1280]{1,0:T(8,128)(2,1)S(1)}, bf16[64,1280]{1,0:T(8,128)(2,1)S(1)}, u32[]{:S(2)}, u32[]{:S(2)}) collective-permute-start(bf16[64,1280]{1,0:T(8,128)(2,1)S(1)} %collective-permute-done.8.refs_4_), channel_id=1, source_target_pairs={{0,2},{1,3},{2,0},{3,1},{4,6},{5,7},{6,4},{7,5},{8,10},{9,11},{10,... | collective-permute-start | bytes 491528 | tf_op jit(solution)/shard_map/ppermute | solution.py:497
  51.0 5.3 %collective-permute-start.11 = (bf16[64,1280]{1,0:T(8,128)(2,1)S(1)}, bf16[64,1280]{1,0:T(8,128)(2,1)S(1)}, u32[]{:S(2)}, u32[]{:S(2)}) collective-permute-start(bf16[64,1280]{1,0:T(8,128)(2,1)S(1)} %collective-permute-done.8.refs_4_), channel_id=1, source_target_pairs={{0,3},{1,0},{2,1},{3,2},{4,7},{5,4},{6,5},{7,6},{8,11},{9,8},{10,9... | collective-permute-start | bytes 491528 | tf_op jit(solution)/shard_map/ppermute | solution.py:497
  68.7 13.2 %collective-permute-start.15 = (f32[2,128]{1,0:T(2,128)S(1)}, f32[2,128]{1,0:T(2,128)S(1)}, u32[]{:S(2)}, u32[]{:S(2)}) collective-permute-start(f32[2,128]{1,0:T(2,128)S(1)} %get-tuple-element.46.refs_4_), channel_id=1, source_target_pairs={{0,1},{1,2},{2,3},{3,0},{4,5},{5,6},{6,7},{7,4},{8,9},{9,10},{10,1... | collective-permute-start | bytes 3080 | tf_op jit(solution)/shard_map/ppermute | solution.py:497
  69.0 12.9 %collective-permute-start.16 = (f32[2,128]{1,0:T(2,128)S(1)}, f32[2,128]{1,0:T(2,128)S(1)}, u32[]{:S(2)}, u32[]{:S(2)}) collective-permute-start(f32[2,128]{1,0:T(2,128)S(1)} %get-tuple-element.46.refs_4_), channel_id=1, source_target_pairs={{0,2},{1,3},{2,0},{3,1},{4,6},{5,7},{6,4},{7,5},{8,10},{9,11},{10,... | collective-permute-start | bytes 3080 | tf_op jit(solution)/shard_map/ppermute | solution.py:497
  72.2 9.7 %collective-permute-start.17 = (f32[2,128]{1,0:T(2,128)S(1)}, f32[2,128]{1,0:T(2,128)S(1)}, u32[]{:S(2)}, u32[]{:S(2)}) collective-permute-start(f32[2,128]{1,0:T(2,128)S(1)} %get-tuple-element.46.refs_4_), channel_id=1, source_target_pairs={{0,3},{1,0},{2,1},{3,2},{4,7},{5,4},{6,5},{7,6},{8,11},{9,8},{10,9... | collective-permute-start | bytes 3080 | tf_op jit(solution)/shard_map/ppermute | solution.py:497
  83.2 21.6 %collective-permute-start.18 = (bf16[128,2048]{1,0:T(8,128)(2,1)S(1)}, bf16[128,2048]{1,0:T(8,128)(2,1)S(1)}, u32[]{:S(2)}, u32[]{:S(2)}) collective-permute-start(bf16[128,2048]{1,0:T(8,128)(2,1)S(1)} %get-tuple-element.47), channel_id=1, source_target_pairs={{0,64},{32,96},{1,65},{33,97},{2,66},{34,98},{3,67},{35,99},{4,68}... | collective-permute-start | bytes 1572872 | tf_op jit(solution)/shard_map/ppermute | solution.py:506
  85.7 19.1 %collective-permute-start.19 = (bf16[128,2048]{1,0:T(8,128)(2,1)S(1)}, bf16[128,2048]{1,0:T(8,128)(2,1)S(1)}, u32[]{:S(2)}, u32[]{:S(2)}) collective-permute-start(bf16[128,2048]{1,0:T(8,128)(2,1)S(1)} %get-tuple-element.50), channel_id=1, source_target_pairs={{0,64},{32,96},{1,65},{33,97},{2,66},{34,98},{3,67},{35,99},{4,68}... | collective-permute-start | bytes 1572872 | tf_op jit(solution)/shard_map/ppermute | solution.py:506
  87.4 3.9 %collective-permute-start.21 = (f32[2,128]{1,0:T(2,128)S(1)}, f32[2,128]{1,0:T(2,128)S(1)}, u32[]{:S(2)}, u32[]{:S(2)}) collective-permute-start(f32[2,128]{1,0:T(2,128)S(1)} %get-tuple-element.53), channel_id=1, source_target_pairs={{0,2},{1,3},{2,0},{3,1},{4,6},{5,7},{6,4},{7,5},{8,10},{9,11},{10,... | collective-permute-start | bytes 3080 | tf_op jit(solution)/shard_map/ppermute | solution.py:497
  94.0 10.8 %collective-permute-start.23 = (f32[2,128]{1,0:T(2,128)S(1)}, f32[2,128]{1,0:T(2,128)S(1)}, u32[]{:S(2)}, u32[]{:S(2)}) collective-permute-start(f32[2,128]{1,0:T(2,128)S(1)} %add_add_fusion), channel_id=1, source_target_pairs={{0,64},{32,96},{1,65},{33,97},{2,66},{34,98},{3,67},{35,99},{4,68}... | collective-permute-start | bytes 3080 | tf_op jit(solution)/shard_map/ppermute | solution.py:506
  109.0 4.0 %collective-permute-start.24 = (f32[2,128]{1,0:T(2,128)S(1)}, f32[2,128]{1,0:T(2,128)S(1)}, u32[]{:S(2)}, u32[]{:S(2)}) collective-permute-start(f32[2,128]{1,0:T(2,128)S(1)} %get-tuple-element.58.refs_6_), channel_id=1, source_target_pairs={{0,1},{1,2},{2,3},{3,0},{4,5},{5,6},{6,7},{7,4},{8,9},{9,10},{10,1... | collective-permute-start | bytes 3080 | tf_op jit(solution)/shard_map/ppermute | solution.py:497
  119.4 10.5 %collective-permute-start.28 = (bf16[128,2048]{1,0:T(8,128)(2,1)S(1)}, bf16[128,2048]{1,0:T(8,128)(2,1)S(1)}, u32[]{:S(2)}, u32[]{:S(2)}) collective-permute-start(bf16[128,2048]{1,0:T(8,128)(2,1)S(1)} %get-tuple-element.64), channel_id=1, source_target_pairs={{0,32},{32,0},{64,96},{96,64},{1,33},{33,1},{65,97},{97,65},{2,34}... | collective-permute-start | bytes 1572872 | tf_op jit(solution)/shard_map/ppermute | solution.py:500
  (9 other events, 88.4 us)

commit v3 on v0

v3 whole, which is shorter than its diff:
```python
import functools

import jax
import jax.numpy as jnp
from jax import lax
from jax.experimental import pallas as pl
from jax.experimental.pallas import tpu as pltpu
from jax.sharding import PartitionSpec as P

D = 8192
HEAD = 128
LATENTS = 64
PHEAD = 96
EPS = 1e-05
NEG = -1e30
LOG2E = 1.4426950408889634
F32 = jnp.float32
BF16 = jnp.bfloat16
MIB = 1024 * 1024
FEW = 1000
SPARE = 16


def normalize(v):
    mean = jnp.mean(v, axis=-1, keepdims=True)
    cent = v - mean
    var = jnp.mean(cent * cent, axis=-1, keepdims=True)
    return cent * lax.rsqrt(var + EPS)


def dot(a, b):
    return jnp.dot(a, b, preferred_element_type=F32)


def dot_nt(a, b):
    return lax.dot_general(a, b, (((1,), (1,)), ((), ())), preferred_element_type=F32)


def up16(n):
    return -(-n // 16) * 16


def up128(n):
    return -(-n // 128) * 128


def near(a):
    return pltpu.with_memory_space_constraint(a, pltpu.VMEM)


def away(a):
    return pltpu.with_memory_space_constraint(a, pltpu.HBM)


IN_VMEM = pl.BlockSpec(memory_space=pltpu.VMEM)
IN_SMEM = pl.BlockSpec(memory_space=pltpu.SMEM)
IN_HBM = pl.BlockSpec(memory_space=pltpu.HBM)


def resample_updates(frames, lat, weights, held, ctx, tail, pk, pv, pqm, mixed, sems):
    n = len(frames)
    patches = frames[0].shape[0]
    keys = LATENTS + patches
    rows = up16(keys)
    qp, kp, vp, op = held
    inner = qp.shape[1]
    heads = inner // PHEAD
    cut = inner // 256 * 256
    side = inner - cut
    loads = [pltpu.make_async_copy(a, b, sems.at[i]) for i, (a, b) in enumerate(zip(weights, held))]
    for i in (1, 2, 0, 3):
        loads[i].start()

    base = normalize(lat[...].astype(F32)).astype(BF16)
    for i in range(n):
        top = i * rows
        ctx[top : top + LATENTS, :] = base
        ctx[top + rows - 16 : top + rows, :] = jnp.zeros((16, ctx.shape[1]), BF16)
        for r in range(0, patches, 64):
            end = min(r + 64, patches)
            block = normalize(frames[i][r:end, :].astype(F32)).astype(BF16)
            ctx[top + LATENTS + r : top + LATENTS + end, :] = block
    pv[:, inner:] = jnp.ones((pv.shape[0], 128), BF16)

    for i in (1, 2):
        loads[i].wait()
    tail[:, :side] = kp[:, cut:]
    tail[:, side:] = vp[:, cut:]
    pk[:, :cut] = dot(ctx[...], kp[:, :cut]).astype(BF16)
    pv[:, :cut] = dot(ctx[...], vp[:, :cut]).astype(BF16)
    both = dot(ctx[...], tail[...]).astype(BF16)
    pk[:, cut:] = both[:, :side]
    pv[:, cut:inner] = both[:, side:]
    loads[0].wait()
    pq = dot(base, qp[...]).astype(BF16).astype(F32)
    which = lax.broadcasted_iota(jnp.int32, (LATENTS, inner), 1) // PHEAD
    for h in range(heads):
        pqm[h * LATENTS : (h + 1) * LATENTS, :] = jnp.where(which == h, pq, 0.0).astype(BF16)

    for i in range(n):
        own = slice(i * rows, (i + 1) * rows)
        score = dot_nt(pqm[...], pk[own, :]) * (PHEAD ** (-0.5) * LOG2E)
        lane = lax.broadcasted_iota(jnp.int32, score.shape, 1)
        score = jnp.where(lane < keys, score, NEG)
        e = jnp.exp2(score - jnp.max(score, axis=1, keepdims=True)).astype(BF16)
        mix = dot(e, pv[own, :])
        inverse = 1.0 / mix[:, inner:]
        for j in range(inner // 128):
            at = lax.broadcasted_iota(jnp.int32, (LATENTS, 128), 1) + j * 128
            tile = jnp.zeros((LATENTS, 128), F32)
            for h in range(j * 128 // PHEAD, (j * 128 + 127) // PHEAD + 1):
                rows_h = slice(h * LATENTS, (h + 1) * LATENTS)
                value = mix[rows_h, j * 128 : (j + 1) * 128] * inverse[rows_h, :]
                tile = jnp.where(at // PHEAD == h, value, tile)
            mixed[i * LATENTS : (i + 1) * LATENTS, j * 128 : (j + 1) * 128] = tile.astype(BF16)
    loads[3].wait()
    return dot(mixed[...], op[...])


def resample_scratch(n, patches, vdim, inner, weights):
    rows = n * up16(LATENTS + patches)
    cut = inner // 256 * 256
    return [pltpu.VMEM(w.shape, BF16) for w in weights] + [
        pltpu.VMEM((rows, vdim), BF16),
        pltpu.VMEM((vdim, 2 * (inner - cut)), BF16),
        pltpu.VMEM((rows, inner), BF16),
        pltpu.VMEM((rows, inner + 128), BF16),
        pltpu.VMEM((inner // PHEAD * LATENTS, inner), BF16),
        pltpu.VMEM((n * LATENTS, inner), BF16),
        pltpu.SemaphoreType.DMA((4,)),
    ]


def resample_sent_kernel(n, ids, lat, feat, hid, *refs):
    weights, sent, squares, refs = refs[:4], refs[4 : 4 + n], refs[4 + n], refs[5 + n :]
    near_hid, hid_sems = refs[0:2], refs[2]
    loads = [
        pltpu.make_async_copy(hid.at[ids[n + i]], near_hid[i], hid_sems.at[i]) for i in range(2)
    ]
    frames = [feat.at[ids[i]] for i in range(n)]
    update = resample_updates(frames, lat, weights, refs[3:7], *refs[7:])
    for load in loads:
        load.start()
    for i in range(n):
        sent[i][0:LATENTS, :] = update[i * LATENTS : (i + 1) * LATENTS].astype(BF16)
    lines = []
    for load, a in zip(loads, near_hid):
        load.wait()
        acc = jnp.zeros((a.shape[0], 128), F32)
        for at in range(0, a.shape[1], 128):
            v = a[:, at : at + 128].astype(F32)
            acc = acc + v * v
        lines.append(jnp.sum(acc.T, axis=0, keepdims=True))
    squares[...] = jnp.concatenate(lines, axis=0)
    line = as_line(lines, sent[0].shape[1])
    for i in range(n):
        sent[i][LATENTS:, :] = line


def resample_sent(ids, features, latent_param, hidden, weights):
    n = ids.shape[0] - 2
    _, patches, vdim = features.shape
    _, rows, width = hidden.shape
    inner = weights[0].shape[1]
    return pl.pallas_call(
        functools.partial(resample_sent_kernel, n),
        out_shape=[pltpu.VMEM((LATENTS + SPARE, vdim), BF16)] * n
        + [pltpu.VMEM((2, rows), F32)],
        in_specs=[IN_SMEM, IN_VMEM, IN_VMEM] + [IN_HBM] * 5,
        out_specs=[IN_VMEM] * (n + 1),
        scratch_shapes=[pltpu.VMEM((rows, width), BF16)] * 2
        + [pltpu.SemaphoreType.DMA((2,))]
        + resample_scratch(n, patches, vdim, inner, weights),
        compiler_params=pltpu.CompilerParams(vmem_limit_bytes=24 * MIB),
        name="resample",
    )(ids, latent_param, near(features), away(hidden), *[away(w) for w in weights])


def resample_own_kernel(ids, lat, feat, *refs):
    refs[4][...] = resample_updates([feat.at[ids[0]]], lat, refs[:4], refs[5:9], *refs[9:])


def resample_own(ids, features, latent_param, weights):
    _, patches, vdim = features.shape
    inner = weights[0].shape[1]
    return pl.pallas_call(
        resample_own_kernel,
        out_shape=pltpu.VMEM((LATENTS, vdim), F32),
        in_specs=[IN_SMEM, IN_VMEM, IN_VMEM] + [IN_HBM] * 4,
        out_specs=IN_VMEM,
        scratch_shapes=resample_scratch(1, patches, vdim, inner, weights),
        compiler_params=pltpu.CompilerParams(vmem_limit_bytes=16 * MIB),
        name="resample",
    )(ids, latent_param, near(features), *[away(w) for w in weights])


def combine_kernel(lat, squares, own, a, b, c, out, total_squares):
    total = own[...]
    sums = squares[...]
    count = squares.shape[0]
    for part in (a, b, c):
        total = total + part[:LATENTS, :].astype(F32)
        line = part[LATENTS:, :].astype(F32)[0:1, :]
        at = lambda i: line[:, i * 128 : (i + 1) * 128]
        sums = sums + jnp.concatenate([at(i) + at(count + i) for i in range(count)], axis=0)
    out[...] = normalize(lat[...].astype(F32) + total).astype(BF16)
    total_squares[...] = sums


def combine(latent_param, squares, own, parts):
    return pl.pallas_call(
        combine_kernel,
        out_shape=[
            pltpu.VMEM(latent_param.shape, BF16),
            pltpu.VMEM(squares.shape, F32),
        ],
        in_specs=[IN_VMEM] * 6,
        out_specs=[IN_VMEM] * 2,
        compiler_params=pltpu.CompilerParams(vmem_limit_bytes=8 * MIB),
        name="combine",
    )(latent_param, squares, near(own), *[near(p) for p in parts])


TILE = 512
AHEAD = 3


def project_kernel(count, moved, flags, *refs):
    chunks, refs = refs[:count], refs[count:]
    hid, own_k, own_v, other_k, other_v = refs[:5]
    keys, vals, tiles = refs[5:8]
    near_hid = refs[8 : 8 + moved]
    chosen, sems, hid_sems = refs[8 + moved :]
    steps = 2 * (keys.shape[1] // TILE)

    def fetch(step, src):
        cols = pl.ds(pl.multiple_of(step // 2 * TILE, TILE), TILE)
        return pltpu.make_async_copy(src.at[0, :, cols], tiles.at[step], sems.at[step])

    def start(step, odd):
        of_own, of_other = (own_v, other_v) if odd else (own_k, other_k)

        @pl.when(flags[0] == 0)
        def _():
            fetch(step, of_own).start()

        @pl.when(flags[0] != 0)
        def _():
            fetch(step, of_other).start()

    @pl.when(flags[1] != 0)
    def _():
        for step in range(AHEAD):
            start(step, step % 2)
        loads = [
            pltpu.make_async_copy(hid.at[flags[2 + i]], near_hid[i], hid_sems.at[i])
            for i in range(moved)
        ]
        for load in loads:
            load.start()
        top = 0
        for a in chunks:
            chosen[top : top + a.shape[0], :] = a[...]
            top += a.shape[0]

        def column(j, carry):
            cols = pl.ds(pl.multiple_of(j * TILE, TILE), TILE)
            for i, out in enumerate((keys, vals)):
                step = 2 * j + i
                fetch(step, own_k).wait()

                @pl.when(step + AHEAD < steps)
                def _():
                    start(step + AHEAD, (i + AHEAD) % 2)

                out[:, cols] = dot(chosen[...], tiles[step]).astype(BF16)
            return carry

        lax.fori_loop(0, steps // 2, column, 0)
        for load in loads:
            load.wait()


def project(flags, chunks, own, other, hidden, moved=0, keep=False):
    vdim, width = own[0].shape[1:]
    rows = sum(a.shape[0] for a in chunks)
    steps = 2 * (width // TILE)
    held = pltpu.VMEM((steps, vdim, TILE), BF16)
    kernel = functools.partial(project_kernel, len(chunks), moved)
    if not keep:
        inner = kernel

        def kernel(*refs):
            at = 1 + len(chunks) + 7
            refs, tiles = refs[:-1], refs[-1]
            return inner(*refs[:at], tiles, *refs[at:])

    return pl.pallas_call(
        kernel,
        out_shape=[pltpu.VMEM((rows, width), BF16)] * 2
        + [held] * keep
        + [pltpu.VMEM(hidden.shape[1:], BF16)] * moved,
        in_specs=[IN_SMEM] + [IN_VMEM] * len(chunks) + [IN_HBM] * 5,
        out_specs=[IN_VMEM] * (2 + keep + moved),
        scratch_shapes=[
            pltpu.VMEM((rows, vdim), BF16),
            pltpu.SemaphoreType.DMA((steps,)),
            pltpu.SemaphoreType.DMA((2,)),
        ]
        + [held] * (not keep),
        compiler_params=pltpu.CompilerParams(vmem_limit_bytes=(8 if keep else 20) * MIB),
        cost_estimate=pl.CostEstimate(
            flops=FEW, bytes_accessed=0, transcendentals=0
        ),
        name="project",
    )(flags, *[near(a) for a in chunks], *[away(a) for a in (hidden, *own, *other)])


def project_both_kernel(flags, a, b, own_k, own_v, other_k, other_v, k1, v1, k2, v2, chosen, ring, sems):
    part = a.shape[0]
    half = 2 * (k1.shape[1] // TILE)
    depth = ring.shape[0]

    def fetch(step, src):
        cols = pl.ds(pl.multiple_of(step % half // 2 * TILE, TILE), TILE)
        return pltpu.make_async_copy(src.at[0, :, cols], ring.at[step % depth], sems.at[step % depth])

    def start(step, odd):
        of_own, of_other = (own_v, other_v) if odd else (own_k, other_k)
        from_own = (step // half) == flags[0]

        @pl.when(from_own)
        def _():
            fetch(step, of_own).start()

        @pl.when(jnp.logical_not(from_own))
        def _():
            fetch(step, of_other).start()

    @pl.when(flags[1] != 0)
    def _():
        for step in range(depth - 1):
            start(step, step % 2)
        chosen[0:part, :] = a[...]
        chosen[part:, :] = b[...]
        for which, outs in enumerate(((k1, v1), (k2, v2))):

            def column(j, carry, which=which, outs=outs):
                cols = pl.ds(pl.multiple_of(j * TILE, TILE), TILE)
                for i, out in enumerate(outs):
                    step = which * half + 2 * j + i
                    fetch(step, own_k).wait()

                    @pl.when(step + depth - 1 < 2 * half)
                    def _():
                        start(step + depth - 1, (i + depth - 1) % 2)

                    out[:, cols] = dot(chosen[...], ring[step % depth]).astype(BF16)
                return carry

            lax.fori_loop(0, half // 2, column, 0)


def project_both(flags, a, b, own, other):
    vdim, width = own[0].shape[1:]
    rows = a.shape[0] + b.shape[0]
    return pl.pallas_call(
        project_both_kernel,
        out_shape=[pltpu.VMEM((rows, width), BF16)] * 4,
        in_specs=[IN_SMEM, IN_VMEM, IN_VMEM] + [IN_HBM] * 4,
        out_specs=[IN_VMEM] * 4,
        scratch_shapes=[
            pltpu.VMEM((rows, vdim), BF16),
            pltpu.VMEM((AHEAD + 1, vdim, TILE), BF16),
            pltpu.SemaphoreType.DMA((AHEAD + 1,)),
        ],
        compiler_params=pltpu.CompilerParams(vmem_limit_bytes=16 * MIB),
        cost_estimate=pl.CostEstimate(flops=FEW, bytes_accessed=0, transcendentals=0),
        name="project",
    )(flags, near(a), near(b), *[away(w) for w in (*own, *other)])


def project_held_kernel(flags, a, tiles, *refs):
    keys, vals = refs[-2:]

    @pl.when(flags[1] != 0)
    def _():
        def column(j, carry):
            cols = pl.ds(pl.multiple_of(j * TILE, TILE), TILE)
            keys[:, cols] = dot(a[...], tiles[2 * j]).astype(BF16)
            vals[:, cols] = dot(a[...], tiles[2 * j + 1]).astype(BF16)
            return carry

        lax.fori_loop(0, keys.shape[1] // TILE, column, 0)


def project_held(flags, a, tiles, after=()):
    steps, vdim, _ = tiles.shape
    rows = a.shape[0]
    width = steps // 2 * TILE
    return pl.pallas_call(
        project_held_kernel,
        out_shape=[pltpu.VMEM((rows, width), BF16)] * 2,
        in_specs=[IN_SMEM] + [IN_VMEM] * (2 + len(after)),
        out_specs=[IN_VMEM] * 2,
        compiler_params=pltpu.CompilerParams(vmem_limit_bytes=8 * MIB),
        cost_estimate=pl.CostEstimate(
            flops=FEW, bytes_accessed=0, transcendentals=0
        ),
        name="project",
    )(flags, near(a), near(tiles), *[near(b) for b in after])


def gather_kernel(*refs):
    for i, a in enumerate(refs[:-1]):
        refs[-1][i * LATENTS : (i + 1) * LATENTS, :] = a[...]


def gather(chunks):
    vdim = chunks[0].shape[1]
    return pl.pallas_call(
        gather_kernel,
        out_shape=pltpu.VMEM((len(chunks) * LATENTS, vdim), BF16),
        in_specs=[IN_VMEM] * len(chunks),
        out_specs=IN_VMEM,
        compiler_params=pltpu.CompilerParams(vmem_limit_bytes=2 * MIB),
        name="gather",
    )(*[near(a) for a in chunks])


def as_line(lines, width):
    high = [line.astype(BF16).astype(F32) for line in lines]
    low = [line - h for line, h in zip(lines, high)]
    parts = high + low
    spare = jnp.zeros((1, width - len(parts) * parts[0].shape[1]), F32)
    line = jnp.concatenate(parts + [spare], axis=1)
    first = lax.broadcasted_iota(jnp.int32, (SPARE, width), 0) == 0
    return jnp.where(first, line, 0.0).astype(BF16)


def from_line_kernel(x, *refs):
    out = refs[-1]
    line = x[x.shape[0] - SPARE :, :].astype(F32)[0:1, :]
    at = lambda i: line[:, i * 128 : (i + 1) * 128]
    count = out.shape[0]
    out[...] = jnp.concatenate([at(i) + at(count + i) for i in range(count)], axis=0)


def from_line(x, after):
    return pl.pallas_call(
        from_line_kernel,
        out_shape=pltpu.VMEM((1, 128), F32),
        in_specs=[IN_VMEM] * (1 + len(after)),
        out_specs=IN_VMEM,
        compiler_params=pltpu.CompilerParams(vmem_limit_bytes=2 * MIB),
        name="from_line",
    )(near(x), *[near(a) for a in after])


def layer_kernel(row, places, count, ahead, riding, others, routed, carried, *refs):
    batches = len(places)
    flags, refs = (refs[0], refs[1:]) if others else (None, refs)
    xs, metas, refs = refs[:batches], refs[batches : 2 * batches], refs[2 * batches :]
    keys, vals, refs = refs[0], refs[1], refs[2:]
    squares, before, refs = refs[:count], refs[count : count + ahead], refs[count + ahead :]
    alts, refs = refs[:others], refs[others + carried :]
    outs, refs = refs[: batches * (1 + routed)], refs[batches * (1 + routed) :]
    square_out, refs = refs[0], refs[1 + carried :]
    scale_s, bias_s, high_s, half_s, gate_s, acc = refs
    rows = metas[0].shape[1]
    heads = xs[0].shape[1] // HEAD
    slots = 4 * LATENTS

    def write(i, cols, old, new):
        if routed:
            outs[2 * i][:, cols] = jnp.where(flags[1] == 0, old, new)
            outs[2 * i + 1][:, cols] = jnp.where(flags[1] == 0, new, old)
        else:
            outs[i][0:rows, cols] = new

    def run():
        total = squares[0][...]
        for part in squares[1:]:
            total = total + part[...]
        ones = jnp.ones((slots, HEAD), BF16)
        lines = [b[...] for b in before]
        for i, (at, line) in enumerate(places):
            scale = lax.rsqrt(total[line : line + 1, :] / D + EPS) * (HEAD ** (-0.5) * LOG2E)
            spare = jnp.zeros((rows - 3, rows), F32)
            gate = metas[i][row : row + 1, :]
            cols = jnp.concatenate([scale, metas[i][0:1, :], gate, spare], axis=0).T
            slot = jnp.broadcast_to(cols[:, 1:2], (rows, HEAD))
            scale_s[...] = jnp.broadcast_to(cols[:, 0:1], (rows, HEAD))
            gate_s[...] = jnp.broadcast_to(cols[:, 2:3], (rows, HEAD))
            upper = jnp.where(slot > 1.5, 1.0, 0.0)
            high_s[...] = upper
            half_s[...] = upper.astype(BF16)
            half = (lax.broadcasted_iota(jnp.int32, (rows, HEAD), 1) // LATENTS).astype(F32)
            bias_s[...] = jnp.where(slot - 2.0 * upper == half, 0.0, NEG)
            high = high_s[...] > 0.5
            sums = jnp.zeros((rows, HEAD), F32)
            for h in range(heads):
                cols = slice(h * HEAD, (h + 1) * HEAD)
                k = keys[at * slots : (at + 1) * slots, cols]
                v = vals[at * slots : (at + 1) * slots, cols]
                q = xs[i][0:rows, cols]
                score = dot_nt(q, k)
                t = jnp.where(high, score[:, HEAD:], score[:, :HEAD]) * scale_s[...] + bias_s[...]
                e = jnp.exp2(t - jnp.max(t, axis=1, keepdims=True)).astype(BF16)
                e_high = e * half_s[...]
                weight = jnp.concatenate([e - e_high, e_high], axis=1)
                mixed = dot(weight, jnp.concatenate([v, ones], axis=1))
                attn = mixed[:, :HEAD] / mixed[:, HEAD:]
                out = (q.astype(F32) + gate_s[...] * attn).astype(BF16)
                write(i, cols, q, out)
                of = out.astype(F32)
                sums = sums + of * of
            acc[...] = sums
            lines.append(jnp.sum(acc[...].T, axis=0, keepdims=True))
        square_out[...] = jnp.concatenate(lines, axis=0)
        if riding:
            outs[-1][rows:, :] = as_line(lines, outs[-1].shape[1])

    if not others:
        run()
        return
    pl.when(flags[0] != 0)(run)

    @pl.when(flags[0] == 0)
    def _():
        for i in range(batches):
            for h in range(heads):
                cols = slice(h * HEAD, (h + 1) * HEAD)
                write(i, cols, alts[i][0:rows, cols], alts[batches + i][0:rows, cols])
        square_out[...] = jnp.zeros_like(square_out)


def layer(
    row, xs, metas, kv, places, squares, before=(), riding=False, flags=None, alts=(), routed=False, carry=()
):
    keys, vals = kv
    rows = metas[0].shape[1]
    width = xs[0].shape[1]
    slots = 4 * LATENTS
    batches = len(xs)
    scratch = pltpu.VMEM((rows, HEAD), F32)
    ys = [pltpu.VMEM((rows, width), BF16)] * (batches * (1 + routed))
    if riding:
        ys[-1] = pltpu.VMEM((rows + SPARE, width), BF16)
    switch = [] if flags is None else [flags]
    first = len(switch) + 2 + 2 * batches + len(squares) + len(before) + len(alts)
    return pl.pallas_call(
        functools.partial(
            layer_kernel,
            row,
            places,
            len(squares),
            len(before),
            riding,
            len(alts),
            routed,
            len(carry),
        ),
        out_shape=ys
        + [pltpu.VMEM((batches + len(before), rows), F32)]
        + [pltpu.VMEM(a.shape, a.dtype) for a in carry],
        in_specs=[IN_SMEM] * len(switch) + [IN_VMEM] * (first - len(switch) + len(carry)),
        out_specs=[IN_VMEM] * (len(ys) + 1 + len(carry)),
        scratch_shapes=[scratch] * 3 + [pltpu.VMEM((rows, HEAD), BF16)] + [scratch] * 2,
        input_output_aliases={first + i: len(ys) + 1 + i for i in range(len(carry))},
        compiler_params=pltpu.CompilerParams(vmem_limit_bytes=8 * MIB),
        cost_estimate=pl.CostEstimate(
            flops=FEW, bytes_accessed=0, transcendentals=0,
        ),
        name="layer",
    )(
        *switch,
        *[near(x) for x in xs],
        *metas,
        near(keys),
        near(vals),
        *[near(a) for a in (*squares, *before, *alts, *carry)],
    )


def place_kernel(lead, core, *refs):
    a, b, out, sems = refs[lead:]
    copies = [
        pltpu.make_async_copy(a, out.at[core[0]], sems.at[0]),
        pltpu.make_async_copy(b, out.at[core[0] ^ 1], sems.at[1]),
    ]
    for copy in copies:
        copy.start()
    for copy in copies:
        copy.wait()


def place(at, a, b, onto=None):
    lead = 0 if onto is None else 1
    return pl.pallas_call(
        functools.partial(place_kernel, lead),
        out_shape=jax.ShapeDtypeStruct((4, *a.shape), a.dtype),
        in_specs=[IN_SMEM] + [IN_HBM] * lead + [IN_VMEM] * 2,
        out_specs=IN_HBM,
        scratch_shapes=[pltpu.SemaphoreType.DMA((2,))],
        input_output_aliases={1: 0} if lead else {},
        compiler_params=pltpu.CompilerParams(vmem_limit_bytes=2 * MIB),
        name="place",
    )(at[None].astype(jnp.int32), *([] if onto is None else [onto]), near(a), near(b))


def body(
    features,
    latent_param,
    query_proj,
    key_proj,
    value_proj,
    out_proj,
    hidden,
    key_weight,
    value_weight,
    gate_angle,
    group_images,
    token_slot,
    attend,
):
    s = lax.axis_index("section")
    c = lax.axis_index("seq")
    m = lax.axis_index("mp")
    core = s & 1
    far = s >> 1
    mates = lax.axis_size("mp")
    seqs = lax.axis_size("seq")
    sections = lax.axis_size("section")

    def mp_swap(a, k):
        return lax.ppermute(a, "mp", [(i, i ^ k) for i in range(mates)])

    def core_swap(a):
        return lax.ppermute(a, "section", [(i, i ^ 1) for i in range(sections)])

    def far_swap(a):
        return lax.ppermute(a, "section", [(i, i ^ 2) for i in range(sections)])

    def cross(a):
        return lax.ppermute(a, "section", [(0, 2), (1, 3)])

    def spread(a):
        return [a] + [mp_swap(a, k) for k in (1, 2, 3)]

    other_w = (core_swap(key_weight), core_swap(value_weight))
    gate_own = jnp.broadcast_to(jnp.tanh(gate_angle)[:, None], (1, 128))
    gate_other = core_swap(gate_own)
    gate_first = jnp.where(core == 0, gate_own, gate_other)
    gate_second = jnp.where(core == 0, gate_other, gate_own)

    order = jnp.stack([m ^ 2, m ^ 1, m ^ 3, core, core + 2]).astype(jnp.int32)
    weights = (query_proj, key_proj, value_proj, out_proj)
    p2, p1, p3, squares = resample_sent(order, features, latent_param, hidden, weights)
    r2, r1, r3 = mp_swap(p2, 2), mp_swap(p1, 1), mp_swap(p3, 3)
    p0 = resample_own(m[None].astype(jnp.int32), features, latent_param, weights)
    latents, entering = combine(latent_param, squares, p0, (r1, r2, r3))

    inner = [(i, i ^ 1) for i in range(seqs)]
    outer = [(i, ((i + 1) ^ 1) - 1) for i in range(1, seqs - 1)]
    in_pair = lax.ppermute(latents, "seq", inner)
    across = lax.ppermute(latents, "seq", outer)
    odd = (c & 1) == 1
    firsts = group_images[:, 0, 0]
    start = lax.dynamic_index_in_dim(firsts, s, 0, keepdims=False)
    where_is = ((start + ((m - start) & 3)) >> 2) - c
    picked = jnp.where(
        where_is == 0, latents, jnp.where((where_is < 0) == odd, in_pair, across)
    )
    own_set = gather(spread(picked))
    far_set = far_swap(own_set)

    block = m ^ ((firsts[:, None] + token_slot[:, 0, :]) & 3)
    alive = attend[:, 0, :].astype(F32)
    rows = jnp.stack(
        [block.astype(F32), alive * gate_first, alive * gate_second]
        + [jnp.zeros_like(alive)] * 5,
        axis=1,
    )
    meta_own = lax.dynamic_index_in_dim(rows, s, 0, keepdims=False)
    meta_far = lax.dynamic_index_in_dim(rows, s ^ 2, 0, keepdims=False)

    own_w = (key_weight, value_weight)
    is_near = 1 - far

    flags = jnp.stack([core, is_near, core, core + 2]).astype(jnp.int32)
    flags_second = jnp.stack([1 - core, is_near]).astype(jnp.int32)
    k, v, tiles, hidden0, hidden1 = project(
        flags, [own_set], own_w, other_w, hidden, moved=2, keep=True
    )
    a0, qa0 = layer(1, [hidden0], [meta_own], (k, v), ((0, 0),), [entering])
    *second, tiles_second = project(flags_second, [own_set], own_w, other_w, hidden, keep=True)
    b0, _ = layer(2, [a0], [meta_own], second, ((0, 0),), spread(qa0), riding=True)
    x0 = cross(b0)
    kv = project_held(flags, far_set, tiles, [b0])
    a1, qa1 = layer(1, [hidden1], [meta_far], kv, ((0, 1),), [entering])
    kv = project_held(flags_second, far_set, tiles_second)
    b1, _ = layer(2, [a1], [meta_far], kv, ((0, 0),), spread(qa1), riding=True)
    x1 = cross(b1)

    flags = jnp.stack([core, far]).astype(jnp.int32)
    kv = project_both(flags, own_set, far_set, own_w, other_w)
    first, second = kv[:2], kv[2:]
    flags = jnp.stack([far, core]).astype(jnp.int32)
    c0, qc0, *second = layer(
        1, [x0], [meta_far], first, ((1, 0),), spread(from_line(x0, (b1, *first, *second))), carry=second
    )
    keep0, send0, _, *second = layer(
        2,
        [c0],
        [meta_far],
        second,
        ((1, 0),),
        spread(qc0),
        flags=flags,
        alts=(a0, b0),
        routed=True,
        carry=second,
    )
    c1, qc1 = layer(1, [x1], [meta_own], first, ((0, 0),), spread(from_line(x1, ())))
    keep1, send1, _ = layer(
        2, [c1], [meta_own], second, ((0, 0),), spread(qc1), flags=flags, alts=(a1, b1), routed=True
    )

    got0, got1 = core_swap(send0), core_swap(send1)
    out = place(core, keep0, got0)
    return place(core + 2, keep1, got1, out)[None]


def solution(mesh):
    return jax.shard_map(
        body,
        mesh=mesh,
        in_specs=(
            P(("section", "seq"), None, None),
            P(),
            P(None, "mp"),
            P(None, "mp"),
            P(None, "mp"),
            P("mp", None),
            P(None, "seq", "mp"),
            P("section", None, "mp"),
            P("section", None, "mp"),
            P("section"),
            P(None, "seq", None),
            P(None, "seq", None),
            P(None, "seq", None),
        ),
        out_specs=P("section", None, "seq", "mp"),
        check_vma=False,
    )
```

time: 514 us -> 129 us (0.25)
  the two profiles are of different devices: /device:TPU:14 before, /device:TPU:7 now
where the time goes in v3:
time: 129 us; the launch traced here: 128 us
  starting transfers between devices  55.1 us (43%)
  Pallas kernels  48.6 us (38%)
  waiting for transfers between devices  18.4 us (14%)
  local copies, waits for them, and re-layouts  3.42 us (3%)
  between operations  2.57 us (2%)
    ppermute x24, starting transfers between devices, mp_swap(): return lax.ppermute(a, 'mp', [(i, i ^ k) for i in range(mates)])  31.5 us
    pallas_call x1, Pallas kernels, project_both(): pl.pallas_call(project_both_kernel, out_shape=[pltpu.VMEM((rows, width),...  15.6 us
    pallas_call x8, Pallas kernels, layer(): pl.pallas_call(functools.partial(layer_kernel, row, places, len(squares),...  13.8 us
    ppermute x5, starting transfers between devices, core_swap(): return lax.ppermute(a, 'section', [(i, i ^ 1) for i in range(sections)])  13.7 us
    ppermute x24, waiting for transfers between devices, mp_swap(): return lax.ppermute(a, 'mp', [(i, i ^ k) for i in range(mates)])  10.5 us
    pallas_call x1, Pallas kernels, resample_sent(): pl.pallas_call(functools.partial(resample_sent_kernel, n), out_shape=[plt...  9.45 us
    ppermute x1, starting transfers between devices, body(): across = lax.ppermute(latents, 'seq', outer)  4.4 us
    ppermute x2, waiting for transfers between devices, cross(): return lax.ppermute(a, 'section', [(0, 2), (1, 3)])  4.1 us
  transfers between devices with their start and end apart: 34, of which 8 were waited for; matrix products, arithmetic and copies ran while one was open for 3% of the time, Pallas kernels for 37%

profile of v3, /device:TPU:7, one launch (start us, length us, event | category | flops | bytes accessed | tf_op | source)
XLA Modules:
  0.0 128.4 jit_solution(4182001187049264788)
XLA Ops:
  0.7 2.1 %copy.21.feat = bf16[4,257,1280]{2,1,0:T(8,128)(2,1)S(1)} copy(bf16[4,257,1280]{2,0,1:T(4,128)(2,1)} %param.13) | data formatting | bytes 5263360 | tf_op args[0]
  2.9 9.4 %resample.2 = (bf16[80,1280]{1,0:T(8,128)(2,1)}, bf16[80,1280]{1,0:T(8,128)(2,1)}, bf16[80,1280]{1,0:T(8,128)(2,1)}, f32[2,128]{1,0:T(2,128)S(1)}) custom-call(s32[5]{0:T(128)S(1)} %stack.58.ids, bf16[64,1280]{1,0:T(8,128)(2,1)S(1)} %copy-done, bf16[4,257,1280]{2,1,0:T(8,128)(2,1)S(1)} %copy.21.feat, bf16[4,128,2048]{2,1,0:T(8,128)(2,1)} %refs_1_.7, ...), custom_call_target="tpu_custom_call" | custom-call | tf_op jit(solution)/shard_map/resample/pallas_call | solution.py:165
  13.7 2.6 %collective-permute-start.1 = (bf16[80,1280]{1,0:T(8,128)(2,1)}, bf16[80,1280]{1,0:T(8,128)(2,1)}, u32[]{:S(2)}, u32[]{:S(2)}) collective-permute-start(bf16[80,1280]{1,0:T(8,128)(2,1)} %get-tuple-element.47), channel_id=1, source_target_pairs={{0,2},{1,3},{2,0},{3,1},{4,6},{5,7},{6,4},{7,5},{8,10},{9,11},{10,... | collective-permute-start | bytes 614408 | tf_op jit(solution)/shard_map/ppermute | solution.py:637
  16.4 3.9 %resample.3.own = f32[64,1280]{1,0:T(8,128)S(1)} custom-call(s32[1]{0:T(128)} %bitcast.8.ids, bf16[64,1280]{1,0:T(8,128)(2,1)S(1)} %copy-done, bf16[4,257,1280]{2,1,0:T(8,128)(2,1)S(1)} %copy.21.feat, bf16[1280,384]{1,0:T(8,128)(2,1)} %refs_0_.3, bf16[1280,384]{1,0:T(8,128)(2,1)} %refs_1_.5, bf16[1280,384]{1,0:T(8,128)(2,1)} %refs_2_.5, ...), custom_call_target="tpu_custom_call" | custom-call | tf_op jit(solution)/shard_map/resample/pallas_call | solution.py:186
  20.3 5.5 %collective-permute-done.1.b = bf16[80,1280]{1,0:T(8,128)(2,1)} collective-permute-done((bf16[80,1280]{1,0:T(8,128)(2,1)}, bf16[80,1280]{1,0:T(8,128)(2,1)}, u32[]{:S(2)}, u32[]{:S(2)}) %collective-permute-start.1) | collective-permute-done | bytes 204832 | tf_op jit(solution)/shard_map/ppermute | solution.py:637
  25.8 2.4 %collective-permute-done.2.c = bf16[80,1280]{1,0:T(8,128)(2,1)} collective-permute-done((bf16[80,1280]{1,0:T(8,128)(2,1)}, bf16[80,1280]{1,0:T(8,128)(2,1)}, u32[]{:S(2)}, u32[]{:S(2)}) %collective-permute-start.2) | collective-permute-done | bytes 204832 | tf_op jit(solution)/shard_map/ppermute | solution.py:637
  31.2 4.4 %collective-permute-start.4 = (bf16[64,1280]{1,0:T(8,128)(2,1)S(1)}, bf16[64,1280]{1,0:T(8,128)(2,1)S(1)}, u32[]{:S(2)}, u32[]{:S(2)}) collective-permute-start(bf16[64,1280]{1,0:T(8,128)(2,1)S(1)} %get-tuple-element.49), channel_id=1, source_target_pairs={{4,8},{8,4},{12,16},{16,12},{20,24},{24,20},{5,9},{9,5},{13,17},{1... | collective-permute-start | bytes 491528 | tf_op jit(solution)/shard_map/ppermute | solution.py:667
  37.6 1.7 %collective-permute-done.4 = bf16[64,1280]{1,0:T(8,128)(2,1)S(1)} collective-permute-done((bf16[64,1280]{1,0:T(8,128)(2,1)S(1)}, bf16[64,1280]{1,0:T(8,128)(2,1)S(1)}, u32[]{:S(2)}, u32[]{:S(2)}) %collective-permute-start.4) | collective-permute-done | bytes 163872 | tf_op jit(solution)/shard_map/ppermute | solution.py:667
  40.7 2.6 %collective-permute-start.7 = (bf16[64,1280]{1,0:T(8,128)(2,1)S(1)}, bf16[64,1280]{1,0:T(8,128)(2,1)S(1)}, u32[]{:S(2)}, u32[]{:S(2)}) collective-permute-start(bf16[64,1280]{1,0:T(8,128)(2,1)S(1)} %select_select_fusion.refs_0_), channel_id=1, source_target_pairs={{0,3},{1,2},{2,1},{3,0},{4,7},{5,6},{6,5},{7,4},{8,11},{9,10},{10,... | collective-permute-start | bytes 491528 | tf_op jit(solution)/shard_map/ppermute | solution.py:637
  44.2 3.9 %collective-permute-start.10 = (f32[1,128]{1,0:T(1,128)S(1)}, f32[1,128]{1,0:T(1,128)S(1)}, u32[]{:S(2)}, u32[]{:S(2)}) collective-permute-start(f32[1,128]{1,0:T(1,128)S(1)} %broadcast_in_dim.24), channel_id=1, source_target_pairs={{0,32},{32,0},{64,96},{96,64},{1,33},{33,1},{65,97},{97,65},{2,34}... | collective-permute-start | bytes 1544 | tf_op jit(solution)/shard_map/ppermute | solution.py:640
  51.7 2.6 %collective-permute-start.12 = (f32[1,128]{1,0:T(1,128)S(1)}, f32[1,128]{1,0:T(1,128)S(1)}, u32[]{:S(2)}, u32[]{:S(2)}) collective-permute-start(f32[1,128]{1,0:T(1,128)S(1)} %get-tuple-element.57.refs_4_), channel_id=1, source_target_pairs={{0,2},{1,3},{2,0},{3,1},{4,6},{5,7},{6,4},{7,5},{8,10},{9,11},{10,... | collective-permute-start | bytes 1544 | tf_op jit(solution)/shard_map/ppermute | solution.py:637
  56.3 1.9 %collective-permute-done.13.refs_7_ = f32[1,128]{1,0:T(1,128)S(1)} collective-permute-done((f32[1,128]{1,0:T(1,128)S(1)}, f32[1,128]{1,0:T(1,128)S(1)}, u32[]{:S(2)}, u32[]{:S(2)}) %collective-permute-start.13) | collective-permute-done | bytes 544 | tf_op jit(solution)/shard_map/ppermute | solution.py:637
  58.2 1.9 %layer.9 = (bf16[144,2048]{1,0:T(8,128)(2,1)S(1)}, f32[1,128]{1,0:T(1,128)}) custom-call(bf16[128,2048]{1,0:T(8,128)(2,1)S(1)} %get-tuple-element.54.refs_0_.refs_9_, f32[8,128]{1,0:T(8,128)S(1)} %get-tuple-element.86.refs_1_.refs_2_, bf16[256,2048]{1,0:T(8,128)(2,1)S(1)} %get-tuple-element.55.refs_2_, bf16[256,2048]{1,0:T(8,128)(2,1)S(1)} %get-tuple-element.56.refs_3_, ...), custom_call_target="tpu_custom_call" | custom-call | flops 1000 | tf_op jit(solution)/shard_map/layer/pallas_call | solution.py:552
  66.3 2.4 %collective-permute-start.18 = (f32[1,128]{1,0:T(1,128)S(1)}, f32[1,128]{1,0:T(1,128)S(1)}, u32[]{:S(2)}, u32[]{:S(2)}) collective-permute-start(f32[1,128]{1,0:T(1,128)S(1)} %get-tuple-element.69.refs_4_), channel_id=1, source_target_pairs={{0,3},{1,2},{2,1},{3,0},{4,7},{5,6},{6,5},{7,4},{8,11},{9,10},{10,... | collective-permute-start | bytes 1544 | tf_op jit(solution)/shard_map/ppermute | solution.py:637
  69.9 1.9 %layer.11 = (bf16[144,2048]{1,0:T(8,128)(2,1)S(1)}, f32[1,128]{1,0:T(1,128)}) custom-call(bf16[128,2048]{1,0:T(8,128)(2,1)S(1)} %get-tuple-element.65.refs_0_.refs_9_, f32[8,128]{1,0:T(8,128)S(1)} %get-tuple-element.85.refs_1_.refs_2_, bf16[256,2048]{1,0:T(8,128)(2,1)S(1)} %get-tuple-element.67.refs_2_, bf16[256,2048]{1,0:T(8,128)(2,1)S(1)} %get-tuple-element.68.refs_3_, ...), custom_call_target="tpu_custom_call" | custom-call | flops 1000 | tf_op jit(solution)/shard_map/layer/pallas_call | solution.py:552
  73.0 15.6 %project.7 = (bf16[512,2048]{1,0:T(8,128)(2,1)S(1)}, bf16[512,2048]{1,0:T(8,128)(2,1)S(1)}, bf16[512,2048]{1,0:T(8,128)(2,1)S(1)}, bf16[512,2048]{1,0:T(8,128)(2,1)S(1)}) custom-call(s32[2]{0:T(128)S(1)} %get-tuple-element.94.flags, bf16[256,1280]{1,0:T(8,128)(2,1)S(1)} %gather.1.refs_0_.a, bf16[256,1280]{1,0:T(8,128)(2,1)S(1)} %collective-permute-done.15.b.a, ...), custom_call_target="tpu_custom_call" | custom-call | flops 1000 | tf_op jit(solution)/shard_map/project/pallas_call | solution.py:367
  89.0 3.3 %collective-permute-start.20 = (f32[1,128]{1,0:T(1,128)S(1)}, f32[1,128]{1,0:T(1,128)S(1)}, u32[]{:S(2)}, u32[]{:S(2)}) collective-permute-start(f32[1,128]{1,0:T(1,128)S(1)} %from_line.2.refs_4_), channel_id=1, source_target_pairs={{0,2},{1,3},{2,0},{3,1},{4,6},{5,7},{6,4},{7,5},{8,10},{9,11},{10,... | collective-permute-start | bytes 1544 | tf_op jit(solution)/shard_map/ppermute | solution.py:637
  92.7 4.1 %collective-permute-done.26.x.refs_0_ = bf16[144,2048]{1,0:T(8,128)(2,1)S(1)} collective-permute-done((bf16[144,2048]{1,0:T(8,128)(2,1)S(1)}, bf16[144,2048]{1,0:T(8,128)(2,1)S(1)}, u32[]{:S(2)}, u32[]{:S(2)}) %collective-permute-start.26) | collective-permute-done | bytes 589856 | tf_op jit(solution)/shard_map/ppermute | solution.py:646
  98.4 2.2 %collective-permute-start.29 = (f32[1,128]{1,0:T(1,128)S(1)}, f32[1,128]{1,0:T(1,128)S(1)}, u32[]{:S(2)}, u32[]{:S(2)}) collective-permute-start(f32[1,128]{1,0:T(1,128)S(1)} %from_line.3.refs_4_), channel_id=1, source_target_pairs={{0,3},{1,2},{2,1},{3,0},{4,7},{5,6},{6,5},{7,4},{8,11},{9,10},{10,... | collective-permute-start | bytes 1544 | tf_op jit(solution)/shard_map/ppermute | solution.py:637
  103.9 2.3 %collective-permute-start.24 = (f32[1,128]{1,0:T(1,128)S(1)}, f32[1,128]{1,0:T(1,128)S(1)}, u32[]{:S(2)}, u32[]{:S(2)}) collective-permute-start(f32[1,128]{1,0:T(1,128)S(1)} %get-tuple-element.76.refs_5_), channel_id=1, source_target_pairs={{0,3},{1,2},{2,1},{3,0},{4,7},{5,6},{6,5},{7,4},{8,11},{9,10},{10,... | collective-permute-start | bytes 1544 | tf_op jit(solution)/shard_map/ppermute | solution.py:637
  109.2 2.2 %collective-permute-start.32 = (f32[1,128]{1,0:T(1,128)S(1)}, f32[1,128]{1,0:T(1,128)S(1)}, u32[]{:S(2)}, u32[]{:S(2)}) collective-permute-start(f32[1,128]{1,0:T(1,128)S(1)} %get-tuple-element.82.refs_5_), channel_id=1, source_target_pairs={{0,3},{1,2},{2,1},{3,0},{4,7},{5,6},{6,5},{7,4},{8,11},{9,10},{10,... | collective-permute-start | bytes 1544 | tf_op jit(solution)/shard_map/ppermute | solution.py:637
  111.7 2.5 %layer.13 = (bf16[128,2048]{1,0:T(8,128)(2,1)S(1)}, bf16[128,2048]{1,0:T(8,128)(2,1)S(1)}, f32[1,128]{1,0:T(1,128)}, bf16[512,2048]{1,0:T(8,128)(2,1)S(1)}, bf16[512,2048]{1,0:T(8,128)(2,1)S(1)}) custom-call(s32[2]{0:T(128)S(1)} %pad_add_fusion.refs_0_, ...), custom_call_target="tpu_custom_call", output_to_operand_aliasing={{3}: (11, {}), {4}: (12, {})} | custom-call | flops 1000 | tf_op jit(solution)/shard_map/layer/pallas_call | solution.py:552
  114.2 8.6 %collective-permute-start.25 = (bf16[128,2048]{1,0:T(8,128)(2,1)S(1)}, bf16[128,2048]{1,0:T(8,128)(2,1)S(1)}, u32[]{:S(2)}, u32[]{:S(2)}) collective-permute-start(bf16[128,2048]{1,0:T(8,128)(2,1)S(1)} %get-tuple-element.78), channel_id=1, source_target_pairs={{0,32},{32,0},{64,96},{96,64},{1,33},{33,1},{65,97},{97,65},{2,34}... | collective-permute-start | bytes 1572872 | tf_op jit(solution)/shard_map/ppermute | solution.py:640
  122.8 2.5 %layer.15 = (bf16[128,2048]{1,0:T(8,128)(2,1)S(1)}, bf16[128,2048]{1,0:T(8,128)(2,1)S(1)}, f32[1,128]{1,0:T(1,128)}) custom-call(s32[2]{0:T(128)S(1)} %pad_add_fusion.refs_0_, bf16[128,2048]{1,0:T(8,128)(2,1)S(1)} %get-tuple-element.79.refs_1_, f32[8,128]{1,0:T(8,128)S(1)} %get-tuple-element.86.refs_1_.refs_2_, ...), custom_call_target="tpu_custom_call" | custom-call | flops 1000 | tf_op jit(solution)/shard_map/layer/pallas_call | solution.py:552
  (91 shorter events, 33.5 us)
Async XLA Ops:
  0.0 49.4 %collective-permute-start.8 = (bf16[1,1280,2048]{2,1,0:T(8,128)(2,1)}, bf16[1,1280,2048]{2,1,0:T(8,128)(2,1)}, u32[]{:S(2)}, u32[]{:S(2)}) collective-permute-start(bf16[1,1280,2048]{2,1,0:T(8,128)(2,1)} %own_k.1), channel_id=1, source_target_pairs={{0,32},{32,0},{64,96},{96,64},{1,33},{33,1},{65,97},{97,65},{2,34}... | collective-permute-start | bytes 15728648 | tf_op jit(solution)/shard_map/ppermute | solution.py:640
  0.7 48.8 %collective-permute-start.9 = (bf16[1,1280,2048]{2,1,0:T(8,128)(2,1)}, bf16[1,1280,2048]{2,1,0:T(8,128)(2,1)}, u32[]{:S(2)}, u32[]{:S(2)}) collective-permute-start(bf16[1,1280,2048]{2,1,0:T(8,128)(2,1)} %own_v.1), channel_id=1, source_target_pairs={{0,32},{32,0},{64,96},{96,64},{1,33},{33,1},{65,97},{97,65},{2,34}... | collective-permute-start | bytes 15728648 | tf_op jit(solution)/shard_map/ppermute | solution.py:640
  12.3 7.9 %collective-permute-start = (bf16[80,1280]{1,0:T(8,128)(2,1)}, bf16[80,1280]{1,0:T(8,128)(2,1)S(1)}, u32[]{:S(2)}, u32[]{:S(2)}) collective-permute-start(bf16[80,1280]{1,0:T(8,128)(2,1)} %get-tuple-element.46), channel_id=1, source_target_pairs={{0,1},{1,0},{2,3},{3,2},{4,5},{5,4},{6,7},{7,6},{8,9},{9,8},{10,11... | collective-permute-start | bytes 614408 | tf_op jit(solution)/shard_map/ppermute | solution.py:637
  13.7 12.0 %collective-permute-start.1 = (bf16[80,1280]{1,0:T(8,128)(2,1)}, bf16[80,1280]{1,0:T(8,128)(2,1)}, u32[]{:S(2)}, u32[]{:S(2)}) collective-permute-start(bf16[80,1280]{1,0:T(8,128)(2,1)} %get-tuple-element.47), channel_id=1, source_target_pairs={{0,2},{1,3},{2,0},{3,1},{4,6},{5,7},{6,4},{7,5},{8,10},{9,11},{10,... | collective-permute-start | bytes 614408 | tf_op jit(solution)/shard_map/ppermute | solution.py:637
  16.3 11.8 %collective-permute-start.2 = (bf16[80,1280]{1,0:T(8,128)(2,1)}, bf16[80,1280]{1,0:T(8,128)(2,1)}, u32[]{:S(2)}, u32[]{:S(2)}) collective-permute-start(bf16[80,1280]{1,0:T(8,128)(2,1)} %get-tuple-element.48), channel_id=1, source_target_pairs={{0,3},{1,2},{2,1},{3,0},{4,7},{5,6},{6,5},{7,4},{8,11},{9,10},{10,... | collective-permute-start | bytes 614408 | tf_op jit(solution)/shard_map/ppermute | solution.py:637
  29.5 8.1 %collective-permute-start.3 = (bf16[64,1280]{1,0:T(8,128)(2,1)S(1)}, bf16[64,1280]{1,0:T(8,128)(2,1)S(1)}, u32[]{:S(2)}, u32[]{:S(2)}) collective-permute-start(bf16[64,1280]{1,0:T(8,128)(2,1)S(1)} %get-tuple-element.49), channel_id=1, source_target_pairs={{0,4},{4,0},{8,12},{12,8},{16,20},{20,16},{24,28},{28,24},{1,5},{5... | collective-permute-start | bytes 491528 | tf_op jit(solution)/shard_map/ppermute | solution.py:666
  31.2 8.2 %collective-permute-start.4 = (bf16[64,1280]{1,0:T(8,128)(2,1)S(1)}, bf16[64,1280]{1,0:T(8,128)(2,1)S(1)}, u32[]{:S(2)}, u32[]{:S(2)}) collective-permute-start(bf16[64,1280]{1,0:T(8,128)(2,1)S(1)} %get-tuple-element.49), channel_id=1, source_target_pairs={{4,8},{8,4},{12,16},{16,12},{20,24},{24,20},{5,9},{9,5},{13,17},{1... | collective-permute-start | bytes 491528 | tf_op jit(solution)/shard_map/ppermute | solution.py:667
  39.5 8.6 %collective-permute-start.6 = (bf16[64,1280]{1,0:T(8,128)(2,1)S(1)}, bf16[64,1280]{1,0:T(8,128)(2,1)S(1)}, u32[]{:S(2)}, u32[]{:S(2)}) collective-permute-start(bf16[64,1280]{1,0:T(8,128)(2,1)S(1)} %select_select_fusion.refs_0_), channel_id=1, source_target_pairs={{0,2},{1,3},{2,0},{3,1},{4,6},{5,7},{6,4},{7,5},{8,10},{9,11},{10,... | collective-permute-start | bytes 491528 | tf_op jit(solution)/shard_map/ppermute | solution.py:637
  40.7 7.4 %collective-permute-start.7 = (bf16[64,1280]{1,0:T(8,128)(2,1)S(1)}, bf16[64,1280]{1,0:T(8,128)(2,1)S(1)}, u32[]{:S(2)}, u32[]{:S(2)}) collective-permute-start(bf16[64,1280]{1,0:T(8,128)(2,1)S(1)} %select_select_fusion.refs_0_), channel_id=1, source_target_pairs={{0,3},{1,2},{2,1},{3,0},{4,7},{5,6},{6,5},{7,4},{8,11},{9,10},{10,... | collective-permute-start | bytes 491528 | tf_op jit(solution)/shard_map/ppermute | solution.py:637
  48.1 14.7 %collective-permute-start.15 = (bf16[256,1280]{1,0:T(8,128)(2,1)S(1)}, bf16[256,1280]{1,0:T(8,128)(2,1)S(1)}, u32[]{:S(2)}, u32[]{:S(2)}) collective-permute-start(bf16[256,1280]{1,0:T(8,128)(2,1)S(1)} %gather.1.refs_0_.a), channel_id=1, source_target_pairs={{0,64},{32,96},{64,0},{96,32},{1,65},{33,97},{65,1},{97,33},{2,66}... | collective-permute-start | bytes 1966088 | tf_op jit(solution)/shard_map/ppermute | solution.py:643
  60.0 28.6 %collective-permute-start.14 = (bf16[144,2048]{1,0:T(8,128)(2,1)S(1)}, bf16[144,2048]{1,0:T(8,128)(2,1)S(1)}, u32[]{:S(2)}, u32[]{:S(2)}) collective-permute-start(bf16[144,2048]{1,0:T(8,128)(2,1)S(1)} %get-tuple-element.58.refs_0_.refs_10_), channel_id=1, source_target_pairs={{0,64},{32,96},{1,65},{33,97},{2,66},{34,98},{3,67},{35,99},{4,68}... | collective-permute-start | bytes 1769480 | tf_op jit(solution)/shard_map/ppermute | solution.py:646
  71.7 25.0 %collective-permute-start.26 = (bf16[144,2048]{1,0:T(8,128)(2,1)S(1)}, bf16[144,2048]{1,0:T(8,128)(2,1)S(1)}, u32[]{:S(2)}, u32[]{:S(2)}) collective-permute-start(bf16[144,2048]{1,0:T(8,128)(2,1)S(1)} %get-tuple-element.70.refs_0_.refs_10_), channel_id=1, source_target_pairs={{0,64},{32,96},{1,65},{33,97},{2,66},{34,98},{3,67},{35,99},{4,68}... | collective-permute-start | bytes 1769480 | tf_op jit(solution)/shard_map/ppermute | solution.py:646
  88.6 9.8 %collective-permute-start.19 = (f32[1,128]{1,0:T(1,128)S(1)}, f32[1,128]{1,0:T(1,128)S(1)}, u32[]{:S(2)}, u32[]{:S(2)}) collective-permute-start(f32[1,128]{1,0:T(1,128)S(1)} %from_line.2.refs_4_), channel_id=1, source_target_pairs={{0,1},{1,0},{2,3},{3,2},{4,5},{5,4},{6,7},{7,6},{8,9},{9,8},{10,11... | collective-permute-start | bytes 1544 | tf_op jit(solution)/shard_map/ppermute | solution.py:637
  89.0 11.6 %collective-permute-start.20 = (f32[1,128]{1,0:T(1,128)S(1)}, f32[1,128]{1,0:T(1,128)S(1)}, u32[]{:S(2)}, u32[]{:S(2)}) collective-permute-start(f32[1,128]{1,0:T(1,128)S(1)} %from_line.2.refs_4_), channel_id=1, source_target_pairs={{0,2},{1,3},{2,0},{3,1},{4,6},{5,7},{6,4},{7,5},{8,10},{9,11},{10,... | collective-permute-start | bytes 1544 | tf_op jit(solution)/shard_map/ppermute | solution.py:637
  92.3 8.4 %collective-permute-start.21 = (f32[1,128]{1,0:T(1,128)S(1)}, f32[1,128]{1,0:T(1,128)S(1)}, u32[]{:S(2)}, u32[]{:S(2)}) collective-permute-start(f32[1,128]{1,0:T(1,128)S(1)} %from_line.2.refs_4_), channel_id=1, source_target_pairs={{0,3},{1,2},{2,1},{3,0},{4,7},{5,6},{6,5},{7,4},{8,11},{9,10},{10,... | collective-permute-start | bytes 1544 | tf_op jit(solution)/shard_map/ppermute | solution.py:637
  96.8 9.4 %collective-permute-start.28 = (f32[1,128]{1,0:T(1,128)S(1)}, f32[1,128]{1,0:T(1,128)S(1)}, u32[]{:S(2)}, u32[]{:S(2)}) collective-permute-start(f32[1,128]{1,0:T(1,128)S(1)} %from_line.3.refs_4_), channel_id=1, source_target_pairs={{0,2},{1,3},{2,0},{3,1},{4,6},{5,7},{6,4},{7,5},{8,10},{9,11},{10,... | collective-permute-start | bytes 1544 | tf_op jit(solution)/shard_map/ppermute | solution.py:637
  98.4 7.8 %collective-permute-start.29 = (f32[1,128]{1,0:T(1,128)S(1)}, f32[1,128]{1,0:T(1,128)S(1)}, u32[]{:S(2)}, u32[]{:S(2)}) collective-permute-start(f32[1,128]{1,0:T(1,128)S(1)} %from_line.3.refs_4_), channel_id=1, source_target_pairs={{0,3},{1,2},{2,1},{3,0},{4,7},{5,6},{6,5},{7,4},{8,11},{9,10},{10,... | collective-permute-start | bytes 1544 | tf_op jit(solution)/shard_map/ppermute | solution.py:637
  101.9 7.3 %collective-permute-start.22 = (f32[1,128]{1,0:T(1,128)S(1)}, f32[1,128]{1,0:T(1,128)S(1)}, u32[]{:S(2)}, u32[]{:S(2)}) collective-permute-start(f32[1,128]{1,0:T(1,128)S(1)} %get-tuple-element.76.refs_5_), channel_id=1, source_target_pairs={{0,1},{1,0},{2,3},{3,2},{4,5},{5,4},{6,7},{7,6},{8,9},{9,8},{10,11... | collective-permute-start | bytes 1544 | tf_op jit(solution)/shard_map/ppermute | solution.py:637
  102.0 9.6 %collective-permute-start.23 = (f32[1,128]{1,0:T(1,128)S(1)}, f32[1,128]{1,0:T(1,128)S(1)}, u32[]{:S(2)}, u32[]{:S(2)}) collective-permute-start(f32[1,128]{1,0:T(1,128)S(1)} %get-tuple-element.76.refs_5_), channel_id=1, source_target_pairs={{0,2},{1,3},{2,0},{3,1},{4,6},{5,7},{6,4},{7,5},{8,10},{9,11},{10,... | collective-permute-start | bytes 1544 | tf_op jit(solution)/shard_map/ppermute | solution.py:637
  103.9 7.7 %collective-permute-start.24 = (f32[1,128]{1,0:T(1,128)S(1)}, f32[1,128]{1,0:T(1,128)S(1)}, u32[]{:S(2)}, u32[]{:S(2)}) collective-permute-start(f32[1,128]{1,0:T(1,128)S(1)} %get-tuple-element.76.refs_5_), channel_id=1, source_target_pairs={{0,3},{1,2},{2,1},{3,0},{4,7},{5,6},{6,5},{7,4},{8,11},{9,10},{10,... | collective-permute-start | bytes 1544 | tf_op jit(solution)/shard_map/ppermute | solution.py:637
  107.5 15.3 %collective-permute-start.30 = (f32[1,128]{1,0:T(1,128)S(1)}, f32[1,128]{1,0:T(1,128)S(1)}, u32[]{:S(2)}, u32[]{:S(2)}) collective-permute-start(f32[1,128]{1,0:T(1,128)S(1)} %get-tuple-element.82.refs_5_), channel_id=1, source_target_pairs={{0,1},{1,0},{2,3},{3,2},{4,5},{5,4},{6,7},{7,6},{8,9},{9,8},{10,11... | collective-permute-start | bytes 1544 | tf_op jit(solution)/shard_map/ppermute | solution.py:637
  107.6 15.2 %collective-permute-start.31 = (f32[1,128]{1,0:T(1,128)S(1)}, f32[1,128]{1,0:T(1,128)S(1)}, u32[]{:S(2)}, u32[]{:S(2)}) collective-permute-start(f32[1,128]{1,0:T(1,128)S(1)} %get-tuple-element.82.refs_5_), channel_id=1, source_target_pairs={{0,2},{1,3},{2,0},{3,1},{4,6},{5,7},{6,4},{7,5},{8,10},{9,11},{10,... | collective-permute-start | bytes 1544 | tf_op jit(solution)/shard_map/ppermute | solution.py:637
  109.2 13.5 %collective-permute-start.32 = (f32[1,128]{1,0:T(1,128)S(1)}, f32[1,128]{1,0:T(1,128)S(1)}, u32[]{:S(2)}, u32[]{:S(2)}) collective-permute-start(f32[1,128]{1,0:T(1,128)S(1)} %get-tuple-element.82.refs_5_), channel_id=1, source_target_pairs={{0,3},{1,2},{2,1},{3,0},{4,7},{5,6},{6,5},{7,4},{8,11},{9,10},{10,... | collective-permute-start | bytes 1544 | tf_op jit(solution)/shard_map/ppermute | solution.py:637
  114.2 11.6 %collective-permute-start.25 = (bf16[128,2048]{1,0:T(8,128)(2,1)S(1)}, bf16[128,2048]{1,0:T(8,128)(2,1)S(1)}, u32[]{:S(2)}, u32[]{:S(2)}) collective-permute-start(bf16[128,2048]{1,0:T(8,128)(2,1)S(1)} %get-tuple-element.78), channel_id=1, source_target_pairs={{0,32},{32,0},{64,96},{96,64},{1,33},{33,1},{65,97},{97,65},{2,34}... | collective-permute-start | bytes 1572872 | tf_op jit(solution)/shard_map/ppermute | solution.py:640
  (14 other events, 122.3 us)

commit v4 on v3

--- a/solution.py
+++ b/solution.py
@@ -221,8 +221,8 @@
     )(latent_param, squares, near(own), *[near(p) for p in parts])
 
 
-TILE = 512
-AHEAD = 3
+TILE = 1024
+AHEAD = 2
 
 
 def project_kernel(count, moved, flags, *refs):
@@ -662,7 +662,7 @@
     latents, entering = combine(latent_param, squares, p0, (r1, r2, r3))
 
     inner = [(i, i ^ 1) for i in range(seqs)]
-    outer = [(i, ((i + 1) ^ 1) - 1) for i in range(1, seqs - 1)]
+    outer = [(i, (((i + 1) ^ 1) - 1) % seqs) for i in range(seqs)]
     in_pair = lax.ppermute(latents, "seq", inner)
     across = lax.ppermute(latents, "seq", outer)
     odd = (c & 1) == 1

time: 129 us -> 126 us (0.977)
  starting transfers between devices: 55.1 us -> 53.4 us
    ppermute x1, starting transfers between devices: 4.4 us -> 2.51 us  [body(): across = lax.ppermute(latents, 'seq', outer)]
where the time goes in v4:
time: 126 us
  starting transfers between devices  53.4 us (42%)
  Pallas kernels  47.8 us (38%)
  waiting for transfers between devices  18.5 us (15%)
  local copies, waits for them, and re-layouts  3.42 us (3%)
  between operations  2.55 us (2%)
    ppermute x24, starting transfers between devices, mp_swap(): return lax.ppermute(a, 'mp', [(i, i ^ k) for i in range(mates)])  31.5 us
    pallas_call x1, Pallas kernels, project_both(): pl.pallas_call(project_both_kernel, out_shape=[pltpu.VMEM((rows, width),...  14.8 us
    ppermute x5, starting transfers between devices, core_swap(): return lax.ppermute(a, 'section', [(i, i ^ 1) for i in range(sections)])  13.9 us
    pallas_call x8, Pallas kernels, layer(): pl.pallas_call(functools.partial(layer_kernel, row, places, len(squares),...  13.8 us
    ppermute x24, waiting for transfers between devices, mp_swap(): return lax.ppermute(a, 'mp', [(i, i ^ k) for i in range(mates)])  10.5 us
    pallas_call x1, Pallas kernels, resample_sent(): pl.pallas_call(functools.partial(resample_sent_kernel, n), out_shape=[plt...  9.45 us
    ppermute x2, waiting for transfers between devices, cross(): return lax.ppermute(a, 'section', [(0, 2), (1, 3)])  4.07 us
    pallas_call x1, Pallas kernels, resample_own(): pl.pallas_call(resample_own_kernel, out_shape=pltpu.VMEM((LATENTS, vdim),...  3.9 us
  transfers between devices with their start and end apart: 34, of which 8 were waited for; matrix products, arithmetic and copies ran while one was open for 3% of the time, Pallas kernels for 37%

profile of v4, /device:TPU:7, one launch (start us, length us, event | category | flops | bytes accessed | tf_op | source)
XLA Modules:
  0.0 126.0 jit_solution(6108326369410834332)
XLA Ops:
  0.7 2.1 %copy.21.feat = bf16[4,257,1280]{2,1,0:T(8,128)(2,1)S(1)} copy(bf16[4,257,1280]{2,0,1:T(4,128)(2,1)} %param.13) | data formatting | bytes 5263360 | tf_op args[0]
  2.9 9.4 %resample.2 = (bf16[80,1280]{1,0:T(8,128)(2,1)}, bf16[80,1280]{1,0:T(8,128)(2,1)}, bf16[80,1280]{1,0:T(8,128)(2,1)}, f32[2,128]{1,0:T(2,128)S(1)}) custom-call(s32[5]{0:T(128)S(1)} %stack.58.ids, bf16[64,1280]{1,0:T(8,128)(2,1)S(1)} %copy-done, bf16[4,257,1280]{2,1,0:T(8,128)(2,1)S(1)} %copy.21.feat, bf16[4,128,2048]{2,1,0:T(8,128)(2,1)} %refs_1_.7, ...), custom_call_target="tpu_custom_call" | custom-call | tf_op jit(solution)/shard_map/resample/pallas_call | solution.py:165
  13.7 2.6 %collective-permute-start.1 = (bf16[80,1280]{1,0:T(8,128)(2,1)}, bf16[80,1280]{1,0:T(8,128)(2,1)}, u32[]{:S(2)}, u32[]{:S(2)}) collective-permute-start(bf16[80,1280]{1,0:T(8,128)(2,1)} %get-tuple-element.47), channel_id=1, source_target_pairs={{0,2},{1,3},{2,0},{3,1},{4,6},{5,7},{6,4},{7,5},{8,10},{9,11},{10,... | collective-permute-start | bytes 614408 | tf_op jit(solution)/shard_map/ppermute | solution.py:637
  16.4 3.9 %resample.3.own = f32[64,1280]{1,0:T(8,128)S(1)} custom-call(s32[1]{0:T(128)} %bitcast.8.ids, bf16[64,1280]{1,0:T(8,128)(2,1)S(1)} %copy-done, bf16[4,257,1280]{2,1,0:T(8,128)(2,1)S(1)} %copy.21.feat, bf16[1280,384]{1,0:T(8,128)(2,1)} %refs_0_.3, bf16[1280,384]{1,0:T(8,128)(2,1)} %refs_1_.5, bf16[1280,384]{1,0:T(8,128)(2,1)} %refs_2_.5, ...), custom_call_target="tpu_custom_call" | custom-call | tf_op jit(solution)/shard_map/resample/pallas_call | solution.py:186
  20.3 5.5 %collective-permute-done.1.b = bf16[80,1280]{1,0:T(8,128)(2,1)} collective-permute-done((bf16[80,1280]{1,0:T(8,128)(2,1)}, bf16[80,1280]{1,0:T(8,128)(2,1)}, u32[]{:S(2)}, u32[]{:S(2)}) %collective-permute-start.1) | collective-permute-done | bytes 204832 | tf_op jit(solution)/shard_map/ppermute | solution.py:637
  25.8 2.4 %collective-permute-done.2.c = bf16[80,1280]{1,0:T(8,128)(2,1)} collective-permute-done((bf16[80,1280]{1,0:T(8,128)(2,1)}, bf16[80,1280]{1,0:T(8,128)(2,1)}, u32[]{:S(2)}, u32[]{:S(2)}) %collective-permute-start.2) | collective-permute-done | bytes 204832 | tf_op jit(solution)/shard_map/ppermute | solution.py:637
  31.2 2.5 %collective-permute-start.4 = (bf16[64,1280]{1,0:T(8,128)(2,1)S(1)}, bf16[64,1280]{1,0:T(8,128)(2,1)S(1)}, u32[]{:S(2)}, u32[]{:S(2)}) collective-permute-start(bf16[64,1280]{1,0:T(8,128)(2,1)S(1)} %get-tuple-element.49), channel_id=1, source_target_pairs={{0,28},{4,8},{8,4},{12,16},{16,12},{20,24},{24,20},{28,0},{1,29},{... | collective-permute-start | bytes 491528 | tf_op jit(solution)/shard_map/ppermute | solution.py:667
  38.8 2.6 %collective-permute-start.7 = (bf16[64,1280]{1,0:T(8,128)(2,1)S(1)}, bf16[64,1280]{1,0:T(8,128)(2,1)S(1)}, u32[]{:S(2)}, u32[]{:S(2)}) collective-permute-start(bf16[64,1280]{1,0:T(8,128)(2,1)S(1)} %select_select_fusion.refs_0_), channel_id=1, source_target_pairs={{0,3},{1,2},{2,1},{3,0},{4,7},{5,6},{6,5},{7,4},{8,11},{9,10},{10,... | collective-permute-start | bytes 491528 | tf_op jit(solution)/shard_map/ppermute | solution.py:637
  42.3 3.9 %collective-permute-start.10 = (f32[1,128]{1,0:T(1,128)S(1)}, f32[1,128]{1,0:T(1,128)S(1)}, u32[]{:S(2)}, u32[]{:S(2)}) collective-permute-start(f32[1,128]{1,0:T(1,128)S(1)} %broadcast_in_dim.24), channel_id=1, source_target_pairs={{0,32},{32,0},{64,96},{96,64},{1,33},{33,1},{65,97},{97,65},{2,34}... | collective-permute-start | bytes 1544 | tf_op jit(solution)/shard_map/ppermute | solution.py:640
  49.8 2.6 %collective-permute-start.12 = (f32[1,128]{1,0:T(1,128)S(1)}, f32[1,128]{1,0:T(1,128)S(1)}, u32[]{:S(2)}, u32[]{:S(2)}) collective-permute-start(f32[1,128]{1,0:T(1,128)S(1)} %get-tuple-element.57.refs_4_), channel_id=1, source_target_pairs={{0,2},{1,3},{2,0},{3,1},{4,6},{5,7},{6,4},{7,5},{8,10},{9,11},{10,... | collective-permute-start | bytes 1544 | tf_op jit(solution)/shard_map/ppermute | solution.py:637
  54.3 1.9 %collective-permute-done.13.refs_7_ = f32[1,128]{1,0:T(1,128)S(1)} collective-permute-done((f32[1,128]{1,0:T(1,128)S(1)}, f32[1,128]{1,0:T(1,128)S(1)}, u32[]{:S(2)}, u32[]{:S(2)}) %collective-permute-start.13) | collective-permute-done | bytes 544 | tf_op jit(solution)/shard_map/ppermute | solution.py:637
  64.4 2.4 %collective-permute-start.18 = (f32[1,128]{1,0:T(1,128)S(1)}, f32[1,128]{1,0:T(1,128)S(1)}, u32[]{:S(2)}, u32[]{:S(2)}) collective-permute-start(f32[1,128]{1,0:T(1,128)S(1)} %get-tuple-element.69.refs_4_), channel_id=1, source_target_pairs={{0,3},{1,2},{2,1},{3,0},{4,7},{5,6},{6,5},{7,4},{8,11},{9,10},{10,... | collective-permute-start | bytes 1544 | tf_op jit(solution)/shard_map/ppermute | solution.py:637
  71.1 14.8 %project.7 = (bf16[512,2048]{1,0:T(8,128)(2,1)S(1)}, bf16[512,2048]{1,0:T(8,128)(2,1)S(1)}, bf16[512,2048]{1,0:T(8,128)(2,1)S(1)}, bf16[512,2048]{1,0:T(8,128)(2,1)S(1)}) custom-call(s32[2]{0:T(128)S(1)} %get-tuple-element.94.flags, bf16[256,1280]{1,0:T(8,128)(2,1)S(1)} %gather.1.refs_0_.a, bf16[256,1280]{1,0:T(8,128)(2,1)S(1)} %collective-permute-done.15.b.a, ...), custom_call_target="tpu_custom_call" | custom-call | flops 1000 | tf_op jit(solution)/shard_map/project/pallas_call | solution.py:367
  86.4 3.3 %collective-permute-start.20 = (f32[1,128]{1,0:T(1,128)S(1)}, f32[1,128]{1,0:T(1,128)S(1)}, u32[]{:S(2)}, u32[]{:S(2)}) collective-permute-start(f32[1,128]{1,0:T(1,128)S(1)} %from_line.2.refs_4_), channel_id=1, source_target_pairs={{0,2},{1,3},{2,0},{3,1},{4,6},{5,7},{6,4},{7,5},{8,10},{9,11},{10,... | collective-permute-start | bytes 1544 | tf_op jit(solution)/shard_map/ppermute | solution.py:637
  90.0 4.1 %collective-permute-done.26.x.refs_0_ = bf16[144,2048]{1,0:T(8,128)(2,1)S(1)} collective-permute-done((bf16[144,2048]{1,0:T(8,128)(2,1)S(1)}, bf16[144,2048]{1,0:T(8,128)(2,1)S(1)}, u32[]{:S(2)}, u32[]{:S(2)}) %collective-permute-start.26) | collective-permute-done | bytes 589856 | tf_op jit(solution)/shard_map/ppermute | solution.py:646
  94.1 1.9 %collective-permute-start.28 = (f32[1,128]{1,0:T(1,128)S(1)}, f32[1,128]{1,0:T(1,128)S(1)}, u32[]{:S(2)}, u32[]{:S(2)}) collective-permute-start(f32[1,128]{1,0:T(1,128)S(1)} %from_line.3.refs_4_), channel_id=1, source_target_pairs={{0,2},{1,3},{2,0},{3,1},{4,6},{5,7},{6,4},{7,5},{8,10},{9,11},{10,... | collective-permute-start | bytes 1544 | tf_op jit(solution)/shard_map/ppermute | solution.py:637
  96.0 2.0 %collective-permute-start.29 = (f32[1,128]{1,0:T(1,128)S(1)}, f32[1,128]{1,0:T(1,128)S(1)}, u32[]{:S(2)}, u32[]{:S(2)}) collective-permute-start(f32[1,128]{1,0:T(1,128)S(1)} %from_line.3.refs_4_), channel_id=1, source_target_pairs={{0,3},{1,2},{2,1},{3,0},{4,7},{5,6},{6,5},{7,4},{8,11},{9,10},{10,... | collective-permute-start | bytes 1544 | tf_op jit(solution)/shard_map/ppermute | solution.py:637
  99.3 1.9 %collective-permute-start.23 = (f32[1,128]{1,0:T(1,128)S(1)}, f32[1,128]{1,0:T(1,128)S(1)}, u32[]{:S(2)}, u32[]{:S(2)}) collective-permute-start(f32[1,128]{1,0:T(1,128)S(1)} %get-tuple-element.76.refs_5_), channel_id=1, source_target_pairs={{0,2},{1,3},{2,0},{3,1},{4,6},{5,7},{6,4},{7,5},{8,10},{9,11},{10,... | collective-permute-start | bytes 1544 | tf_op jit(solution)/shard_map/ppermute | solution.py:637
  101.5 2.0 %collective-permute-start.24 = (f32[1,128]{1,0:T(1,128)S(1)}, f32[1,128]{1,0:T(1,128)S(1)}, u32[]{:S(2)}, u32[]{:S(2)}) collective-permute-start(f32[1,128]{1,0:T(1,128)S(1)} %get-tuple-element.76.refs_5_), channel_id=1, source_target_pairs={{0,3},{1,2},{2,1},{3,0},{4,7},{5,6},{6,5},{7,4},{8,11},{9,10},{10,... | collective-permute-start | bytes 1544 | tf_op jit(solution)/shard_map/ppermute | solution.py:637
  104.9 1.9 %collective-permute-start.31 = (f32[1,128]{1,0:T(1,128)S(1)}, f32[1,128]{1,0:T(1,128)S(1)}, u32[]{:S(2)}, u32[]{:S(2)}) collective-permute-start(f32[1,128]{1,0:T(1,128)S(1)} %get-tuple-element.82.refs_5_), channel_id=1, source_target_pairs={{0,2},{1,3},{2,0},{3,1},{4,6},{5,7},{6,4},{7,5},{8,10},{9,11},{10,... | collective-permute-start | bytes 1544 | tf_op jit(solution)/shard_map/ppermute | solution.py:637
  106.8 2.0 %collective-permute-start.32 = (f32[1,128]{1,0:T(1,128)S(1)}, f32[1,128]{1,0:T(1,128)S(1)}, u32[]{:S(2)}, u32[]{:S(2)}) collective-permute-start(f32[1,128]{1,0:T(1,128)S(1)} %get-tuple-element.82.refs_5_), channel_id=1, source_target_pairs={{0,3},{1,2},{2,1},{3,0},{4,7},{5,6},{6,5},{7,4},{8,11},{9,10},{10,... | collective-permute-start | bytes 1544 | tf_op jit(solution)/shard_map/ppermute | solution.py:637
  109.0 2.5 %layer.13 = (bf16[128,2048]{1,0:T(8,128)(2,1)S(1)}, bf16[128,2048]{1,0:T(8,128)(2,1)S(1)}, f32[1,128]{1,0:T(1,128)}, bf16[512,2048]{1,0:T(8,128)(2,1)S(1)}, bf16[512,2048]{1,0:T(8,128)(2,1)S(1)}) custom-call(s32[2]{0:T(128)S(1)} %pad_add_fusion.refs_0_, ...), custom_call_target="tpu_custom_call", output_to_operand_aliasing={{3}: (11, {}), {4}: (12, {})} | custom-call | flops 1000 | tf_op jit(solution)/shard_map/layer/pallas_call | solution.py:552
  111.5 8.8 %collective-permute-start.25 = (bf16[128,2048]{1,0:T(8,128)(2,1)S(1)}, bf16[128,2048]{1,0:T(8,128)(2,1)S(1)}, u32[]{:S(2)}, u32[]{:S(2)}) collective-permute-start(bf16[128,2048]{1,0:T(8,128)(2,1)S(1)} %get-tuple-element.78), channel_id=1, source_target_pairs={{0,32},{32,0},{64,96},{96,64},{1,33},{33,1},{65,97},{97,65},{2,34}... | collective-permute-start | bytes 1572872 | tf_op jit(solution)/shard_map/ppermute | solution.py:640
  120.3 2.5 %layer.15 = (bf16[128,2048]{1,0:T(8,128)(2,1)S(1)}, bf16[128,2048]{1,0:T(8,128)(2,1)S(1)}, f32[1,128]{1,0:T(1,128)}) custom-call(s32[2]{0:T(128)S(1)} %pad_add_fusion.refs_0_, bf16[128,2048]{1,0:T(8,128)(2,1)S(1)} %get-tuple-element.79.refs_1_, f32[8,128]{1,0:T(8,128)S(1)} %get-tuple-element.86.refs_1_.refs_2_, ...), custom_call_target="tpu_custom_call" | custom-call | flops 1000 | tf_op jit(solution)/shard_map/layer/pallas_call | solution.py:552
  (91 shorter events, 33.9 us)
Async XLA Ops:
  0.0 47.6 %collective-permute-start.8 = (bf16[1,1280,2048]{2,1,0:T(8,128)(2,1)}, bf16[1,1280,2048]{2,1,0:T(8,128)(2,1)}, u32[]{:S(2)}, u32[]{:S(2)}) collective-permute-start(bf16[1,1280,2048]{2,1,0:T(8,128)(2,1)} %own_k.1), channel_id=1, source_target_pairs={{0,32},{32,0},{64,96},{96,64},{1,33},{33,1},{65,97},{97,65},{2,34}... | collective-permute-start | bytes 15728648 | tf_op jit(solution)/shard_map/ppermute | solution.py:640
  0.7 46.9 %collective-permute-start.9 = (bf16[1,1280,2048]{2,1,0:T(8,128)(2,1)}, bf16[1,1280,2048]{2,1,0:T(8,128)(2,1)}, u32[]{:S(2)}, u32[]{:S(2)}) collective-permute-start(bf16[1,1280,2048]{2,1,0:T(8,128)(2,1)} %own_v.1), channel_id=1, source_target_pairs={{0,32},{32,0},{64,96},{96,64},{1,33},{33,1},{65,97},{97,65},{2,34}... | collective-permute-start | bytes 15728648 | tf_op jit(solution)/shard_map/ppermute | solution.py:640
  12.3 7.9 %collective-permute-start = (bf16[80,1280]{1,0:T(8,128)(2,1)}, bf16[80,1280]{1,0:T(8,128)(2,1)S(1)}, u32[]{:S(2)}, u32[]{:S(2)}) collective-permute-start(bf16[80,1280]{1,0:T(8,128)(2,1)} %get-tuple-element.46), channel_id=1, source_target_pairs={{0,1},{1,0},{2,3},{3,2},{4,5},{5,4},{6,7},{7,6},{8,9},{9,8},{10,11... | collective-permute-start | bytes 614408 | tf_op jit(solution)/shard_map/ppermute | solution.py:637
  13.7 12.0 %collective-permute-start.1 = (bf16[80,1280]{1,0:T(8,128)(2,1)}, bf16[80,1280]{1,0:T(8,128)(2,1)}, u32[]{:S(2)}, u32[]{:S(2)}) collective-permute-start(bf16[80,1280]{1,0:T(8,128)(2,1)} %get-tuple-element.47), channel_id=1, source_target_pairs={{0,2},{1,3},{2,0},{3,1},{4,6},{5,7},{6,4},{7,5},{8,10},{9,11},{10,... | collective-permute-start | bytes 614408 | tf_op jit(solution)/shard_map/ppermute | solution.py:637
  16.3 11.8 %collective-permute-start.2 = (bf16[80,1280]{1,0:T(8,128)(2,1)}, bf16[80,1280]{1,0:T(8,128)(2,1)}, u32[]{:S(2)}, u32[]{:S(2)}) collective-permute-start(bf16[80,1280]{1,0:T(8,128)(2,1)} %get-tuple-element.48), channel_id=1, source_target_pairs={{0,3},{1,2},{2,1},{3,0},{4,7},{5,6},{6,5},{7,4},{8,11},{9,10},{10,... | collective-permute-start | bytes 614408 | tf_op jit(solution)/shard_map/ppermute | solution.py:637
  31.2 6.3 %collective-permute-start.4 = (bf16[64,1280]{1,0:T(8,128)(2,1)S(1)}, bf16[64,1280]{1,0:T(8,128)(2,1)S(1)}, u32[]{:S(2)}, u32[]{:S(2)}) collective-permute-start(bf16[64,1280]{1,0:T(8,128)(2,1)S(1)} %get-tuple-element.49), channel_id=1, source_target_pairs={{0,28},{4,8},{8,4},{12,16},{16,12},{20,24},{24,20},{28,0},{1,29},{... | collective-permute-start | bytes 491528 | tf_op jit(solution)/shard_map/ppermute | solution.py:667
  37.6 8.6 %collective-permute-start.6 = (bf16[64,1280]{1,0:T(8,128)(2,1)S(1)}, bf16[64,1280]{1,0:T(8,128)(2,1)S(1)}, u32[]{:S(2)}, u32[]{:S(2)}) collective-permute-start(bf16[64,1280]{1,0:T(8,128)(2,1)S(1)} %select_select_fusion.refs_0_), channel_id=1, source_target_pairs={{0,2},{1,3},{2,0},{3,1},{4,6},{5,7},{6,4},{7,5},{8,10},{9,11},{10,... | collective-permute-start | bytes 491528 | tf_op jit(solution)/shard_map/ppermute | solution.py:637
  38.8 7.4 %collective-permute-start.7 = (bf16[64,1280]{1,0:T(8,128)(2,1)S(1)}, bf16[64,1280]{1,0:T(8,128)(2,1)S(1)}, u32[]{:S(2)}, u32[]{:S(2)}) collective-permute-start(bf16[64,1280]{1,0:T(8,128)(2,1)S(1)} %select_select_fusion.refs_0_), channel_id=1, source_target_pairs={{0,3},{1,2},{2,1},{3,0},{4,7},{5,6},{6,5},{7,4},{8,11},{9,10},{10,... | collective-permute-start | bytes 491528 | tf_op jit(solution)/shard_map/ppermute | solution.py:637
  46.3 14.7 %collective-permute-start.15 = (bf16[256,1280]{1,0:T(8,128)(2,1)S(1)}, bf16[256,1280]{1,0:T(8,128)(2,1)S(1)}, u32[]{:S(2)}, u32[]{:S(2)}) collective-permute-start(bf16[256,1280]{1,0:T(8,128)(2,1)S(1)} %gather.1.refs_0_.a), channel_id=1, source_target_pairs={{0,64},{32,96},{64,0},{96,32},{1,65},{33,97},{65,1},{97,33},{2,66}... | collective-permute-start | bytes 1966088 | tf_op jit(solution)/shard_map/ppermute | solution.py:643
  58.1 27.9 %collective-permute-start.14 = (bf16[144,2048]{1,0:T(8,128)(2,1)S(1)}, bf16[144,2048]{1,0:T(8,128)(2,1)S(1)}, u32[]{:S(2)}, u32[]{:S(2)}) collective-permute-start(bf16[144,2048]{1,0:T(8,128)(2,1)S(1)} %get-tuple-element.58.refs_0_.refs_10_), channel_id=1, source_target_pairs={{0,64},{32,96},{1,65},{33,97},{2,66},{34,98},{3,67},{35,99},{4,68}... | collective-permute-start | bytes 1769480 | tf_op jit(solution)/shard_map/ppermute | solution.py:646
  69.8 24.2 %collective-permute-start.26 = (bf16[144,2048]{1,0:T(8,128)(2,1)S(1)}, bf16[144,2048]{1,0:T(8,128)(2,1)S(1)}, u32[]{:S(2)}, u32[]{:S(2)}) collective-permute-start(bf16[144,2048]{1,0:T(8,128)(2,1)S(1)} %get-tuple-element.70.refs_0_.refs_10_), channel_id=1, source_target_pairs={{0,64},{32,96},{1,65},{33,97},{2,66},{34,98},{3,67},{35,99},{4,68}... | collective-permute-start | bytes 1769480 | tf_op jit(solution)/shard_map/ppermute | solution.py:646
  86.0 10.0 %collective-permute-start.19 = (f32[1,128]{1,0:T(1,128)S(1)}, f32[1,128]{1,0:T(1,128)S(1)}, u32[]{:S(2)}, u32[]{:S(2)}) collective-permute-start(f32[1,128]{1,0:T(1,128)S(1)} %from_line.2.refs_4_), channel_id=1, source_target_pairs={{0,1},{1,0},{2,3},{3,2},{4,5},{5,4},{6,7},{7,6},{8,9},{9,8},{10,11... | collective-permute-start | bytes 1544 | tf_op jit(solution)/shard_map/ppermute | solution.py:637
  86.4 11.6 %collective-permute-start.20 = (f32[1,128]{1,0:T(1,128)S(1)}, f32[1,128]{1,0:T(1,128)S(1)}, u32[]{:S(2)}, u32[]{:S(2)}) collective-permute-start(f32[1,128]{1,0:T(1,128)S(1)} %from_line.2.refs_4_), channel_id=1, source_target_pairs={{0,2},{1,3},{2,0},{3,1},{4,6},{5,7},{6,4},{7,5},{8,10},{9,11},{10,... | collective-permute-start | bytes 1544 | tf_op jit(solution)/shard_map/ppermute | solution.py:637
  89.6 8.3 %collective-permute-start.21 = (f32[1,128]{1,0:T(1,128)S(1)}, f32[1,128]{1,0:T(1,128)S(1)}, u32[]{:S(2)}, u32[]{:S(2)}) collective-permute-start(f32[1,128]{1,0:T(1,128)S(1)} %from_line.2.refs_4_), channel_id=1, source_target_pairs={{0,3},{1,2},{2,1},{3,0},{4,7},{5,6},{6,5},{7,4},{8,11},{9,10},{10,... | collective-permute-start | bytes 1544 | tf_op jit(solution)/shard_map/ppermute | solution.py:637
  94.1 7.4 %collective-permute-start.27 = (f32[1,128]{1,0:T(1,128)S(1)}, f32[1,128]{1,0:T(1,128)S(1)}, u32[]{:S(2)}, u32[]{:S(2)}) collective-permute-start(f32[1,128]{1,0:T(1,128)S(1)} %from_line.3.refs_4_), channel_id=1, source_target_pairs={{0,1},{1,0},{2,3},{3,2},{4,5},{5,4},{6,7},{7,6},{8,9},{9,8},{10,11... | collective-permute-start | bytes 1544 | tf_op jit(solution)/shard_map/ppermute | solution.py:637
  94.1 9.4 %collective-permute-start.28 = (f32[1,128]{1,0:T(1,128)S(1)}, f32[1,128]{1,0:T(1,128)S(1)}, u32[]{:S(2)}, u32[]{:S(2)}) collective-permute-start(f32[1,128]{1,0:T(1,128)S(1)} %from_line.3.refs_4_), channel_id=1, source_target_pairs={{0,2},{1,3},{2,0},{3,1},{4,6},{5,7},{6,4},{7,5},{8,10},{9,11},{10,... | collective-permute-start | bytes 1544 | tf_op jit(solution)/shard_map/ppermute | solution.py:637
  96.0 7.5 %collective-permute-start.29 = (f32[1,128]{1,0:T(1,128)S(1)}, f32[1,128]{1,0:T(1,128)S(1)}, u32[]{:S(2)}, u32[]{:S(2)}) collective-permute-start(f32[1,128]{1,0:T(1,128)S(1)} %from_line.3.refs_4_), channel_id=1, source_target_pairs={{0,3},{1,2},{2,1},{3,0},{4,7},{5,6},{6,5},{7,4},{8,11},{9,10},{10,... | collective-permute-start | bytes 1544 | tf_op jit(solution)/shard_map/ppermute | solution.py:637
  99.2 7.5 %collective-permute-start.22 = (f32[1,128]{1,0:T(1,128)S(1)}, f32[1,128]{1,0:T(1,128)S(1)}, u32[]{:S(2)}, u32[]{:S(2)}) collective-permute-start(f32[1,128]{1,0:T(1,128)S(1)} %get-tuple-element.76.refs_5_), channel_id=1, source_target_pairs={{0,1},{1,0},{2,3},{3,2},{4,5},{5,4},{6,7},{7,6},{8,9},{9,8},{10,11... | collective-permute-start | bytes 1544 | tf_op jit(solution)/shard_map/ppermute | solution.py:637
  99.3 9.6 %collective-permute-start.23 = (f32[1,128]{1,0:T(1,128)S(1)}, f32[1,128]{1,0:T(1,128)S(1)}, u32[]{:S(2)}, u32[]{:S(2)}) collective-permute-start(f32[1,128]{1,0:T(1,128)S(1)} %get-tuple-element.76.refs_5_), channel_id=1, source_target_pairs={{0,2},{1,3},{2,0},{3,1},{4,6},{5,7},{6,4},{7,5},{8,10},{9,11},{10,... | collective-permute-start | bytes 1544 | tf_op jit(solution)/shard_map/ppermute | solution.py:637
  101.5 7.5 %collective-permute-start.24 = (f32[1,128]{1,0:T(1,128)S(1)}, f32[1,128]{1,0:T(1,128)S(1)}, u32[]{:S(2)}, u32[]{:S(2)}) collective-permute-start(f32[1,128]{1,0:T(1,128)S(1)} %get-tuple-element.76.refs_5_), channel_id=1, source_target_pairs={{0,3},{1,2},{2,1},{3,0},{4,7},{5,6},{6,5},{7,4},{8,11},{9,10},{10,... | collective-permute-start | bytes 1544 | tf_op jit(solution)/shard_map/ppermute | solution.py:637
  104.8 15.5 %collective-permute-start.30 = (f32[1,128]{1,0:T(1,128)S(1)}, f32[1,128]{1,0:T(1,128)S(1)}, u32[]{:S(2)}, u32[]{:S(2)}) collective-permute-start(f32[1,128]{1,0:T(1,128)S(1)} %get-tuple-element.82.refs_5_), channel_id=1, source_target_pairs={{0,1},{1,0},{2,3},{3,2},{4,5},{5,4},{6,7},{7,6},{8,9},{9,8},{10,11... | collective-permute-start | bytes 1544 | tf_op jit(solution)/shard_map/ppermute | solution.py:637
  104.9 15.4 %collective-permute-start.31 = (f32[1,128]{1,0:T(1,128)S(1)}, f32[1,128]{1,0:T(1,128)S(1)}, u32[]{:S(2)}, u32[]{:S(2)}) collective-permute-start(f32[1,128]{1,0:T(1,128)S(1)} %get-tuple-element.82.refs_5_), channel_id=1, source_target_pairs={{0,2},{1,3},{2,0},{3,1},{4,6},{5,7},{6,4},{7,5},{8,10},{9,11},{10,... | collective-permute-start | bytes 1544 | tf_op jit(solution)/shard_map/ppermute | solution.py:637
  106.8 13.6 %collective-permute-start.32 = (f32[1,128]{1,0:T(1,128)S(1)}, f32[1,128]{1,0:T(1,128)S(1)}, u32[]{:S(2)}, u32[]{:S(2)}) collective-permute-start(f32[1,128]{1,0:T(1,128)S(1)} %get-tuple-element.82.refs_5_), channel_id=1, source_target_pairs={{0,3},{1,2},{2,1},{3,0},{4,7},{5,6},{6,5},{7,4},{8,11},{9,10},{10,... | collective-permute-start | bytes 1544 | tf_op jit(solution)/shard_map/ppermute | solution.py:637
  111.5 11.8 %collective-permute-start.25 = (bf16[128,2048]{1,0:T(8,128)(2,1)S(1)}, bf16[128,2048]{1,0:T(8,128)(2,1)S(1)}, u32[]{:S(2)}, u32[]{:S(2)}) collective-permute-start(bf16[128,2048]{1,0:T(8,128)(2,1)S(1)} %get-tuple-element.78), channel_id=1, source_target_pairs={{0,32},{32,0},{64,96},{96,64},{1,33},{33,1},{65,97},{97,65},{2,34}... | collective-permute-start | bytes 1572872 | tf_op jit(solution)/shard_map/ppermute | solution.py:640
  (14 other events, 115.6 us)

commit v5 on v4

--- a/solution.py
+++ b/solution.py
@@ -57,7 +57,7 @@
 IN_HBM = pl.BlockSpec(memory_space=pltpu.HBM)
 
 
-def resample_updates(frames, lat, weights, held, ctx, tail, pk, pv, pqm, mixed, sems):
+def resample_updates(frames, lat, weights, held, ctx, tail, pk, pv, pqm, mixed, sems, midway=()):
     n = len(frames)
     patches = frames[0].shape[0]
     keys = LATENTS + patches
@@ -92,6 +92,8 @@
     pk[:, cut:] = both[:, :side]
     pv[:, cut:inner] = both[:, side:]
     loads[0].wait()
+    for load in midway:
+        load.start()
     pq = dot(base, qp[...]).astype(BF16).astype(F32)
     which = lax.broadcasted_iota(jnp.int32, (LATENTS, inner), 1) // PHEAD
     for h in range(heads):
@@ -138,9 +140,7 @@
         pltpu.make_async_copy(hid.at[ids[n + i]], near_hid[i], hid_sems.at[i]) for i in range(2)
     ]
     frames = [feat.at[ids[i]] for i in range(n)]
-    update = resample_updates(frames, lat, weights, refs[3:7], *refs[7:])
-    for load in loads:
-        load.start()
+    update = resample_updates(frames, lat, weights, refs[3:7], *refs[7:], midway=loads)
     for i in range(n):
         sent[i][0:LATENTS, :] = update[i * LATENTS : (i + 1) * LATENTS].astype(BF16)
     lines = []

time: 126 us -> 126 us (level)
  no operation moved by 1% of the time
where the time goes in v5:
time: 126 us; the launch traced here: 125 us
  starting transfers between devices  53.4 us (42%)
  Pallas kernels  47.2 us (37%)
  waiting for transfers between devices  18.5 us (15%)
  local copies, waits for them, and re-layouts  3.42 us (3%)
  between operations  2.55 us (2%)
    ppermute x24, starting transfers between devices, mp_swap(): return lax.ppermute(a, 'mp', [(i, i ^ k) for i in range(mates)])  31.5 us
    pallas_call x1, Pallas kernels, project_both(): pl.pallas_call(project_both_kernel, out_shape=[pltpu.VMEM((rows, width),...  14.8 us
    ppermute x5, starting transfers between devices, core_swap(): return lax.ppermute(a, 'section', [(i, i ^ 1) for i in range(sections)])  13.9 us
    pallas_call x8, Pallas kernels, layer(): pl.pallas_call(functools.partial(layer_kernel, row, places, len(squares),...  13.8 us
    ppermute x24, waiting for transfers between devices, mp_swap(): return lax.ppermute(a, 'mp', [(i, i ^ k) for i in range(mates)])  10.5 us
    pallas_call x1, Pallas kernels, resample_sent(): pl.pallas_call(functools.partial(resample_sent_kernel, n), out_shape=[plt...  8.87 us
    ppermute x2, waiting for transfers between devices, cross(): return lax.ppermute(a, 'section', [(0, 2), (1, 3)])  4.07 us
    pallas_call x1, Pallas kernels, resample_own(): pl.pallas_call(resample_own_kernel, out_shape=pltpu.VMEM((LATENTS, vdim),...  3.88 us
  transfers between devices with their start and end apart: 34, of which 8 were waited for; matrix products, arithmetic and copies ran while one was open for 3% of the time, Pallas kernels for 37%

profile of v5, /device:TPU:7, one launch (start us, length us, event | category | flops | bytes accessed | tf_op | source)
XLA Modules:
  0.0 125.4 jit_solution(1021960448413662366)
XLA Ops:
  0.7 2.1 %copy.21.feat = bf16[4,257,1280]{2,1,0:T(8,128)(2,1)S(1)} copy(bf16[4,257,1280]{2,0,1:T(4,128)(2,1)} %param.13) | data formatting | bytes 5263360 | tf_op args[0]
  2.9 8.9 %resample.2 = (bf16[80,1280]{1,0:T(8,128)(2,1)}, bf16[80,1280]{1,0:T(8,128)(2,1)}, bf16[80,1280]{1,0:T(8,128)(2,1)}, f32[2,128]{1,0:T(2,128)S(1)}) custom-call(s32[5]{0:T(128)S(1)} %stack.58.ids, bf16[64,1280]{1,0:T(8,128)(2,1)S(1)} %copy-done, bf16[4,257,1280]{2,1,0:T(8,128)(2,1)S(1)} %copy.21.feat, bf16[4,128,2048]{2,1,0:T(8,128)(2,1)} %refs_1_.7, ...), custom_call_target="tpu_custom_call" | custom-call | tf_op jit(solution)/shard_map/resample/pallas_call | solution.py:165
  13.1 2.6 %collective-permute-start.1 = (bf16[80,1280]{1,0:T(8,128)(2,1)}, bf16[80,1280]{1,0:T(8,128)(2,1)}, u32[]{:S(2)}, u32[]{:S(2)}) collective-permute-start(bf16[80,1280]{1,0:T(8,128)(2,1)} %get-tuple-element.47), channel_id=1, source_target_pairs={{0,2},{1,3},{2,0},{3,1},{4,6},{5,7},{6,4},{7,5},{8,10},{9,11},{10,... | collective-permute-start | bytes 614408 | tf_op jit(solution)/shard_map/ppermute | solution.py:637
  15.8 3.9 %resample.3.own = f32[64,1280]{1,0:T(8,128)S(1)} custom-call(s32[1]{0:T(128)} %bitcast.8.ids, bf16[64,1280]{1,0:T(8,128)(2,1)S(1)} %copy-done, bf16[4,257,1280]{2,1,0:T(8,128)(2,1)S(1)} %copy.21.feat, bf16[1280,384]{1,0:T(8,128)(2,1)} %refs_0_.3, bf16[1280,384]{1,0:T(8,128)(2,1)} %refs_1_.5, bf16[1280,384]{1,0:T(8,128)(2,1)} %refs_2_.5, ...), custom_call_target="tpu_custom_call" | custom-call | tf_op jit(solution)/shard_map/resample/pallas_call | solution.py:186
  19.7 5.5 %collective-permute-done.1.b = bf16[80,1280]{1,0:T(8,128)(2,1)} collective-permute-done((bf16[80,1280]{1,0:T(8,128)(2,1)}, bf16[80,1280]{1,0:T(8,128)(2,1)}, u32[]{:S(2)}, u32[]{:S(2)}) %collective-permute-start.1) | collective-permute-done | bytes 204832 | tf_op jit(solution)/shard_map/ppermute | solution.py:637
  25.2 2.4 %collective-permute-done.2.c = bf16[80,1280]{1,0:T(8,128)(2,1)} collective-permute-done((bf16[80,1280]{1,0:T(8,128)(2,1)}, bf16[80,1280]{1,0:T(8,128)(2,1)}, u32[]{:S(2)}, u32[]{:S(2)}) %collective-permute-start.2) | collective-permute-done | bytes 204832 | tf_op jit(solution)/shard_map/ppermute | solution.py:637
  30.6 2.5 %collective-permute-start.4 = (bf16[64,1280]{1,0:T(8,128)(2,1)S(1)}, bf16[64,1280]{1,0:T(8,128)(2,1)S(1)}, u32[]{:S(2)}, u32[]{:S(2)}) collective-permute-start(bf16[64,1280]{1,0:T(8,128)(2,1)S(1)} %get-tuple-element.49), channel_id=1, source_target_pairs={{0,28},{4,8},{8,4},{12,16},{16,12},{20,24},{24,20},{28,0},{1,29},{... | collective-permute-start | bytes 491528 | tf_op jit(solution)/shard_map/ppermute | solution.py:667
  38.2 2.6 %collective-permute-start.7 = (bf16[64,1280]{1,0:T(8,128)(2,1)S(1)}, bf16[64,1280]{1,0:T(8,128)(2,1)S(1)}, u32[]{:S(2)}, u32[]{:S(2)}) collective-permute-start(bf16[64,1280]{1,0:T(8,128)(2,1)S(1)} %select_select_fusion.refs_0_), channel_id=1, source_target_pairs={{0,3},{1,2},{2,1},{3,0},{4,7},{5,6},{6,5},{7,4},{8,11},{9,10},{10,... | collective-permute-start | bytes 491528 | tf_op jit(solution)/shard_map/ppermute | solution.py:637
  41.7 3.9 %collective-permute-start.10 = (f32[1,128]{1,0:T(1,128)S(1)}, f32[1,128]{1,0:T(1,128)S(1)}, u32[]{:S(2)}, u32[]{:S(2)}) collective-permute-start(f32[1,128]{1,0:T(1,128)S(1)} %broadcast_in_dim.24), channel_id=1, source_target_pairs={{0,32},{32,0},{64,96},{96,64},{1,33},{33,1},{65,97},{97,65},{2,34}... | collective-permute-start | bytes 1544 | tf_op jit(solution)/shard_map/ppermute | solution.py:640
  49.2 2.6 %collective-permute-start.12 = (f32[1,128]{1,0:T(1,128)S(1)}, f32[1,128]{1,0:T(1,128)S(1)}, u32[]{:S(2)}, u32[]{:S(2)}) collective-permute-start(f32[1,128]{1,0:T(1,128)S(1)} %get-tuple-element.57.refs_4_), channel_id=1, source_target_pairs={{0,2},{1,3},{2,0},{3,1},{4,6},{5,7},{6,4},{7,5},{8,10},{9,11},{10,... | collective-permute-start | bytes 1544 | tf_op jit(solution)/shard_map/ppermute | solution.py:637
  53.7 1.9 %collective-permute-done.13.refs_7_ = f32[1,128]{1,0:T(1,128)S(1)} collective-permute-done((f32[1,128]{1,0:T(1,128)S(1)}, f32[1,128]{1,0:T(1,128)S(1)}, u32[]{:S(2)}, u32[]{:S(2)}) %collective-permute-start.13) | collective-permute-done | bytes 544 | tf_op jit(solution)/shard_map/ppermute | solution.py:637
  63.8 2.4 %collective-permute-start.18 = (f32[1,128]{1,0:T(1,128)S(1)}, f32[1,128]{1,0:T(1,128)S(1)}, u32[]{:S(2)}, u32[]{:S(2)}) collective-permute-start(f32[1,128]{1,0:T(1,128)S(1)} %get-tuple-element.69.refs_4_), channel_id=1, source_target_pairs={{0,3},{1,2},{2,1},{3,0},{4,7},{5,6},{6,5},{7,4},{8,11},{9,10},{10,... | collective-permute-start | bytes 1544 | tf_op jit(solution)/shard_map/ppermute | solution.py:637
  70.6 14.8 %project.7 = (bf16[512,2048]{1,0:T(8,128)(2,1)S(1)}, bf16[512,2048]{1,0:T(8,128)(2,1)S(1)}, bf16[512,2048]{1,0:T(8,128)(2,1)S(1)}, bf16[512,2048]{1,0:T(8,128)(2,1)S(1)}) custom-call(s32[2]{0:T(128)S(1)} %get-tuple-element.94.flags, bf16[256,1280]{1,0:T(8,128)(2,1)S(1)} %gather.1.refs_0_.a, bf16[256,1280]{1,0:T(8,128)(2,1)S(1)} %collective-permute-done.15.b.a, ...), custom_call_target="tpu_custom_call" | custom-call | flops 1000 | tf_op jit(solution)/shard_map/project/pallas_call | solution.py:367
  85.8 3.3 %collective-permute-start.20 = (f32[1,128]{1,0:T(1,128)S(1)}, f32[1,128]{1,0:T(1,128)S(1)}, u32[]{:S(2)}, u32[]{:S(2)}) collective-permute-start(f32[1,128]{1,0:T(1,128)S(1)} %from_line.2.refs_4_), channel_id=1, source_target_pairs={{0,2},{1,3},{2,0},{3,1},{4,6},{5,7},{6,4},{7,5},{8,10},{9,11},{10,... | collective-permute-start | bytes 1544 | tf_op jit(solution)/shard_map/ppermute | solution.py:637
  89.4 4.1 %collective-permute-done.26.x.refs_0_ = bf16[144,2048]{1,0:T(8,128)(2,1)S(1)} collective-permute-done((bf16[144,2048]{1,0:T(8,128)(2,1)S(1)}, bf16[144,2048]{1,0:T(8,128)(2,1)S(1)}, u32[]{:S(2)}, u32[]{:S(2)}) %collective-permute-start.26) | collective-permute-done | bytes 589856 | tf_op jit(solution)/shard_map/ppermute | solution.py:646
  93.5 1.9 %collective-permute-start.28 = (f32[1,128]{1,0:T(1,128)S(1)}, f32[1,128]{1,0:T(1,128)S(1)}, u32[]{:S(2)}, u32[]{:S(2)}) collective-permute-start(f32[1,128]{1,0:T(1,128)S(1)} %from_line.3.refs_4_), channel_id=1, source_target_pairs={{0,2},{1,3},{2,0},{3,1},{4,6},{5,7},{6,4},{7,5},{8,10},{9,11},{10,... | collective-permute-start | bytes 1544 | tf_op jit(solution)/shard_map/ppermute | solution.py:637
  95.4 2.0 %collective-permute-start.29 = (f32[1,128]{1,0:T(1,128)S(1)}, f32[1,128]{1,0:T(1,128)S(1)}, u32[]{:S(2)}, u32[]{:S(2)}) collective-permute-start(f32[1,128]{1,0:T(1,128)S(1)} %from_line.3.refs_4_), channel_id=1, source_target_pairs={{0,3},{1,2},{2,1},{3,0},{4,7},{5,6},{6,5},{7,4},{8,11},{9,10},{10,... | collective-permute-start | bytes 1544 | tf_op jit(solution)/shard_map/ppermute | solution.py:637
  98.8 1.9 %collective-permute-start.23 = (f32[1,128]{1,0:T(1,128)S(1)}, f32[1,128]{1,0:T(1,128)S(1)}, u32[]{:S(2)}, u32[]{:S(2)}) collective-permute-start(f32[1,128]{1,0:T(1,128)S(1)} %get-tuple-element.76.refs_5_), channel_id=1, source_target_pairs={{0,2},{1,3},{2,0},{3,1},{4,6},{5,7},{6,4},{7,5},{8,10},{9,11},{10,... | collective-permute-start | bytes 1544 | tf_op jit(solution)/shard_map/ppermute | solution.py:637
  100.9 2.0 %collective-permute-start.24 = (f32[1,128]{1,0:T(1,128)S(1)}, f32[1,128]{1,0:T(1,128)S(1)}, u32[]{:S(2)}, u32[]{:S(2)}) collective-permute-start(f32[1,128]{1,0:T(1,128)S(1)} %get-tuple-element.76.refs_5_), channel_id=1, source_target_pairs={{0,3},{1,2},{2,1},{3,0},{4,7},{5,6},{6,5},{7,4},{8,11},{9,10},{10,... | collective-permute-start | bytes 1544 | tf_op jit(solution)/shard_map/ppermute | solution.py:637
  104.3 1.9 %collective-permute-start.31 = (f32[1,128]{1,0:T(1,128)S(1)}, f32[1,128]{1,0:T(1,128)S(1)}, u32[]{:S(2)}, u32[]{:S(2)}) collective-permute-start(f32[1,128]{1,0:T(1,128)S(1)} %get-tuple-element.82.refs_5_), channel_id=1, source_target_pairs={{0,2},{1,3},{2,0},{3,1},{4,6},{5,7},{6,4},{7,5},{8,10},{9,11},{10,... | collective-permute-start | bytes 1544 | tf_op jit(solution)/shard_map/ppermute | solution.py:637
  106.2 2.0 %collective-permute-start.32 = (f32[1,128]{1,0:T(1,128)S(1)}, f32[1,128]{1,0:T(1,128)S(1)}, u32[]{:S(2)}, u32[]{:S(2)}) collective-permute-start(f32[1,128]{1,0:T(1,128)S(1)} %get-tuple-element.82.refs_5_), channel_id=1, source_target_pairs={{0,3},{1,2},{2,1},{3,0},{4,7},{5,6},{6,5},{7,4},{8,11},{9,10},{10,... | collective-permute-start | bytes 1544 | tf_op jit(solution)/shard_map/ppermute | solution.py:637
  108.4 2.5 %layer.13 = (bf16[128,2048]{1,0:T(8,128)(2,1)S(1)}, bf16[128,2048]{1,0:T(8,128)(2,1)S(1)}, f32[1,128]{1,0:T(1,128)}, bf16[512,2048]{1,0:T(8,128)(2,1)S(1)}, bf16[512,2048]{1,0:T(8,128)(2,1)S(1)}) custom-call(s32[2]{0:T(128)S(1)} %pad_add_fusion.refs_0_, ...), custom_call_target="tpu_custom_call", output_to_operand_aliasing={{3}: (11, {}), {4}: (12, {})} | custom-call | flops 1000 | tf_op jit(solution)/shard_map/layer/pallas_call | solution.py:552
  110.9 8.8 %collective-permute-start.25 = (bf16[128,2048]{1,0:T(8,128)(2,1)S(1)}, bf16[128,2048]{1,0:T(8,128)(2,1)S(1)}, u32[]{:S(2)}, u32[]{:S(2)}) collective-permute-start(bf16[128,2048]{1,0:T(8,128)(2,1)S(1)} %get-tuple-element.78), channel_id=1, source_target_pairs={{0,32},{32,0},{64,96},{96,64},{1,33},{33,1},{65,97},{97,65},{2,34}... | collective-permute-start | bytes 1572872 | tf_op jit(solution)/shard_map/ppermute | solution.py:640
  119.8 2.5 %layer.15 = (bf16[128,2048]{1,0:T(8,128)(2,1)S(1)}, bf16[128,2048]{1,0:T(8,128)(2,1)S(1)}, f32[1,128]{1,0:T(1,128)}) custom-call(s32[2]{0:T(128)S(1)} %pad_add_fusion.refs_0_, bf16[128,2048]{1,0:T(8,128)(2,1)S(1)} %get-tuple-element.79.refs_1_, f32[8,128]{1,0:T(8,128)S(1)} %get-tuple-element.86.refs_1_.refs_2_, ...), custom_call_target="tpu_custom_call" | custom-call | flops 1000 | tf_op jit(solution)/shard_map/layer/pallas_call | solution.py:552
  (91 shorter events, 33.9 us)
Async XLA Ops:
  0.0 47.0 %collective-permute-start.8 = (bf16[1,1280,2048]{2,1,0:T(8,128)(2,1)}, bf16[1,1280,2048]{2,1,0:T(8,128)(2,1)}, u32[]{:S(2)}, u32[]{:S(2)}) collective-permute-start(bf16[1,1280,2048]{2,1,0:T(8,128)(2,1)} %own_k.1), channel_id=1, source_target_pairs={{0,32},{32,0},{64,96},{96,64},{1,33},{33,1},{65,97},{97,65},{2,34}... | collective-permute-start | bytes 15728648 | tf_op jit(solution)/shard_map/ppermute | solution.py:640
  0.7 46.3 %collective-permute-start.9 = (bf16[1,1280,2048]{2,1,0:T(8,128)(2,1)}, bf16[1,1280,2048]{2,1,0:T(8,128)(2,1)}, u32[]{:S(2)}, u32[]{:S(2)}) collective-permute-start(bf16[1,1280,2048]{2,1,0:T(8,128)(2,1)} %own_v.1), channel_id=1, source_target_pairs={{0,32},{32,0},{64,96},{96,64},{1,33},{33,1},{65,97},{97,65},{2,34}... | collective-permute-start | bytes 15728648 | tf_op jit(solution)/shard_map/ppermute | solution.py:640
  11.8 7.9 %collective-permute-start = (bf16[80,1280]{1,0:T(8,128)(2,1)}, bf16[80,1280]{1,0:T(8,128)(2,1)S(1)}, u32[]{:S(2)}, u32[]{:S(2)}) collective-permute-start(bf16[80,1280]{1,0:T(8,128)(2,1)} %get-tuple-element.46), channel_id=1, source_target_pairs={{0,1},{1,0},{2,3},{3,2},{4,5},{5,4},{6,7},{7,6},{8,9},{9,8},{10,11... | collective-permute-start | bytes 614408 | tf_op jit(solution)/shard_map/ppermute | solution.py:637
  13.1 12.0 %collective-permute-start.1 = (bf16[80,1280]{1,0:T(8,128)(2,1)}, bf16[80,1280]{1,0:T(8,128)(2,1)}, u32[]{:S(2)}, u32[]{:S(2)}) collective-permute-start(bf16[80,1280]{1,0:T(8,128)(2,1)} %get-tuple-element.47), channel_id=1, source_target_pairs={{0,2},{1,3},{2,0},{3,1},{4,6},{5,7},{6,4},{7,5},{8,10},{9,11},{10,... | collective-permute-start | bytes 614408 | tf_op jit(solution)/shard_map/ppermute | solution.py:637
  15.8 11.8 %collective-permute-start.2 = (bf16[80,1280]{1,0:T(8,128)(2,1)}, bf16[80,1280]{1,0:T(8,128)(2,1)}, u32[]{:S(2)}, u32[]{:S(2)}) collective-permute-start(bf16[80,1280]{1,0:T(8,128)(2,1)} %get-tuple-element.48), channel_id=1, source_target_pairs={{0,3},{1,2},{2,1},{3,0},{4,7},{5,6},{6,5},{7,4},{8,11},{9,10},{10,... | collective-permute-start | bytes 614408 | tf_op jit(solution)/shard_map/ppermute | solution.py:637
  30.6 6.3 %collective-permute-start.4 = (bf16[64,1280]{1,0:T(8,128)(2,1)S(1)}, bf16[64,1280]{1,0:T(8,128)(2,1)S(1)}, u32[]{:S(2)}, u32[]{:S(2)}) collective-permute-start(bf16[64,1280]{1,0:T(8,128)(2,1)S(1)} %get-tuple-element.49), channel_id=1, source_target_pairs={{0,28},{4,8},{8,4},{12,16},{16,12},{20,24},{24,20},{28,0},{1,29},{... | collective-permute-start | bytes 491528 | tf_op jit(solution)/shard_map/ppermute | solution.py:667
  37.0 8.6 %collective-permute-start.6 = (bf16[64,1280]{1,0:T(8,128)(2,1)S(1)}, bf16[64,1280]{1,0:T(8,128)(2,1)S(1)}, u32[]{:S(2)}, u32[]{:S(2)}) collective-permute-start(bf16[64,1280]{1,0:T(8,128)(2,1)S(1)} %select_select_fusion.refs_0_), channel_id=1, source_target_pairs={{0,2},{1,3},{2,0},{3,1},{4,6},{5,7},{6,4},{7,5},{8,10},{9,11},{10,... | collective-permute-start | bytes 491528 | tf_op jit(solution)/shard_map/ppermute | solution.py:637
  38.2 7.4 %collective-permute-start.7 = (bf16[64,1280]{1,0:T(8,128)(2,1)S(1)}, bf16[64,1280]{1,0:T(8,128)(2,1)S(1)}, u32[]{:S(2)}, u32[]{:S(2)}) collective-permute-start(bf16[64,1280]{1,0:T(8,128)(2,1)S(1)} %select_select_fusion.refs_0_), channel_id=1, source_target_pairs={{0,3},{1,2},{2,1},{3,0},{4,7},{5,6},{6,5},{7,4},{8,11},{9,10},{10,... | collective-permute-start | bytes 491528 | tf_op jit(solution)/shard_map/ppermute | solution.py:637
  45.7 14.7 %collective-permute-start.15 = (bf16[256,1280]{1,0:T(8,128)(2,1)S(1)}, bf16[256,1280]{1,0:T(8,128)(2,1)S(1)}, u32[]{:S(2)}, u32[]{:S(2)}) collective-permute-start(bf16[256,1280]{1,0:T(8,128)(2,1)S(1)} %gather.1.refs_0_.a), channel_id=1, source_target_pairs={{0,64},{32,96},{64,0},{96,32},{1,65},{33,97},{65,1},{97,33},{2,66}... | collective-permute-start | bytes 1966088 | tf_op jit(solution)/shard_map/ppermute | solution.py:643
  57.5 27.9 %collective-permute-start.14 = (bf16[144,2048]{1,0:T(8,128)(2,1)S(1)}, bf16[144,2048]{1,0:T(8,128)(2,1)S(1)}, u32[]{:S(2)}, u32[]{:S(2)}) collective-permute-start(bf16[144,2048]{1,0:T(8,128)(2,1)S(1)} %get-tuple-element.58.refs_0_.refs_10_), channel_id=1, source_target_pairs={{0,64},{32,96},{1,65},{33,97},{2,66},{34,98},{3,67},{35,99},{4,68}... | collective-permute-start | bytes 1769480 | tf_op jit(solution)/shard_map/ppermute | solution.py:646
  69.3 24.2 %collective-permute-start.26 = (bf16[144,2048]{1,0:T(8,128)(2,1)S(1)}, bf16[144,2048]{1,0:T(8,128)(2,1)S(1)}, u32[]{:S(2)}, u32[]{:S(2)}) collective-permute-start(bf16[144,2048]{1,0:T(8,128)(2,1)S(1)} %get-tuple-element.70.refs_0_.refs_10_), channel_id=1, source_target_pairs={{0,64},{32,96},{1,65},{33,97},{2,66},{34,98},{3,67},{35,99},{4,68}... | collective-permute-start | bytes 1769480 | tf_op jit(solution)/shard_map/ppermute | solution.py:646
  85.4 10.0 %collective-permute-start.19 = (f32[1,128]{1,0:T(1,128)S(1)}, f32[1,128]{1,0:T(1,128)S(1)}, u32[]{:S(2)}, u32[]{:S(2)}) collective-permute-start(f32[1,128]{1,0:T(1,128)S(1)} %from_line.2.refs_4_), channel_id=1, source_target_pairs={{0,1},{1,0},{2,3},{3,2},{4,5},{5,4},{6,7},{7,6},{8,9},{9,8},{10,11... | collective-permute-start | bytes 1544 | tf_op jit(solution)/shard_map/ppermute | solution.py:637
  85.8 11.6 %collective-permute-start.20 = (f32[1,128]{1,0:T(1,128)S(1)}, f32[1,128]{1,0:T(1,128)S(1)}, u32[]{:S(2)}, u32[]{:S(2)}) collective-permute-start(f32[1,128]{1,0:T(1,128)S(1)} %from_line.2.refs_4_), channel_id=1, source_target_pairs={{0,2},{1,3},{2,0},{3,1},{4,6},{5,7},{6,4},{7,5},{8,10},{9,11},{10,... | collective-permute-start | bytes 1544 | tf_op jit(solution)/shard_map/ppermute | solution.py:637
  89.1 8.3 %collective-permute-start.21 = (f32[1,128]{1,0:T(1,128)S(1)}, f32[1,128]{1,0:T(1,128)S(1)}, u32[]{:S(2)}, u32[]{:S(2)}) collective-permute-start(f32[1,128]{1,0:T(1,128)S(1)} %from_line.2.refs_4_), channel_id=1, source_target_pairs={{0,3},{1,2},{2,1},{3,0},{4,7},{5,6},{6,5},{7,4},{8,11},{9,10},{10,... | collective-permute-start | bytes 1544 | tf_op jit(solution)/shard_map/ppermute | solution.py:637
  93.5 7.4 %collective-permute-start.27 = (f32[1,128]{1,0:T(1,128)S(1)}, f32[1,128]{1,0:T(1,128)S(1)}, u32[]{:S(2)}, u32[]{:S(2)}) collective-permute-start(f32[1,128]{1,0:T(1,128)S(1)} %from_line.3.refs_4_), channel_id=1, source_target_pairs={{0,1},{1,0},{2,3},{3,2},{4,5},{5,4},{6,7},{7,6},{8,9},{9,8},{10,11... | collective-permute-start | bytes 1544 | tf_op jit(solution)/shard_map/ppermute | solution.py:637
  93.5 9.4 %collective-permute-start.28 = (f32[1,128]{1,0:T(1,128)S(1)}, f32[1,128]{1,0:T(1,128)S(1)}, u32[]{:S(2)}, u32[]{:S(2)}) collective-permute-start(f32[1,128]{1,0:T(1,128)S(1)} %from_line.3.refs_4_), channel_id=1, source_target_pairs={{0,2},{1,3},{2,0},{3,1},{4,6},{5,7},{6,4},{7,5},{8,10},{9,11},{10,... | collective-permute-start | bytes 1544 | tf_op jit(solution)/shard_map/ppermute | solution.py:637
  95.4 7.5 %collective-permute-start.29 = (f32[1,128]{1,0:T(1,128)S(1)}, f32[1,128]{1,0:T(1,128)S(1)}, u32[]{:S(2)}, u32[]{:S(2)}) collective-permute-start(f32[1,128]{1,0:T(1,128)S(1)} %from_line.3.refs_4_), channel_id=1, source_target_pairs={{0,3},{1,2},{2,1},{3,0},{4,7},{5,6},{6,5},{7,4},{8,11},{9,10},{10,... | collective-permute-start | bytes 1544 | tf_op jit(solution)/shard_map/ppermute | solution.py:637
  98.7 7.5 %collective-permute-start.22 = (f32[1,128]{1,0:T(1,128)S(1)}, f32[1,128]{1,0:T(1,128)S(1)}, u32[]{:S(2)}, u32[]{:S(2)}) collective-permute-start(f32[1,128]{1,0:T(1,128)S(1)} %get-tuple-element.76.refs_5_), channel_id=1, source_target_pairs={{0,1},{1,0},{2,3},{3,2},{4,5},{5,4},{6,7},{7,6},{8,9},{9,8},{10,11... | collective-permute-start | bytes 1544 | tf_op jit(solution)/shard_map/ppermute | solution.py:637
  98.8 9.6 %collective-permute-start.23 = (f32[1,128]{1,0:T(1,128)S(1)}, f32[1,128]{1,0:T(1,128)S(1)}, u32[]{:S(2)}, u32[]{:S(2)}) collective-permute-start(f32[1,128]{1,0:T(1,128)S(1)} %get-tuple-element.76.refs_5_), channel_id=1, source_target_pairs={{0,2},{1,3},{2,0},{3,1},{4,6},{5,7},{6,4},{7,5},{8,10},{9,11},{10,... | collective-permute-start | bytes 1544 | tf_op jit(solution)/shard_map/ppermute | solution.py:637
  100.9 7.5 %collective-permute-start.24 = (f32[1,128]{1,0:T(1,128)S(1)}, f32[1,128]{1,0:T(1,128)S(1)}, u32[]{:S(2)}, u32[]{:S(2)}) collective-permute-start(f32[1,128]{1,0:T(1,128)S(1)} %get-tuple-element.76.refs_5_), channel_id=1, source_target_pairs={{0,3},{1,2},{2,1},{3,0},{4,7},{5,6},{6,5},{7,4},{8,11},{9,10},{10,... | collective-permute-start | bytes 1544 | tf_op jit(solution)/shard_map/ppermute | solution.py:637
  104.2 15.5 %collective-permute-start.30 = (f32[1,128]{1,0:T(1,128)S(1)}, f32[1,128]{1,0:T(1,128)S(1)}, u32[]{:S(2)}, u32[]{:S(2)}) collective-permute-start(f32[1,128]{1,0:T(1,128)S(1)} %get-tuple-element.82.refs_5_), channel_id=1, source_target_pairs={{0,1},{1,0},{2,3},{3,2},{4,5},{5,4},{6,7},{7,6},{8,9},{9,8},{10,11... | collective-permute-start | bytes 1544 | tf_op jit(solution)/shard_map/ppermute | solution.py:637
  104.3 15.4 %collective-permute-start.31 = (f32[1,128]{1,0:T(1,128)S(1)}, f32[1,128]{1,0:T(1,128)S(1)}, u32[]{:S(2)}, u32[]{:S(2)}) collective-permute-start(f32[1,128]{1,0:T(1,128)S(1)} %get-tuple-element.82.refs_5_), channel_id=1, source_target_pairs={{0,2},{1,3},{2,0},{3,1},{4,6},{5,7},{6,4},{7,5},{8,10},{9,11},{10,... | collective-permute-start | bytes 1544 | tf_op jit(solution)/shard_map/ppermute | solution.py:637
  106.2 13.6 %collective-permute-start.32 = (f32[1,128]{1,0:T(1,128)S(1)}, f32[1,128]{1,0:T(1,128)S(1)}, u32[]{:S(2)}, u32[]{:S(2)}) collective-permute-start(f32[1,128]{1,0:T(1,128)S(1)} %get-tuple-element.82.refs_5_), channel_id=1, source_target_pairs={{0,3},{1,2},{2,1},{3,0},{4,7},{5,6},{6,5},{7,4},{8,11},{9,10},{10,... | collective-permute-start | bytes 1544 | tf_op jit(solution)/shard_map/ppermute | solution.py:637
  110.9 11.8 %collective-permute-start.25 = (bf16[128,2048]{1,0:T(8,128)(2,1)S(1)}, bf16[128,2048]{1,0:T(8,128)(2,1)S(1)}, u32[]{:S(2)}, u32[]{:S(2)}) collective-permute-start(bf16[128,2048]{1,0:T(8,128)(2,1)S(1)} %get-tuple-element.78), channel_id=1, source_target_pairs={{0,32},{32,0},{64,96},{96,64},{1,33},{33,1},{65,97},{97,65},{2,34}... | collective-permute-start | bytes 1572872 | tf_op jit(solution)/shard_map/ppermute | solution.py:640
  (14 other events, 115.7 us)
